TPU v7x, 256 devices: a whole 4x4x8 slice. The times are simulated.
256 devices in a mesh: trainer: 32 (over z, y), vocab: 8 (over x, core).
Axes of the slice: x: 4, y: 4, z: 8, core: 2. Of those that a mesh axis runs over, the one named last changes fastest.
Arguments:
- hidden_table: bfloat16 [1024, 3072], P('trainer')
- head_weight: bfloat16 [3072, 8, 12288], P(None, 'vocab', 'trainer'), may hold values from -0.109375 to 0.109375
- targets: bfloat16 [1024, 8, 12288], P('trainer', 'vocab')
- counts: int32 [32], replicated, may hold values from 8 to 32, as said below
- dest: int32 [1024], replicated, may hold values from 0 to 31
- token: int32 [1024], replicated, may hold values from 0 to 31
Outputs:
- head_grad: float32 [3072, 8, 12288], P(None, 'vocab', 'trainer')
- table_grad: float32 [1024, 3072], P('trainer', 'vocab')
- mean_loss: float32 [], replicated
Inputs may be any that keep to these rules, and one draw needn't show every extreme that they name: `counts`: some replica has all 32 rows live and some has 8.
All inputs are finite; a program needn't handle non-finite values.
Results may differ from a plain program's by a relative error of at most 0.00095.
The roundings to bfloat16 on the way count: a program that leaves them out, or rounds other values in their place, can miss the bound.
Values may be sent and summed in bfloat16 or wider, within the bound.
No kernel may reach another device: no remote copies, remote signals or barrier semaphores. Data moves between devices by JAX's collectives and lax.ppermute only.
A program may use at most 128 MiB of HBM per device.

v0:
```python
import math

import jax
import jax.numpy as jnp
from jax import lax
from jax.sharding import PartitionSpec as P

VOCAB = 98304


def on_device(hidden_table, head_weight, targets, counts, dest, token):
    weight = head_weight[:, 0, :]
    rows = dest.shape[0]
    slots = rows // lax.axis_size("trainer")
    moved = lax.all_to_all(targets, "trainer", split_axis=2, concat_axis=0, tiled=True)
    probs = moved[:, 0, :]
    gid = dest * slots + token
    index = jnp.arange(rows, dtype=jnp.int32)
    live = (index % slots < jnp.repeat(counts, slots)).astype(jnp.float32)
    empty = jnp.zeros((rows, hidden_table.shape[1]), jnp.bfloat16)
    piece = lax.all_gather(hidden_table, "trainer", axis=0, tiled=True)
    count = piece.shape[0]
    inside = (gid >= 0) & (gid < count)
    picked = jnp.take(piece, jnp.clip(gid, 0, count - 1), axis=0)
    drafts = jnp.where(inside[:, None], picked, empty)
    logits = jnp.dot(drafts, weight, preferred_element_type=jnp.float32)
    local_top = jnp.max(logits, axis=1)
    top = lax.pmax(local_top, ("trainer", "vocab"))
    total = lax.psum(jnp.sum(jnp.exp(logits - top[:, None]), axis=1), ("trainer", "vocab"))
    lse = top + jnp.log(total)
    scale = VOCAB / math.sqrt(rows)
    probs_f = probs.astype(jnp.float32)
    grad_logits = (live[:, None] * scale * (jnp.exp(logits - lse[:, None]) - probs_f)).astype(
        jnp.bfloat16
    )
    head_grad = lax.dot_general(
        drafts, grad_logits, (((0,), (0,)), ((), ())), preferred_element_type=jnp.float32
    )
    head_grad = head_grad[:, None, :]
    loss_local = jnp.sum(
        live * (lse * jnp.sum(probs_f, axis=1) - jnp.sum(probs_f * logits, axis=1))
    )
    mean_loss = lax.psum(loss_local, ("trainer", "vocab")) / jnp.sum(counts).astype(jnp.float32)
    onehot = (gid[:, None] == index[None, :]).astype(jnp.bfloat16)
    gsum = lax.dot_general(
        onehot, grad_logits, (((0,), (0,)), ((), ())), preferred_element_type=jnp.float32
    ).astype(jnp.bfloat16)
    terms = lax.dot_general(
        gsum, weight, (((1,), (1,)), ((), ())), preferred_element_type=jnp.float32
    )
    partial_value = lax.psum_scatter(terms, "trainer", scatter_dimension=0, tiled=True)
    table_grad = lax.psum_scatter(partial_value, "vocab", scatter_dimension=1, tiled=True)
    return (head_grad, table_grad, mean_loss)


def solution(mesh):
    return jax.shard_map(
        on_device,
        mesh=mesh,
        in_specs=(
            P("trainer", None),
            P(None, "vocab", "trainer"),
            P("trainer", "vocab", None),
            P(),
            P(),
            P(),
        ),
        out_specs=(P(None, "vocab", "trainer"), P("trainer", "vocab"), P()),
        check_vma=False,
    )
```

profile of v0, /device:TPU:8, one launch (start us, length us, event | category | flops | bytes accessed | tf_op | source)
XLA Modules:
  0.0 628.0 jit_solution(8947618817332167014)
XLA Ops:
  7.2 0.0 copy-start
  7.2 0.0 all-gather.2.cloned.1.call-start
  7.2 0.7 all-gather.2.cloned.1.call-update
  7.9 12.5 %copy.18 = bf16[32,1,12288]{0,1,2:T(2,128)(2,1)} copy(bf16[32,1,12288]{2,0,1:T(8,128)(2,1)} %param.8) | data formatting | bytes 1572864 | tf_op args[2]
  20.4 0.5 broadcast.50
  20.9 68.6 %reduce.3 = bf16[12288,32]{1,0:T(8,128)(2,1)} reduce(bf16[12288,1,32]{2,1,0:T(2,128)(2,1)} %bitcast.22, bf16[]{:T(256)} %broadcast.50), dimensions={1}, to_apply=%bitcast.13.reduce_sub_computation | reduce | bytes 1572866
  89.6 0.0 copy-start.3
  89.6 0.0 copy-start.1
  89.6 0.0 copy-start.2
  89.6 5.9 reshape.57
  95.4 11.7 %all-to-all-start = ((bf16[32,2,6144]{2,1,0:T(2,128)(2,1)}), bf16[32,2,6144]{2,1,0:T(2,128)(2,1)S(1)}, u32[]{:S(2)}, u32[]{:S(2)}) async-start(bf16[32,2,6144]{2,1,0:T(2,128)(2,1)} %reshape.57), calls=%async_computation | async-start | bytes 1572864 | tf_op jit(solution)/shard_map/all_to_all | solution.py:15
  107.1 0.2 reduce-scatter.3.cloned.1.call-start
  107.4 0.0 copy-done.3
  107.4 0.1 broadcast_in_dim.40
  107.5 0.1 reshape.43
  107.5 0.0 copy-done.1
  107.5 0.0 copy-done.2
  107.6 22.0 %all-to-all-done = bf16[32,2,6144]{2,1,0:T(2,128)(2,1)S(1)} async-done(((bf16[32,2,6144]{2,1,0:T(2,128)(2,1)}), bf16[32,2,6144]{2,1,0:T(2,128)(2,1)S(1)}, u32[]{:S(2)}, u32[]{:S(2)}) %all-to-all-start) | async-done | bytes 786464 | tf_op jit(solution)/shard_map/all_to_all | solution.py:15
  129.6 7.9 %reshape.58 = bf16[12288,1,32]{2,1,0:T(2,128)(2,1)} reshape(bf16[32,2,6144]{2,1,0:T(2,128)(2,1)S(1)} %all-to-all-done) | data formatting | bytes 1572864
  137.6 8.5 %bitcast_convert_fusion = f32[32,1,12288]{0,1,2:T(1,128)} fusion(bf16[12288,1,32]{2,1,0:T(2,128)(2,1)} %reshape.58), kind=kLoop, calls=%fused_computation.30 | loop fusion | flops 393216 | bytes 2359296 | tf_op jit(solution)/shard_map/convert_element_type | solution.py:32
  146.1 5.7 copy.26
  151.8 3.5 copy.20
  155.3 3.0 copy.21
  158.3 3.3 reduce_sum.50
  161.6 0.1 reduce_sum.52
  161.6 0.0 all-gather.2.cloned.1.call-done
  161.6 15.8 %gather_fusion = bf16[1024,3072]{1,0:T(8,128)(2,1)} fusion(bf16[1024,3072]{1,0:T(8,128)(2,1)} %all-gather.2.cloned.1.call-done, s32[1024]{0:T(1024)S(1)} %fusion.17), kind=kCustom, calls=%fused_computation | custom fusion | bytes 12587008 | tf_op jit(solution)/shard_map/jit(_take)/gather | solution.py:24
  177.5 0.0 copy-done
  177.5 6.9 %fusion.19 = (f32[1024]{0:T(1024)S(1)}, f32[1024,384]{0,1:T(8,128)}) fusion(bf16[3072,1,384]{2,0,1:T(8,128)(2,1)S(1)} %copy-done, bf16[1024,3072]{1,0:T(8,128)(2,1)} %gather_fusion, pred[1024]{0:T(1024)(128)(4,1)S(1)} %compare_and_fusion, pred[1024]{0:T(1024)(128)(4,1)S(1)} %get-tuple-element.20), kind=kOutput, calls=%fused_computation.29 | convolution fusion | flops 2422602752 | bytes 10229760 | tf_op jit(solution)/shard_map/dot_general | solution.py:26
  184.3 73.4 %pmax.7 = f32[1024]{0:T(1024)S(1)} all-reduce(f32[1024]{0:T(1024)S(1)} %get-tuple-element.22), channel_id=1, replica_groups=mesh['trainer'=32,'vocab'=8] {'trainer','vocab'}, use_global_device_ids=true, to_apply=%region_1.2 | all-reduce | flops 1024 | bytes 8192 | tf_op jit(solution)/shard_map/pmax | solution.py:28
  257.7 2.3 multiply_reduce_fusion
  260.0 74.5 %psum.14 = f32[1024]{0:T(1024)S(1)} all-reduce(f32[1024]{0:T(1024)S(1)} %get-tuple-element.16), channel_id=1, replica_groups=mesh['trainer'=32,'vocab'=8] {'trainer','vocab'}, use_global_device_ids=true, to_apply=%region_3.4 | all-reduce | flops 1024 | bytes 8192 | tf_op jit(solution)/shard_map/psum | solution.py:29
  334.5 0.6 select_reduce_fusion
  335.1 2.2 multiply_convert_fusion
  337.4 8.0 %fusion.1 = f32[1024,3072]{1,0:T(8,128)} fusion(bf16[3072,1,384]{2,0,1:T(8,128)(2,1)S(1)} %copy-done, bf16[1024,384]{0,1:T(8,128)(2,1)S(1)} %multiply_convert_fusion, s32[1024]{0:T(1024)S(1)} %get-tuple-element.21), kind=kOutput, calls=%fused_computation.5 | convolution fusion | flops 3223715840 | bytes 15732736 | tf_op jit(solution)/shard_map/dot_general | solution.py:48
  345.4 0.0 reduce-scatter.3.cloned.1.call-update
  345.4 0.0 reduce-scatter.5.cloned.1.call-start
  345.5 0.6 reduce_sum.55
  346.8 74.0 %psum.15 = f32[]{:T(128)} all-reduce(f32[]{:T(128)} %get-tuple-element.17), channel_id=1, replica_groups=mesh['trainer'=32,'vocab'=8] {'trainer','vocab'}, use_global_device_ids=true, to_apply=%region_9.10 | all-reduce | flops 1 | bytes 8 | tf_op jit(solution)/shard_map/psum | solution.py:43
  420.8 156.9 %reduce-scatter.3.cloned.1.call-done = f32[32,3072]{1,0:T(8,128)} async-done(((f32[1024,3072]{1,0:T(8,128)}), f32[32,3072]{1,0:T(8,128)}) %reduce-scatter.3.cloned.1.call-update) | async-done | bytes 393232 | tf_op jit(solution)/shard_map/reduce_scatter | solution.py:51
  577.7 0.0 reduce-scatter.5.cloned.1.call-update
  577.7 7.0 %convolution_bitcast_fusion = f32[3072,1,384]{2,0,1:T(8,128)S(1)} fusion(bf16[1024,384]{0,1:T(8,128)(2,1)S(1)} %multiply_convert_fusion, bf16[1024,3072]{1,0:T(8,128)(2,1)} %gather_fusion, pred[1024]{0:T(1024)(128)(4,1)S(1)} %compare_and_fusion, pred[1024]{0:T(1024)(128)(4,1)S(1)} %get-tuple-element.20), kind=kOutput, calls=%fused_computation.2 | convolution fusion | flops 2422210560 | bytes 11798528 | tf_op jit(solution)/shard_map/dot_general | solution.py:36
  584.7 34.9 %copy.25 = f32[3072,1,384]{2,1,0:T(1,128)} copy(f32[3072,1,384]{2,0,1:T(8,128)S(1)} %convolution_bitcast_fusion) | data formatting | bytes 9437184
  620.3 0.0 reduce-scatter.5.cloned.1.call-done
  (4 shorter events, 0.0 us)
Async XLA Ops:
  7.2 170.3 %copy-start = (bf16[3072,1,384]{2,0,1:T(8,128)(2,1)S(1)}, bf16[3072,1,384]{2,0,1:T(8,128)(2,1)}, u32[]{:S(2)}) copy-start(bf16[3072,1,384]{2,0,1:T(8,128)(2,1)} %param.7) | copy-start | bytes 7077892
  7.2 154.5 %all-gather.2.cloned.1.call-start = ((), (), s32[]{:S(2)}) async-start(), calls=%async_computation.3 | async-start | bytes 6488064 | tf_op jit(solution)/shard_map/all_gather | solution.py:21
  89.6 17.8 %copy-start.3 = (s32[32]{0:T(128)S(1)}, s32[32]{0:T(128)}, u32[]{:S(2)}) copy-start(s32[32]{0:T(128)} %param.9) | copy-start | bytes 388
  89.6 18.0 %copy-start.1 = (s32[1024]{0:T(1024)S(1)}, s32[1024]{0:T(1024)}, u32[]{:S(2)}) copy-start(s32[1024]{0:T(1024)} %param.11) | copy-start | bytes 12292
  89.6 18.0 %copy-start.2 = (s32[1024]{0:T(1024)S(1)}, s32[1024]{0:T(1024)}, u32[]{:S(2)}) copy-start(s32[1024]{0:T(1024)} %param.10) | copy-start | bytes 12292
  95.4 34.2 %all-to-all-start = ((bf16[32,2,6144]{2,1,0:T(2,128)(2,1)}), bf16[32,2,6144]{2,1,0:T(2,128)(2,1)S(1)}, u32[]{:S(2)}, u32[]{:S(2)}) async-start(bf16[32,2,6144]{2,1,0:T(2,128)(2,1)} %reshape.57), calls=%async_computation | async-start | bytes 1572864 | tf_op jit(solution)/shard_map/all_to_all | solution.py:15
  107.1 470.6 %reduce-scatter.3.cloned.1.call-start = ((), (), s32[]{:S(2)}) async-start(), calls=%async_computation.4 | async-start | bytes 12976128 | tf_op jit(solution)/shard_map/reduce_scatter | solution.py:51
  345.4 274.9 %reduce-scatter.5.cloned.1.call-start = ((), (), s32[]{:S(2)}) async-start(), calls=%async_computation.5 | async-start | bytes 442368 | tf_op jit(solution)/shard_map/reduce_scatter | solution.py:52
Sparse Core Ops, SparseCore 0:
  10.6 90.3 all-gather.1
  345.5 232.1 reduce-scatter.2
  580.8 32.2 reduce-scatter.4
where the time goes:
time: 631 us; the launch traced here: 628 us
  blocking collectives  222 us (35%)
  waiting for transfers between devices  180 us (29%)
  local copies, waits for them, and re-layouts  90.1 us (14%)
  other arithmetic  86.2 us (14%)
  matrix products  21.9 us (3%)
  between operations  16.3 us (3%)
  starting transfers between devices  12 us (2%)
    reduce_scatter x1, waiting for transfers between devices, on_device(): lax.psum_scatter(terms, 'trainer', scatter_dimension=0, tiled=True)  157 us
    psum x1, blocking collectives, on_device(): lax.psum(jnp.sum(jnp.exp(logits - top[:, None]), axis=1), ('trainer', 'vo...  74.5 us
    psum x1, blocking collectives, on_device(): lax.psum(loss_local, ('trainer', 'vocab'))  74 us
    pmax x1, blocking collectives, on_device(): top = lax.pmax(local_top, ('trainer', 'vocab'))  73.4 us
    unnamed x1, other arithmetic  68.6 us
    unnamed x13, local copies, waits for them, and re-layouts  61.8 us
    all_to_all x1, waiting for transfers between devices, on_device(): lax.all_to_all(targets, 'trainer', split_axis=2, concat_axis=0, tiled=True)  22 us
    gather x1, local copies, waits for them, and re-layouts, on_device(): picked = jnp.take(piece, jnp.clip(gid, 0, count - 1), axis=0)  15.8 us
  transfers between devices with their start and end apart: 4, of which 2 were waited for; matrix products, arithmetic and copies ran while one was open for 26% of the time, Pallas kernels for 0%

commit v1 on v0

v1 whole, which is shorter than its diff:
```python
import functools
import math

import jax
import jax.numpy as jnp
from jax import lax
from jax.experimental import pallas as pl
from jax.experimental.pallas import tpu as pltpu
from jax.sharding import PartitionSpec as P

D = 3072
VOCAB = 98304
ROWS = 1024
TRAINERS = 32
SLOTS = 32
SHARDS = 8
LOCAL = VOCAB // (TRAINERS * SHARDS)
HALF = D // 2
BLOCK = 256
BF16 = jnp.bfloat16
F32 = jnp.float32
VMEM_LIMIT = 48 * 1024 * 1024
PARAMS = pltpu.CompilerParams(vmem_limit_bytes=VMEM_LIMIT)
VMEM = pl.BlockSpec(memory_space=pltpu.VMEM)
SMEM = pl.BlockSpec(memory_space=pltpu.SMEM)


def dot(a, b, dims=((1,), (0,))):
    return lax.dot_general(a, b, (dims, ((), ())), preferred_element_type=F32)


def split_kernel(x_ref, o_ref):
    for j in range(TRAINERS):
        o_ref[j] = x_ref[:, j * LOCAL : (j + 1) * LOCAL]


def split_targets(x):
    return pl.pallas_call(
        split_kernel,
        out_shape=jax.ShapeDtypeStruct((TRAINERS, SLOTS, LOCAL), BF16),
        in_specs=[VMEM],
        out_specs=VMEM,
        compiler_params=PARAMS,
    )(x)


def target_kernel(gid_ref, live_ref, p_ref, psum_ref, stat_ref):
    base = pl.program_id(0) * BLOCK
    rows = lax.broadcasted_iota(jnp.int32, (BLOCK, ROWS), 0) + base
    hot = jnp.where(gid_ref[...] == rows, live_ref[...], 0.0).astype(BF16)
    psum = dot(hot, p_ref[...])
    psum_ref[...] = psum
    lane = lax.broadcasted_iota(jnp.int32, (BLOCK, 128), 1)
    mass = jnp.sum(psum, axis=1, keepdims=True)
    stat_ref[...] = jnp.where(lane == 1, mass, 0.0)


def target_sums(gid, live, probs):
    return pl.pallas_call(
        target_kernel,
        grid=(ROWS // BLOCK,),
        out_shape=(
            jax.ShapeDtypeStruct((ROWS, LOCAL), F32),
            jax.ShapeDtypeStruct((ROWS, 128), F32),
        ),
        in_specs=[
            pl.BlockSpec((1, ROWS), lambda i: (0, 0)),
            pl.BlockSpec((1, ROWS), lambda i: (0, 0)),
            pl.BlockSpec((ROWS, LOCAL), lambda i: (0, 0)),
        ],
        out_specs=(
            pl.BlockSpec((BLOCK, LOCAL), lambda i: (i, 0)),
            pl.BlockSpec((BLOCK, 128), lambda i: (i, 0)),
        ),
        compiler_params=PARAMS,
    )(gid, live, probs)


def logit_kernel(c_ref, own_ref, other_ref, w_ref, psum_ref, stat_ref, logits_ref, o_ref):
    c = c_ref[0]
    near = pl.multiple_of(c * HALF, HALF)
    far = pl.multiple_of((1 - c) * HALF, HALF)
    logits = dot(own_ref[...], w_ref[pl.ds(near, HALF), :])
    logits += dot(other_ref[...], w_ref[pl.ds(far, HALF), :])
    logits_ref[...] = logits
    top = jnp.max(logits, axis=1, keepdims=True)
    lse = top + jnp.log(jnp.sum(jnp.exp(logits - top), axis=1, keepdims=True))
    cross = jnp.sum(psum_ref[...] * logits, axis=1, keepdims=True)
    lane = lax.broadcasted_iota(jnp.int32, (BLOCK, 128), 1)
    stat = jnp.where(lane == 0, lse, jnp.where(lane == 2, cross, stat_ref[...]))
    flat = stat.T[0:4]
    for k in range(SHARDS):
        o_ref[k] = flat


def logits_and_stats(c, own, other, weight, psum, stat):
    return pl.pallas_call(
        logit_kernel,
        grid_spec=pltpu.PrefetchScalarGridSpec(
            num_scalar_prefetch=1,
            grid=(ROWS // BLOCK,),
            in_specs=[
                pl.BlockSpec((BLOCK, HALF), lambda i, c: (i, 0)),
                pl.BlockSpec((BLOCK, HALF), lambda i, c: (i, 0)),
                pl.BlockSpec((D, LOCAL), lambda i, c: (0, 0)),
                pl.BlockSpec((BLOCK, LOCAL), lambda i, c: (i, 0)),
                pl.BlockSpec((BLOCK, 128), lambda i, c: (i, 0)),
            ],
            out_specs=(
                pl.BlockSpec((BLOCK, LOCAL), lambda i, c: (i, 0)),
                pl.BlockSpec((SHARDS, 4, BLOCK), lambda i, c: (0, 0, i)),
            ),
        ),
        out_shape=(
            jax.ShapeDtypeStruct((ROWS, LOCAL), F32),
            jax.ShapeDtypeStruct((SHARDS, 4, ROWS), F32),
        ),
        compiler_params=PARAMS,
    )(c, own, other, weight, psum, stat)


def merge(x):
    lse = x[:, 0, :]
    top = jnp.max(lse, axis=0, keepdims=True)
    lse = top + jnp.log(jnp.sum(jnp.exp(lse - top), axis=0, keepdims=True))
    rest = jnp.sum(x[:, 1:3, :], axis=0)
    return lse, rest[0:1], rest[1:2]


def merge_kernel(x_ref, o_ref):
    lse, mass, cross = merge(x_ref[...])
    flat = jnp.concatenate([lse, mass, cross, jnp.zeros_like(lse)], axis=0)
    for k in range(TRAINERS):
        o_ref[k] = flat


def merge_stats(x):
    return pl.pallas_call(
        merge_kernel,
        out_shape=jax.ShapeDtypeStruct((TRAINERS, 4, ROWS), F32),
        in_specs=[VMEM],
        out_specs=VMEM,
        compiler_params=PARAMS,
    )(x)


def column(row):
    return jnp.broadcast_to(row, (128, row.shape[1])).T


def grad_kernel(
    x_ref, logits_ref, p_ref, gid_ref, live_ref, sum_ref, loss_ref, parts_ref, g_ref
):
    lse, mass, cross = merge(x_ref[...])
    loss_ref[0, 0] = jnp.sum(lse * mass - cross)
    lse_col = column(lse)
    for j in range(LOCAL // 128):
        cols = pl.ds(j * 128, 128)
        p = jnp.exp(logits_ref[:, cols] - lse_col)
        first = p.astype(BF16)
        p = p - first.astype(F32)
        second = p.astype(BF16)
        third = (p - second.astype(F32)).astype(BF16)
        parts_ref[:, pl.ds(j * 128, 128)] = first
        parts_ref[:, pl.ds(LOCAL + j * 128, 128)] = second
        parts_ref[:, pl.ds(2 * LOCAL + j * 128, 128)] = third
    scale = VOCAB / math.sqrt(ROWS)

    @pl.loop(0, ROWS // BLOCK)
    def _(i):
        rows = pl.ds(pl.multiple_of(i * BLOCK, BLOCK), BLOCK)
        gid = column(gid_ref[:, rows])
        live = column(live_ref[:, rows])
        lane = lax.broadcasted_iota(jnp.int32, (BLOCK, 128), 1).astype(F32)
        hot = jnp.concatenate(
            [
                jnp.where(gid == lane + float(128 * k), 1.0, 0.0).astype(BF16)
                for k in range(ROWS // 128)
            ],
            axis=1,
        )
        sel = dot(hot, parts_ref[...])
        p = sel[:, 0:LOCAL] + sel[:, LOCAL : 2 * LOCAL] + sel[:, 2 * LOCAL :]
        diff = p - p_ref[rows, :].astype(F32)
        factor = live * scale
        g = jnp.concatenate(
            [factor * diff[:, j * 128 : (j + 1) * 128] for j in range(LOCAL // 128)],
            axis=1,
        )
        g_ref[rows, :] = g.astype(BF16)

    @pl.loop(0, ROWS // BLOCK)
    def _(i):
        rows = pl.ds(pl.multiple_of(i * BLOCK, BLOCK), BLOCK)
        row = lax.broadcasted_iota(jnp.int32, (BLOCK, ROWS), 0) + i * BLOCK
        hot = jnp.where(gid_ref[...] == row.astype(F32), 1.0, 0.0).astype(BF16)
        total = dot(hot, g_ref[...])
        high = total.astype(BF16)
        low = (total - high.astype(F32)).astype(BF16)
        sum_ref[0, rows, :] = high
        sum_ref[1, rows, :] = low


def gradients(x, logits, probs, gid, live):
    return pl.pallas_call(
        grad_kernel,
        out_shape=(
            jax.ShapeDtypeStruct((2, ROWS, LOCAL), BF16),
            jax.ShapeDtypeStruct((1, 1), F32),
        ),
        in_specs=[VMEM] * 5,
        out_specs=(VMEM, SMEM),
        scratch_shapes=[
            pltpu.VMEM((ROWS, 3 * LOCAL), BF16),
            pltpu.VMEM((ROWS, LOCAL), BF16),
        ],
        compiler_params=PARAMS,
    )(x, logits, probs, gid, live)


def term_kernel(x_ref, own_ref, other_ref, w_own_ref, w_other_ref, c0, c1, c2, c3):
    for k, out in enumerate((c0, c1, c2, c3)):
        at = lax.rem(x_ref[0] + k, 4)
        w_own = w_own_ref[at]
        w_other = w_other_ref[at]

        @pl.loop(0, ROWS // BLOCK)
        def _(i):
            rows = pl.ds(pl.multiple_of(i * BLOCK, BLOCK), BLOCK)
            nt = ((1,), (1,))
            val = dot(own_ref[0, rows, :], w_own, nt) + dot(other_ref[rows, :], w_other, nt)
            if k == 0:
                out[rows, :] = val
            else:
                half = ROWS // 2 // BLOCK
                at = pl.ds(pl.multiple_of(lax.rem(i, half) * BLOCK, BLOCK), BLOCK)
                out[i // half, at, :] = val


def terms(x, own, other, w_own, w_other):
    split = jax.ShapeDtypeStruct((2, ROWS // 2, LOCAL), F32)
    return pl.pallas_call(
        term_kernel,
        out_shape=(jax.ShapeDtypeStruct((ROWS, LOCAL), F32), split, split, split),
        in_specs=[SMEM] + [VMEM] * 4,
        out_specs=(VMEM,) * 4,
        compiler_params=PARAMS,
    )(x, own, other, w_own, w_other)


HEAD_BLOCK = 256
HEAD_STEPS = HALF // HEAD_BLOCK


def head_kernel(c_ref, own_ref, other_ref, sum_ref, o_ref):
    i = pl.program_id(0)

    def work(t_ref):
        both = dot(t_ref[...], sum_ref[0], ((0,), (0,)))
        both += dot(t_ref[...], sum_ref[1], ((0,), (0,)))
        for j in range(LOCAL // 128):
            o_ref[pl.ds(j, HEAD_BLOCK, stride=LOCAL // 128), :] = both[:, j * 128 : (j + 1) * 128]

    @pl.when(i < HEAD_STEPS)
    def _():
        work(own_ref)

    @pl.when(i >= HEAD_STEPS)
    def _():
        work(other_ref)


def head_gradient(c, own, other, sums):
    def place(i, c):
        mine = i < HEAD_STEPS
        side = jnp.where(mine, c[0], 1 - c[0])
        return (side * HEAD_STEPS + jnp.where(mine, i, i - HEAD_STEPS), 0)

    return pl.pallas_call(
        head_kernel,
        grid_spec=pltpu.PrefetchScalarGridSpec(
            num_scalar_prefetch=1,
            grid=(2 * HEAD_STEPS,),
            in_specs=[
                pl.BlockSpec((ROWS, HEAD_BLOCK), lambda i, c: (0, jnp.minimum(i, HEAD_STEPS - 1))),
                pl.BlockSpec((ROWS, HEAD_BLOCK), lambda i, c: (0, jnp.maximum(i - HEAD_STEPS, 0))),
                pl.BlockSpec((2, ROWS, LOCAL), lambda i, c: (0, 0, 0)),
            ],
            out_specs=pl.BlockSpec((HEAD_BLOCK * LOCAL // 128, 128), place),
        ),
        out_shape=jax.ShapeDtypeStruct((D * LOCAL // 128, 128), F32),
        compiler_params=PARAMS,
        cost_estimate=pl.CostEstimate(
            flops=4 * ROWS * D * LOCAL, bytes_accessed=12 * 1024 * 1024, transcendentals=0
        ),
    )(c, own, other, sums)


PAIR = [(i, i ^ 1) for i in range(SHARDS)]
RIGHT = [(i, (i + 2) % SHARDS) for i in range(SHARDS)]
LEFT = [(i, (i - 2) % SHARDS) for i in range(SHARDS)]


def on_device(hidden_table, head_weight, targets, counts, dest, token):
    me = lax.axis_index("vocab")
    c = lax.rem(me, 2)
    x = me // 2
    c1 = c.reshape(1).astype(jnp.int32)
    x1 = x.reshape(1).astype(jnp.int32)
    weight = head_weight[:, 0, :]

    half = lax.dynamic_slice(hidden_table, (0, c * HALF), (SLOTS, HALF))
    own = lax.all_gather(half, "trainer", axis=0, tiled=True)

    moved = lax.all_to_all(
        split_targets(targets[:, 0, :]), "trainer", split_axis=0, concat_axis=0, tiled=True
    )
    probs = moved.reshape(ROWS, LOCAL)

    blocks = weight.reshape(4, 2, LOCAL, LOCAL)
    w_own = lax.dynamic_index_in_dim(blocks, c, axis=1, keepdims=False)
    w_give = lax.dynamic_index_in_dim(blocks, 1 - c, axis=1, keepdims=False)
    w_other = lax.ppermute(w_give, "vocab", PAIR)

    gid = dest * SLOTS + token
    index = jnp.arange(ROWS, dtype=jnp.int32)
    live = (index % SLOTS < jnp.repeat(counts, SLOTS)).astype(F32).reshape(1, ROWS)
    psum, mass = target_sums(gid.reshape(1, ROWS), live, probs)

    other = lax.ppermute(own, "vocab", PAIR)
    logits, stats = logits_and_stats(c1, own, other, weight, psum, mass)
    stats = lax.all_to_all(stats, "vocab", split_axis=0, concat_axis=0, tiled=True)
    stats = lax.all_to_all(merge_stats(stats), "trainer", split_axis=0, concat_axis=0, tiled=True)

    sums, loss = gradients(stats, logits, probs, gid.astype(F32).reshape(1, ROWS), live)
    mean_loss = loss[0, 0] / jnp.sum(counts).astype(F32)

    sum_other = lax.ppermute(sums[0], "vocab", PAIR)
    t0, t1, t2, t3 = terms(x1, sums, sum_other, w_own, w_other)
    low_r = lax.ppermute(t2[0], "vocab", RIGHT)
    high_l = lax.ppermute(t2[1], "vocab", LEFT)
    high_r = lax.ppermute(t1[1], "vocab", RIGHT)
    low_l = lax.ppermute(t3[0], "vocab", LEFT)
    low_r = lax.ppermute(t1[0] + low_r, "vocab", RIGHT)
    high_l = lax.ppermute(t3[1] + high_l, "vocab", LEFT)
    head = head_gradient(c1, own, other, sums)
    total = t0 + jnp.concatenate([low_r + low_l, high_r + high_l], axis=0)
    got = lax.all_to_all(
        total.reshape(TRAINERS, SLOTS, LOCAL), "trainer", split_axis=0, concat_axis=0, tiled=True
    )
    table_grad = jnp.sum(got, axis=0)
    return head.reshape(D, 1, LOCAL), table_grad, mean_loss


def solution(mesh):
    return jax.shard_map(
        on_device,
        mesh=mesh,
        in_specs=(
            P("trainer", None),
            P(None, "vocab", "trainer"),
            P("trainer", "vocab", None),
            P(),
            P(),
            P(),
        ),
        out_specs=(P(None, "vocab", "trainer"), P("trainer", "vocab"), P()),
        check_vma=False,
    )
```

time: 631 us -> 303 us (0.48)
  blocking collectives: 222 us -> 10.2 us
  other arithmetic: 86.2 us -> 3.01 us
  local copies, waits for them, and re-layouts: 90.1 us -> 14.4 us
  Pallas kernels: 0 us -> 38.7 us
  matrix products: 21.9 us -> 0 us
  starting transfers between devices: 12 us -> 27.3 us
  waiting for transfers between devices: 180 us -> 192 us
    reduce_scatter x2 -> x0, waiting for transfers between devices: 157 us -> none  [the longest x1 157 us: on_device(): lax.psum_scatter(terms, 'trainer', scatter_dimension=0, tiled=True)]
    psum x2 -> x0, blocking collectives: 149 us -> none  [the longest x1 74.5 us: on_device(): lax.psum(jnp.sum(jnp.exp(logits - top[:, None]), axis=1), ('trainer', 'vo...]
    all_gather x1, waiting for transfers between devices: 0.01 us -> 84 us  [on_device(): own = lax.all_gather(half, 'trainer', axis=0, tiled=True)]
    pmax x1 -> x0, blocking collectives: 73.4 us -> none  [on_device(): top = lax.pmax(local_top, ('trainer', 'vocab'))]
    unnamed x1 -> x0, other arithmetic: 68.6 us -> none
    unnamed x13 -> x32, local copies, waits for them, and re-layouts: 61.8 us -> 9.28 us
    ppermute x0 -> x9, waiting for transfers between devices: none -> 47.7 us  [the longest x1 16.5 us: on_device(): low_r = lax.ppermute(t1[0] + low_r, 'vocab', RIGHT)]
    pallas_call x0 -> x7, Pallas kernels: none -> 38.7 us  [the longest x1 12.5 us: head_gradient(): pl.pallas_call(head_kernel, grid_spec=pltpu.PrefetchScalarGridSpec(num_sc...]
  transfers between devices with their start and end apart: 4 -> 13, of which waited for: 2 -> 8; matrix products, arithmetic and copies ran while one was open for 26% -> 1% of each run, Pallas kernels for 0% -> 7%
where the time goes in v1:
time: 303 us; the launch traced here: 302 us
  waiting for transfers between devices  192 us (63%)
  Pallas kernels  38.7 us (13%)
  starting transfers between devices  27.3 us (9%)
  between operations  16.7 us (6%)
  local copies, waits for them, and re-layouts  14.4 us (5%)
  blocking collectives  10.2 us (3%)
    all_gather x1, waiting for transfers between devices, on_device(): own = lax.all_gather(half, 'trainer', axis=0, tiled=True)  84 us
    all_to_all x1, waiting for transfers between devices, on_device(): lax.all_to_all(split_targets(targets[:, 0, :]), 'trainer', split_axis=0,...  22.9 us
    all_to_all x1, waiting for transfers between devices, on_device(): lax.all_to_all(total.reshape(TRAINERS, SLOTS, LOCAL), 'trainer', split_ax...  22.6 us
    ppermute x1, waiting for transfers between devices, on_device(): low_r = lax.ppermute(t1[0] + low_r, 'vocab', RIGHT)  16.5 us
    ppermute x1, waiting for transfers between devices, on_device(): low_r = lax.ppermute(t2[0], 'vocab', RIGHT)  15.9 us
    all_to_all x1, waiting for transfers between devices, on_device(): lax.all_to_all(merge_stats(stats), 'trainer', split_axis=0, concat_axis=0...  15 us
    ppermute x1, waiting for transfers between devices, on_device(): low_l = lax.ppermute(t3[0], 'vocab', LEFT)  12.9 us
    pallas_call x1, Pallas kernels, head_gradient(): pl.pallas_call(head_kernel, grid_spec=pltpu.PrefetchScalarGridSpec(num_sc...  12.5 us
  transfers between devices with their start and end apart: 13, of which 8 were waited for; matrix products, arithmetic and copies ran while one was open for 1% of the time, Pallas kernels for 7%

profile of v1, /device:TPU:8, one launch (start us, length us, event | category | flops | bytes accessed | tf_op | source)
XLA Modules:
  0.0 302.5 jit_solution(14625393310123462674)
XLA Ops:
  7.2 0.9 copy-done
  8.1 0.6 constant_dynamic-slice_fusion
  8.8 84.0 %all-gather.2.cloned.1.call-done.own_ref = bf16[1024,1536]{1,0:T(8,128)(2,1)} async-done(((bf16[32,1536]{1,0:T(8,128)(2,1)}), bf16[1024,1536]{1,0:T(8,128)(2,1)}) %all-gather.2.cloned.1.call-update) | async-done | bytes 3145744 | tf_op jit(solution)/shard_map/all_gather | solution.py:313
  92.8 1.1 copy-done.10
  93.9 0.1 shard_map.85
  94.0 0.9 copy-done.5
  94.9 6.9 %all-to-all-start = ((bf16[32,32,384]{2,1,0:T(8,128)(2,1)}), bf16[32,32,384]{2,1,0:T(8,128)(2,1)S(1)}, u32[]{:S(2)}, u32[]{:S(2)}) async-start(bf16[32,32,384]{2,1,0:T(8,128)(2,1)} %copy-done.5), calls=%async_computation | async-start | bytes 1572864 | tf_op jit(solution)/shard_map/all_to_all | solution.py:315
  101.8 0.1 broadcast_in_dim.3
  101.8 0.1 reshape.68
  102.0 22.9 %all-to-all-done = bf16[32,32,384]{2,1,0:T(8,128)(2,1)S(1)} async-done(((bf16[32,32,384]{2,1,0:T(8,128)(2,1)}), bf16[32,32,384]{2,1,0:T(8,128)(2,1)S(1)}, u32[]{:S(2)}, u32[]{:S(2)}) %all-to-all-start) | async-done | bytes 786464 | tf_op jit(solution)/shard_map/all_to_all | solution.py:315
  124.9 2.1 shard_map.86
  127.0 6.4 %shard_map.87 = (f32[1024,384]{1,0:T(8,128)S(1)}, f32[8,4,1024]{2,1,0:T(4,128)S(1)}) custom-call(s32[1]{0:T(128)} %bitcast.c_ref, bf16[1024,1536]{1,0:T(8,128)(2,1)} %all-gather.2.cloned.1.call-done.own_ref, bf16[1024,1536]{1,0:T(8,128)(2,1)} %collective-permute-done.other_ref, bf16[3072,384]{1,0:T(8,128)(2,1)S(1)} %bitcast.33, ...), custom_call_target="tpu_custom_call" | custom-call | tf_op jit(solution)/shard_map/pallas_call | solution.py:97
  133.4 1.1 copy-done.8
  134.5 10.2 %all_to_all.20.x_ref = f32[8,4,1024]{2,1,0:T(4,128)S(1)} all-to-all(f32[8,4,1024]{2,1,0:T(4,128)S(1)} %get-tuple-element.15), channel_id=1, replica_groups=mesh['trainer'=32,'vocab'=8] {'vocab'}, dimensions={0} | all-to-all | bytes 262144 | tf_op jit(solution)/shard_map/all_to_all | solution.py:332
  144.7 0.1 shard_map.88
  144.8 0.8 copy-done.7
  145.6 5.6 %all-to-all-start.2 = ((f32[32,4,1024]{2,1,0:T(4,128)}), f32[32,4,1024]{2,1,0:T(4,128)}, u32[]{:S(2)}, u32[]{:S(2)}) async-start(f32[32,4,1024]{2,1,0:T(4,128)} %copy-done.7), calls=%async_computation.2 | async-start | bytes 1048576 | tf_op jit(solution)/shard_map/all_to_all | solution.py:333
  151.3 1.6 dynamic-slice_bitcast_fusion
  152.9 15.0 %all-to-all-done.2.x_ref = f32[32,4,1024]{2,1,0:T(4,128)} async-done(((f32[32,4,1024]{2,1,0:T(4,128)}), f32[32,4,1024]{2,1,0:T(4,128)}, u32[]{:S(2)}, u32[]{:S(2)}) %all-to-all-start.2) | async-done | bytes 524320 | tf_op jit(solution)/shard_map/all_to_all | solution.py:333
  167.9 1.4 copy-done.9
  169.3 7.5 %shard_map.89 = (bf16[2,1024,384]{2,1,0:T(8,128)(2,1)S(1)}, f32[1,1]{1,0:T(1,128)}) custom-call(f32[32,4,1024]{2,1,0:T(4,128)} %all-to-all-done.2.x_ref, f32[1024,384]{1,0:T(8,128)S(1)} %copy-done.9, bf16[1024,384]{1,0:T(8,128)(2,1)S(1)} %bitcast.36, f32[1,1024]{1,0:T(1,128)S(1)} %bitcast.38, f32[1,1024]{1,0:T(1,128)S(1)} %compare_convert_fusion.live_ref), custom_call_target="tpu_custom_call" | custom-call | tf_op jit(solution)/shard_map/pallas_call | solution.py:205
  176.9 1.1 copy-done.3
  178.0 1.0 slice_bitcast_fusion.4
  179.0 2.5 collective-permute-done.1.other_ref
  181.5 10.1 %shard_map.91 = (f32[1024,384]{1,0:T(8,128)S(1)}, f32[2,512,384]{2,1,0:T(8,128)}, f32[2,512,384]{2,1,0:T(8,128)}, f32[2,512,384]{2,1,0:T(8,128)}) custom-call(s32[1]{0:T(128)} %bitcast.7.x_ref, bf16[2,1024,384]{2,1,0:T(8,128)(2,1)} %copy-done.3, bf16[1024,384]{1,0:T(8,128)(2,1)S(1)} %collective-permute-done.1.other_ref, bf16[4,384,384]{2,1,0:T(8,128)(2,1)S(1)} %copy-done.2, ...), custom_call_target="tpu_custom_call" | custom-call | tf_op jit(solution)/shard_map/pallas_call | solution.py:242
  191.5 1.6 slice_bitcast_fusion.3
  193.2 0.6 collective-permute-start.3
  193.8 2.7 collective-permute-start.7
  196.5 0.1 slice_bitcast_fusion.2
  196.5 0.1 collective-permute-start.5
  196.6 0.1 slice_bitcast_fusion.1
  196.7 2.3 collective-permute-start.6
  198.9 15.9 %collective-permute-done.3 = f32[512,384]{1,0:T(8,128)S(1)} collective-permute-done((f32[512,384]{1,0:T(8,128)S(1)}, f32[512,384]{1,0:T(8,128)S(1)}, u32[]{:S(2)}, u32[]{:S(2)}) %collective-permute-start.3) | collective-permute-done | bytes 786464 | tf_op jit(solution)/shard_map/ppermute | solution.py:340
  214.8 0.1 bitcast_add_fusion.1
  214.9 0.1 collective-permute-start.4
  215.0 0.1 bitcast_add_fusion
  215.1 3.3 %collective-permute-start.8 = (f32[512,384]{1,0:T(8,128)S(1)}, f32[512,384]{1,0:T(8,128)S(1)}, u32[]{:S(2)}, u32[]{:S(2)}) collective-permute-start(f32[512,384]{1,0:T(8,128)S(1)} %bitcast_add_fusion), channel_id=1, source_target_pairs={{0,6},{1,7},{2,0},{3,1},{4,2},{5,3},{6,4},{7,5},{8,14},{9,15},{10,... | collective-permute-start | bytes 2359304 | tf_op jit(solution)/shard_map/ppermute | solution.py:345
  218.4 12.9 %collective-permute-done.5 = f32[512,384]{1,0:T(8,128)S(1)} collective-permute-done((f32[512,384]{1,0:T(8,128)S(1)}, f32[512,384]{1,0:T(8,128)S(1)}, u32[]{:S(2)}, u32[]{:S(2)}) %collective-permute-start.5) | collective-permute-done | bytes 786464 | tf_op jit(solution)/shard_map/ppermute | solution.py:343
  231.3 16.5 %collective-permute-done.4 = f32[512,384]{1,0:T(8,128)S(1)} collective-permute-done((f32[512,384]{1,0:T(8,128)S(1)}, f32[512,384]{1,0:T(8,128)S(1)}, u32[]{:S(2)}, u32[]{:S(2)}) %collective-permute-start.4) | collective-permute-done | bytes 786464 | tf_op jit(solution)/shard_map/ppermute | solution.py:344
  247.7 0.1 add.49
  247.8 0.1 add.51
  247.9 1.4 maximum_add_fusion
  249.3 5.7 %all-to-all-start.3 = ((f32[32,32,384]{2,1,0:T(8,128)}), f32[32,32,384]{2,1,0:T(8,128)S(1)}, u32[]{:S(2)}, u32[]{:S(2)}) async-start(f32[32,32,384]{2,1,0:T(8,128)} %bitcast.40), calls=%async_computation.3 | async-start | bytes 3145728 | tf_op jit(solution)/shard_map/all_to_all | solution.py:348
  255.0 0.6 reduce_sum.19
  256.8 1.9 copy-done.6
  258.7 12.5 %shard_map.90 = f32[9216,128]{1,0:T(8,128)} custom-call(s32[1]{0:T(128)} %bitcast.c_ref, bf16[1024,1536]{1,0:T(8,128)(2,1)S(1)} %copy-done.6, bf16[1024,1536]{1,0:T(8,128)(2,1)} %collective-permute-done.other_ref, bf16[2,1024,384]{2,1,0:T(8,128)(2,1)S(1)} %copy-done.4), custom_call_target="tpu_custom_call" | custom-call | flops 4831838208 | bytes 12582912 | tf_op jit(solution)/shard_map/pallas_call | solution.py:279
  271.2 22.6 %all-to-all-done.3 = f32[32,32,384]{2,1,0:T(8,128)S(1)} async-done(((f32[32,32,384]{2,1,0:T(8,128)}), f32[32,32,384]{2,1,0:T(8,128)S(1)}, u32[]{:S(2)}, u32[]{:S(2)}) %all-to-all-start.3) | async-done | bytes 1572896 | tf_op jit(solution)/shard_map/all_to_all | solution.py:348
  293.8 0.7 reduce_sum.18
  (36 shorter events, 0.1 us)
Async XLA Ops:
  7.2 0.9 copy-start
  7.2 85.6 %all-gather.2.cloned.1.call-start = ((), (), s32[]{:S(2)}) async-start(), calls=%async_computation.4 | async-start | bytes 3244032 | tf_op jit(solution)/shard_map/all_gather | solution.py:313
  92.8 34.1 %collective-permute-start = (bf16[1024,1536]{1,0:T(8,128)(2,1)}, bf16[1024,1536]{1,0:T(8,128)(2,1)}, u32[]{:S(2)}, u32[]{:S(2)}) collective-permute-start(bf16[1024,1536]{1,0:T(8,128)(2,1)} %all-gather.2.cloned.1.call-done.own_ref), channel_id=1, source_target_pairs={{0,1},{1,0},{2,3},{3,2},{4,5},{5,4},{6,7},{7,6},{8,9},{9,8},{10,11... | collective-permute-start | bytes 9437192 | tf_op jit(solution)/shard_map/ppermute | solution.py:330
  92.8 1.1 copy-start.10
  93.9 7.8 %copy-start.15 = (s32[32]{0:T(128)S(1)}, s32[32]{0:T(128)}, u32[]{:S(2)}) copy-start(s32[32]{0:T(128)} %param.9) | copy-start | bytes 388
  93.9 8.0 %copy-start.13 = (s32[1024]{0:T(1024)S(1)}, s32[1024]{0:T(1024)}, u32[]{:S(2)}) copy-start(s32[1024]{0:T(1024)} %param.11) | copy-start | bytes 12292
  93.9 8.0 %copy-start.14 = (s32[1024]{0:T(1024)S(1)}, s32[1024]{0:T(1024)}, u32[]{:S(2)}) copy-start(s32[1024]{0:T(1024)} %param.10) | copy-start | bytes 12292
  94.0 0.9 copy-start.5
  94.9 32.1 %copy-start.1 = (bf16[3072,1,384]{2,0,1:T(8,128)(2,1)S(1)}, bf16[3072,1,384]{2,0,1:T(8,128)(2,1)}, u32[]{:S(2)}) copy-start(bf16[3072,1,384]{2,0,1:T(8,128)(2,1)} %param.7) | copy-start | bytes 7077892
  94.9 30.0 %all-to-all-start = ((bf16[32,32,384]{2,1,0:T(8,128)(2,1)}), bf16[32,32,384]{2,1,0:T(8,128)(2,1)S(1)}, u32[]{:S(2)}, u32[]{:S(2)}) async-start(bf16[32,32,384]{2,1,0:T(8,128)(2,1)} %copy-done.5), calls=%async_computation | async-start | bytes 1572864 | tf_op jit(solution)/shard_map/all_to_all | solution.py:315
  133.4 1.2 copy-start.8
  144.8 0.8 copy-start.7
  145.6 22.3 %all-to-all-start.2 = ((f32[32,4,1024]{2,1,0:T(4,128)}), f32[32,4,1024]{2,1,0:T(4,128)}, u32[]{:S(2)}, u32[]{:S(2)}) async-start(f32[32,4,1024]{2,1,0:T(4,128)} %copy-done.7), calls=%async_computation.2 | async-start | bytes 1048576 | tf_op jit(solution)/shard_map/all_to_all | solution.py:333
  152.9 26.1 %collective-permute-start.2 = (bf16[4,384,384]{2,1,0:T(8,128)(2,1)}, bf16[4,384,384]{2,1,0:T(8,128)(2,1)S(1)}, u32[]{:S(2)}, u32[]{:S(2)}) collective-permute-start(bf16[4,384,384]{2,1,0:T(8,128)(2,1)} %get-tuple-element.28), channel_id=1, source_target_pairs={{0,1},{1,0},{2,3},{3,2},{4,5},{5,4},{6,7},{7,6},{8,9},{9,8},{10,11... | collective-permute-start | bytes 3538952 | tf_op jit(solution)/shard_map/ppermute | solution.py:323
  167.9 1.4 copy-start.9
  169.3 12.1 %copy-start.2 = (bf16[4,384,384]{2,1,0:T(8,128)(2,1)S(1)}, bf16[4,384,384]{2,1,0:T(8,128)(2,1)}, u32[]{:S(2)}) copy-start(bf16[4,384,384]{2,1,0:T(8,128)(2,1)} %get-tuple-element.29.w_own_ref) | copy-start | bytes 3538948
  176.8 1.1 copy-start.3
  179.0 2.5 collective-permute-start.1
  191.5 4.9 %copy-start.11 = (f32[2,512,384]{2,1,0:T(8,128)S(1)}, f32[2,512,384]{2,1,0:T(8,128)}, u32[]{:S(2)}) copy-start(f32[2,512,384]{2,1,0:T(8,128)} %get-tuple-element.21) | copy-start | bytes 4718596
  193.1 3.5 %copy-start.12 = (f32[2,512,384]{2,1,0:T(8,128)S(1)}, f32[2,512,384]{2,1,0:T(8,128)}, u32[]{:S(2)}) copy-start(f32[2,512,384]{2,1,0:T(8,128)} %get-tuple-element.19) | copy-start | bytes 4718596
  193.2 21.7 %collective-permute-start.3 = (f32[512,384]{1,0:T(8,128)S(1)}, f32[512,384]{1,0:T(8,128)S(1)}, u32[]{:S(2)}, u32[]{:S(2)}) collective-permute-start(f32[512,384]{1,0:T(8,128)S(1)} %get-tuple-element.30), channel_id=1, source_target_pairs={{0,2},{1,3},{2,4},{3,5},{4,6},{5,7},{6,0},{7,1},{8,10},{9,11},{10,... | collective-permute-start | bytes 2359304 | tf_op jit(solution)/shard_map/ppermute | solution.py:340
  193.8 21.2 %collective-permute-start.7 = (f32[512,384]{1,0:T(8,128)S(1)}, f32[512,384]{1,0:T(8,128)S(1)}, u32[]{:S(2)}, u32[]{:S(2)}) collective-permute-start(f32[512,384]{1,0:T(8,128)S(1)} %get-tuple-element.31), channel_id=1, source_target_pairs={{0,6},{1,7},{2,0},{3,1},{4,2},{5,3},{6,4},{7,5},{8,14},{9,15},{10,... | collective-permute-start | bytes 2359304 | tf_op jit(solution)/shard_map/ppermute | solution.py:341
  196.5 34.7 %collective-permute-start.5 = (f32[512,384]{1,0:T(8,128)S(1)}, f32[512,384]{1,0:T(8,128)S(1)}, u32[]{:S(2)}, u32[]{:S(2)}) collective-permute-start(f32[512,384]{1,0:T(8,128)S(1)} %slice_bitcast_fusion.2), channel_id=1, source_target_pairs={{0,6},{1,7},{2,0},{3,1},{4,2},{5,3},{6,4},{7,5},{8,14},{9,15},{10,... | collective-permute-start | bytes 2359304 | tf_op jit(solution)/shard_map/ppermute | solution.py:343
  196.7 51.1 %collective-permute-start.6 = (f32[512,384]{1,0:T(8,128)S(1)}, f32[512,384]{1,0:T(8,128)S(1)}, u32[]{:S(2)}, u32[]{:S(2)}) collective-permute-start(f32[512,384]{1,0:T(8,128)S(1)} %slice_bitcast_fusion.1), channel_id=1, source_target_pairs={{0,2},{1,3},{2,4},{3,5},{4,6},{5,7},{6,0},{7,1},{8,10},{9,11},{10,... | collective-permute-start | bytes 2359304 | tf_op jit(solution)/shard_map/ppermute | solution.py:342
  214.9 32.8 %collective-permute-start.4 = (f32[512,384]{1,0:T(8,128)S(1)}, f32[512,384]{1,0:T(8,128)S(1)}, u32[]{:S(2)}, u32[]{:S(2)}) collective-permute-start(f32[512,384]{1,0:T(8,128)S(1)} %bitcast_add_fusion.1), channel_id=1, source_target_pairs={{0,2},{1,3},{2,4},{3,5},{4,6},{5,7},{6,0},{7,1},{8,10},{9,11},{10,... | collective-permute-start | bytes 2359304 | tf_op jit(solution)/shard_map/ppermute | solution.py:344
  215.1 32.7 %collective-permute-start.8 = (f32[512,384]{1,0:T(8,128)S(1)}, f32[512,384]{1,0:T(8,128)S(1)}, u32[]{:S(2)}, u32[]{:S(2)}) collective-permute-start(f32[512,384]{1,0:T(8,128)S(1)} %bitcast_add_fusion), channel_id=1, source_target_pairs={{0,6},{1,7},{2,0},{3,1},{4,2},{5,3},{6,4},{7,5},{8,14},{9,15},{10,... | collective-permute-start | bytes 2359304 | tf_op jit(solution)/shard_map/ppermute | solution.py:345
  249.3 7.5 %copy-start.4 = (bf16[2,1024,384]{2,1,0:T(8,128)(2,1)S(1)}, bf16[2,1024,384]{2,1,0:T(8,128)(2,1)}, u32[]{:S(2)}) copy-start(bf16[2,1024,384]{2,1,0:T(8,128)(2,1)} %copy-done.3) | copy-start | bytes 4718596
  249.3 44.5 %all-to-all-start.3 = ((f32[32,32,384]{2,1,0:T(8,128)}), f32[32,32,384]{2,1,0:T(8,128)S(1)}, u32[]{:S(2)}, u32[]{:S(2)}) async-start(f32[32,32,384]{2,1,0:T(8,128)} %bitcast.40), calls=%async_computation.3 | async-start | bytes 3145728 | tf_op jit(solution)/shard_map/all_to_all | solution.py:348
  256.8 1.9 copy-start.6
Sparse Core Ops, SparseCore 0:
  11.2 81.5 all-gather.1

commit v2 on v1

--- a/solution.py
+++ b/solution.py
@@ -76,47 +76,57 @@
     )(gid, live, probs)
 
 
-def logit_kernel(c_ref, own_ref, other_ref, w_ref, psum_ref, stat_ref, logits_ref, o_ref):
-    c = c_ref[0]
-    near = pl.multiple_of(c * HALF, HALF)
-    far = pl.multiple_of((1 - c) * HALF, HALF)
-    logits = dot(own_ref[...], w_ref[pl.ds(near, HALF), :])
-    logits += dot(other_ref[...], w_ref[pl.ds(far, HALF), :])
-    logits_ref[...] = logits
-    top = jnp.max(logits, axis=1, keepdims=True)
-    lse = top + jnp.log(jnp.sum(jnp.exp(logits - top), axis=1, keepdims=True))
-    cross = jnp.sum(psum_ref[...] * logits, axis=1, keepdims=True)
-    lane = lax.broadcasted_iota(jnp.int32, (BLOCK, 128), 1)
-    stat = jnp.where(lane == 0, lse, jnp.where(lane == 2, cross, stat_ref[...]))
-    flat = stat.T[0:4]
-    for k in range(SHARDS):
-        o_ref[k] = flat
-
-
-def logits_and_stats(c, own, other, weight, psum, stat):
+Z = 8
+Y = 4
+PIECE = (Z // 2, SLOTS, HALF)
+
+
+def logit_kernel(at_ref, *refs):
+    pieces, refs = refs[:16], refs[16:]
+    w_ref, psum_ref, stat_ref, own_ref, other_ref, logits_ref, o_ref = refs
+    c, y, z = at_ref[0], at_ref[1], at_ref[2]
+    for side, tab_ref in enumerate((own_ref, other_ref)):
+        for dy in range(Y):
+            for dz in range(Z):
+                z_at = lax.rem(z + Z - dz, Z)
+                y_at = lax.rem(y + Y - dy, Y)
+                piece = pieces[side * 8 + dy * 2 + dz // 4]
+                rows = pl.ds(pl.multiple_of((z_at * Y + y_at) * SLOTS, SLOTS), SLOTS)
+                tab_ref[rows, :] = piece[dz % 4]
+    near = pl.ds(pl.multiple_of(c * HALF, HALF), HALF)
+    far = pl.ds(pl.multiple_of((1 - c) * HALF, HALF), HALF)
+    block = 2 * BLOCK
+
+    @pl.loop(0, ROWS // block)
+    def _(i):
+        rows = pl.ds(pl.multiple_of(i * block, block), block)
+        logits = dot(own_ref[rows, :], w_ref[near, :])
+        logits += dot(other_ref[rows, :], w_ref[far, :])
+        logits_ref[rows, :] = logits
+        top = jnp.max(logits, axis=1, keepdims=True)
+        lse = top + jnp.log(jnp.sum(jnp.exp(logits - top), axis=1, keepdims=True))
+        cross = jnp.sum(psum_ref[rows, :] * logits, axis=1, keepdims=True)
+        lane = lax.broadcasted_iota(jnp.int32, (block, 128), 1)
+        stat = jnp.where(lane == 0, lse, jnp.where(lane == 2, cross, stat_ref[rows, :]))
+        flat = stat.T[0:4]
+        for k in range(SHARDS):
+            o_ref[k, :, rows] = flat
+
+
+def logits_and_stats(at, pieces, weight, psum, stat):
+    table = jax.ShapeDtypeStruct((ROWS, HALF), BF16)
     return pl.pallas_call(
         logit_kernel,
-        grid_spec=pltpu.PrefetchScalarGridSpec(
-            num_scalar_prefetch=1,
-            grid=(ROWS // BLOCK,),
-            in_specs=[
-                pl.BlockSpec((BLOCK, HALF), lambda i, c: (i, 0)),
-                pl.BlockSpec((BLOCK, HALF), lambda i, c: (i, 0)),
-                pl.BlockSpec((D, LOCAL), lambda i, c: (0, 0)),
-                pl.BlockSpec((BLOCK, LOCAL), lambda i, c: (i, 0)),
-                pl.BlockSpec((BLOCK, 128), lambda i, c: (i, 0)),
-            ],
-            out_specs=(
-                pl.BlockSpec((BLOCK, LOCAL), lambda i, c: (i, 0)),
-                pl.BlockSpec((SHARDS, 4, BLOCK), lambda i, c: (0, 0, i)),
-            ),
-        ),
         out_shape=(
+            table,
+            table,
             jax.ShapeDtypeStruct((ROWS, LOCAL), F32),
             jax.ShapeDtypeStruct((SHARDS, 4, ROWS), F32),
         ),
-        compiler_params=PARAMS,
-    )(c, own, other, weight, psum, stat)
+        in_specs=[SMEM] + [VMEM] * 19,
+        out_specs=(VMEM,) * 4,
+        compiler_params=PARAMS,
+    )(at, *pieces, weight, psum, stat)
 
 
 def merge(x):
@@ -149,7 +159,7 @@
 
 
 def grad_kernel(
-    x_ref, logits_ref, p_ref, gid_ref, live_ref, sum_ref, loss_ref, parts_ref, g_ref
+    x_ref, logits_ref, p_ref, gid_ref, live_ref, high_ref, low_ref, loss_ref, parts_ref, g_ref
 ):
     lse, mass, cross = merge(x_ref[...])
     loss_ref[0, 0] = jnp.sum(lse * mass - cross)
@@ -197,19 +207,20 @@
         total = dot(hot, g_ref[...])
         high = total.astype(BF16)
         low = (total - high.astype(F32)).astype(BF16)
-        sum_ref[0, rows, :] = high
-        sum_ref[1, rows, :] = low
+        high_ref[rows, :] = high
+        low_ref[rows, :] = low
 
 
 def gradients(x, logits, probs, gid, live):
     return pl.pallas_call(
         grad_kernel,
         out_shape=(
-            jax.ShapeDtypeStruct((2, ROWS, LOCAL), BF16),
+            jax.ShapeDtypeStruct((ROWS, LOCAL), BF16),
+            jax.ShapeDtypeStruct((ROWS, LOCAL), BF16),
             jax.ShapeDtypeStruct((1, 1), F32),
         ),
         in_specs=[VMEM] * 5,
-        out_specs=(VMEM, SMEM),
+        out_specs=(VMEM, VMEM, SMEM),
         scratch_shapes=[
             pltpu.VMEM((ROWS, 3 * LOCAL), BF16),
             pltpu.VMEM((ROWS, LOCAL), BF16),
@@ -218,46 +229,62 @@
     )(x, logits, probs, gid, live)
 
 
-def term_kernel(x_ref, own_ref, other_ref, w_own_ref, w_other_ref, c0, c1, c2, c3):
-    for k, out in enumerate((c0, c1, c2, c3)):
+def weight_kernel(x_ref, own_ref, other_ref, o_ref):
+    for k in range(4):
         at = lax.rem(x_ref[0] + k, 4)
-        w_own = w_own_ref[at]
-        w_other = w_other_ref[at]
-
-        @pl.loop(0, ROWS // BLOCK)
-        def _(i):
-            rows = pl.ds(pl.multiple_of(i * BLOCK, BLOCK), BLOCK)
-            nt = ((1,), (1,))
-            val = dot(own_ref[0, rows, :], w_own, nt) + dot(other_ref[rows, :], w_other, nt)
-            if k == 0:
-                out[rows, :] = val
-            else:
-                half = ROWS // 2 // BLOCK
-                at = pl.ds(pl.multiple_of(lax.rem(i, half) * BLOCK, BLOCK), BLOCK)
-                out[i // half, at, :] = val
-
-
-def terms(x, own, other, w_own, w_other):
-    split = jax.ShapeDtypeStruct((2, ROWS // 2, LOCAL), F32)
+        cols = pl.ds(k * LOCAL, LOCAL)
+        o_ref[0:LOCAL, cols] = own_ref[at].T
+        o_ref[LOCAL : 2 * LOCAL, cols] = other_ref[at].T
+
+
+def pair_weights(x, own, other):
+    return pl.pallas_call(
+        weight_kernel,
+        out_shape=jax.ShapeDtypeStruct((2 * LOCAL, 4 * LOCAL), BF16),
+        in_specs=[SMEM, VMEM, VMEM],
+        out_specs=VMEM,
+        compiler_params=PARAMS,
+    )(x, own, other)
+
+
+ROWS2 = ROWS // 2
+
+
+def term_kernel(own_ref, other_ref, w_ref, c0, l1, h1, l2, h2, l3, h3, g_ref):
+    g_ref[:, 0:LOCAL] = own_ref[...]
+    g_ref[:, LOCAL:] = other_ref[...]
+    outs = {1: (l1, h1), 2: (l2, h2), 3: (l3, h3)}
+
+    for i in range(2):
+        rows = pl.ds(i * ROWS2, ROWS2)
+        val = dot(g_ref[rows, :], w_ref[...])
+        c0[rows, :] = val[:, 0:LOCAL]
+        for k in range(1, 4):
+            outs[k][i][...] = val[:, k * LOCAL : (k + 1) * LOCAL]
+
+
+def terms(own, other, weights):
+    part = jax.ShapeDtypeStruct((ROWS2, LOCAL), F32)
     return pl.pallas_call(
         term_kernel,
-        out_shape=(jax.ShapeDtypeStruct((ROWS, LOCAL), F32), split, split, split),
-        in_specs=[SMEM] + [VMEM] * 4,
-        out_specs=(VMEM,) * 4,
-        compiler_params=PARAMS,
-    )(x, own, other, w_own, w_other)
+        out_shape=(jax.ShapeDtypeStruct((ROWS, LOCAL), F32),) + (part,) * 6,
+        in_specs=[VMEM] * 3,
+        out_specs=(VMEM,) * 7,
+        scratch_shapes=[pltpu.VMEM((ROWS, 2 * LOCAL), BF16)],
+        compiler_params=PARAMS,
+    )(own, other, weights)
 
 
 HEAD_BLOCK = 256
 HEAD_STEPS = HALF // HEAD_BLOCK
 
 
-def head_kernel(c_ref, own_ref, other_ref, sum_ref, o_ref):
+def head_kernel(c_ref, own_ref, other_ref, high_ref, low_ref, o_ref):
     i = pl.program_id(0)
 
     def work(t_ref):
-        both = dot(t_ref[...], sum_ref[0], ((0,), (0,)))
-        both += dot(t_ref[...], sum_ref[1], ((0,), (0,)))
+        both = dot(t_ref[...], high_ref[...], ((0,), (0,)))
+        both += dot(t_ref[...], low_ref[...], ((0,), (0,)))
         for j in range(LOCAL // 128):
             o_ref[pl.ds(j, HEAD_BLOCK, stride=LOCAL // 128), :] = both[:, j * 128 : (j + 1) * 128]
 
@@ -270,7 +297,7 @@
         work(other_ref)
 
 
-def head_gradient(c, own, other, sums):
+def head_gradient(c, own, other, high, low):
     def place(i, c):
         mine = i < HEAD_STEPS
         side = jnp.where(mine, c[0], 1 - c[0])
@@ -284,7 +311,8 @@
             in_specs=[
                 pl.BlockSpec((ROWS, HEAD_BLOCK), lambda i, c: (0, jnp.minimum(i, HEAD_STEPS - 1))),
                 pl.BlockSpec((ROWS, HEAD_BLOCK), lambda i, c: (0, jnp.maximum(i - HEAD_STEPS, 0))),
-                pl.BlockSpec((2, ROWS, LOCAL), lambda i, c: (0, 0, 0)),
+                pl.BlockSpec((ROWS, LOCAL), lambda i, c: (0, 0)),
+                pl.BlockSpec((ROWS, LOCAL), lambda i, c: (0, 0)),
             ],
             out_specs=pl.BlockSpec((HEAD_BLOCK * LOCAL // 128, 128), place),
         ),
@@ -293,7 +321,7 @@
         cost_estimate=pl.CostEstimate(
             flops=4 * ROWS * D * LOCAL, bytes_accessed=12 * 1024 * 1024, transcendentals=0
         ),
-    )(c, own, other, sums)
+    )(c, own, other, high, low)
 
 
 PAIR = [(i, i ^ 1) for i in range(SHARDS)]
@@ -301,16 +329,40 @@
 LEFT = [(i, (i - 2) % SHARDS) for i in range(SHARDS)]
 
 
+def along_z(k):
+    return [(i, (i // Y + k) % Z * Y + i % Y) for i in range(TRAINERS)]
+
+
+def along_y(k):
+    return [(i, i // Y * Y + (i + k) % Y) for i in range(TRAINERS)]
+
+
+def gather_pieces(half):
+    near = [half] + [lax.ppermute(half, "trainer", along_z(k)) for k in range(1, Z)]
+    low0 = jnp.stack(near[: Z // 2])
+    high0 = jnp.stack(near[Z // 2 :])
+    low1 = lax.ppermute(low0, "trainer", along_y(1))
+    high3 = lax.ppermute(high0, "trainer", along_y(-1))
+    high1 = lax.ppermute(high0, "trainer", along_y(1))
+    low3 = lax.ppermute(low0, "trainer", along_y(-1))
+    low2 = lax.ppermute(low1, "trainer", along_y(1))
+    high2 = lax.ppermute(high3, "trainer", along_y(-1))
+    return low0, high0, low1, high1, low2, high2, low3, high3
+
+
 def on_device(hidden_table, head_weight, targets, counts, dest, token):
     me = lax.axis_index("vocab")
+    trainer = lax.axis_index("trainer")
     c = lax.rem(me, 2)
     x = me // 2
+    at = jnp.stack([c, lax.rem(trainer, Y), trainer // Y]).astype(jnp.int32)
     c1 = c.reshape(1).astype(jnp.int32)
     x1 = x.reshape(1).astype(jnp.int32)
     weight = head_weight[:, 0, :]
 
     half = lax.dynamic_slice(hidden_table, (0, c * HALF), (SLOTS, HALF))
-    own = lax.all_gather(half, "trainer", axis=0, tiled=True)
+    pieces = gather_pieces(half)
+    pieces += tuple(lax.ppermute(p, "vocab", PAIR) for p in pieces)
 
     moved = lax.all_to_all(
         split_targets(targets[:, 0, :]), "trainer", split_axis=0, concat_axis=0, tiled=True
@@ -320,30 +372,28 @@
     blocks = weight.reshape(4, 2, LOCAL, LOCAL)
     w_own = lax.dynamic_index_in_dim(blocks, c, axis=1, keepdims=False)
     w_give = lax.dynamic_index_in_dim(blocks, 1 - c, axis=1, keepdims=False)
-    w_other = lax.ppermute(w_give, "vocab", PAIR)
+    weights = pair_weights(x1, w_own, lax.ppermute(w_give, "vocab", PAIR))
 
     gid = dest * SLOTS + token
     index = jnp.arange(ROWS, dtype=jnp.int32)
     live = (index % SLOTS < jnp.repeat(counts, SLOTS)).astype(F32).reshape(1, ROWS)
     psum, mass = target_sums(gid.reshape(1, ROWS), live, probs)
 
-    other = lax.ppermute(own, "vocab", PAIR)
-    logits, stats = logits_and_stats(c1, own, other, weight, psum, mass)
+    own, other, logits, stats = logits_and_stats(at, pieces, weight, psum, mass)
     stats = lax.all_to_all(stats, "vocab", split_axis=0, concat_axis=0, tiled=True)
     stats = lax.all_to_all(merge_stats(stats), "trainer", split_axis=0, concat_axis=0, tiled=True)
 
-    sums, loss = gradients(stats, logits, probs, gid.astype(F32).reshape(1, ROWS), live)
+    high, low, loss = gradients(stats, logits, probs, gid.astype(F32).reshape(1, ROWS), live)
     mean_loss = loss[0, 0] / jnp.sum(counts).astype(F32)
 
-    sum_other = lax.ppermute(sums[0], "vocab", PAIR)
-    t0, t1, t2, t3 = terms(x1, sums, sum_other, w_own, w_other)
-    low_r = lax.ppermute(t2[0], "vocab", RIGHT)
-    high_l = lax.ppermute(t2[1], "vocab", LEFT)
-    high_r = lax.ppermute(t1[1], "vocab", RIGHT)
-    low_l = lax.ppermute(t3[0], "vocab", LEFT)
-    low_r = lax.ppermute(t1[0] + low_r, "vocab", RIGHT)
-    high_l = lax.ppermute(t3[1] + high_l, "vocab", LEFT)
-    head = head_gradient(c1, own, other, sums)
+    t0, l1, h1, l2, h2, l3, h3 = terms(high, lax.ppermute(high, "vocab", PAIR), weights)
+    low_r = lax.ppermute(l2, "vocab", RIGHT)
+    high_l = lax.ppermute(h2, "vocab", LEFT)
+    high_r = lax.ppermute(h1, "vocab", RIGHT)
+    low_l = lax.ppermute(l3, "vocab", LEFT)
+    low_r = lax.ppermute(l1 + low_r, "vocab", RIGHT)
+    high_l = lax.ppermute(h3 + high_l, "vocab", LEFT)
+    head = head_gradient(c1, own, other, high, low)
     total = t0 + jnp.concatenate([low_r + low_l, high_r + high_l], axis=0)
     got = lax.all_to_all(
         total.reshape(TRAINERS, SLOTS, LOCAL), "trainer", split_axis=0, concat_axis=0, tiled=True

time: 303 us -> 251 us (0.83)
  waiting for transfers between devices: 192 us -> 118 us
  starting transfers between devices: 27.3 us -> 62.4 us
  between operations: 16.7 us -> 3.33 us
    all_gather x1 -> x0, waiting for transfers between devices: 84 us -> none  [on_device(): own = lax.all_gather(half, 'trainer', axis=0, tiled=True)]
    ppermute x9 -> x29, waiting for transfers between devices: 47.7 us -> 82.1 us  [the longest x7 17.6 us: gather_pieces(): lax.ppermute(half, 'trainer', along_z(k))]
    ppermute x9 -> x29, starting transfers between devices: 9.03 us -> 36.3 us  [the longest x7 18 us: gather_pieces(): lax.ppermute(half, 'trainer', along_z(k))]
    all_to_all x1, waiting for transfers between devices: 22.9 us -> 0.01 us  [on_device(): lax.all_to_all(split_targets(targets[:, 0, :]), 'trainer', split_axis=0,...]
    all_to_all x1, starting transfers between devices: 5.62 us -> 12.4 us  [on_device(): lax.all_to_all(merge_stats(stats), 'trainer', split_axis=0, concat_axis=0...]
    pallas_call x1, Pallas kernels: 10.1 us -> 4.87 us  [terms(): pl.pallas_call(term_kernel, out_shape=(jax.ShapeDtypeStruct((ROWS, LOCAL)...]
    pallas_call x2 -> x3, Pallas kernels: 13.9 us -> 17.5 us  [the longest x1 9.24 us: logits_and_stats(): pl.pallas_call(logit_kernel, out_shape=(table, table, jax.ShapeDtypeStruc...]
    unnamed x32 -> x28, local copies, waits for them, and re-layouts: 9.28 us -> 10.6 us
  transfers between devices with their start and end apart: 13 -> 32, of which waited for: 8 -> 12; matrix products, arithmetic and copies ran while one was open for 1% -> 2% of each run, Pallas kernels for 7% -> 10%
where the time goes in v2:
time: 251 us; the launch traced here: 250 us
  waiting for transfers between devices  118 us (47%)
  starting transfers between devices  62.4 us (25%)
  Pallas kernels  38.8 us (15%)
  local copies, waits for them, and re-layouts  13.7 us (5%)
  blocking collectives  10.2 us (4%)
  between operations  3.33 us (1%)
  other arithmetic  3.18 us (1%)
    all_to_all x1, waiting for transfers between devices, on_device(): lax.all_to_all(total.reshape(TRAINERS, SLOTS, LOCAL), 'trainer', split_ax...  22.6 us
    ppermute x7, starting transfers between devices, gather_pieces(): lax.ppermute(half, 'trainer', along_z(k))  18 us
    ppermute x7, waiting for transfers between devices, gather_pieces(): lax.ppermute(half, 'trainer', along_z(k))  17.6 us
    ppermute x1, waiting for transfers between devices, on_device(): high_r = lax.ppermute(h1, 'vocab', RIGHT)  16.6 us
    ppermute x1, waiting for transfers between devices, on_device(): high_l = lax.ppermute(h2, 'vocab', LEFT)  15.1 us
    ppermute x1, waiting for transfers between devices, on_device(): high_l = lax.ppermute(h3 + high_l, 'vocab', LEFT)  14.1 us
    all_to_all x1, waiting for transfers between devices, on_device(): lax.all_to_all(merge_stats(stats), 'trainer', split_axis=0, concat_axis=0...  13.7 us
    pallas_call x1, Pallas kernels, head_gradient(): pl.pallas_call(head_kernel, grid_spec=pltpu.PrefetchScalarGridSpec(num_sc...  12.5 us
  transfers between devices with their start and end apart: 32, of which 12 were waited for; matrix products, arithmetic and copies ran while one was open for 2% of the time, Pallas kernels for 10%

profile of v2, /device:TPU:8, one launch (start us, length us, event | category | flops | bytes accessed | tf_op | source)
XLA Modules:
  0.0 250.1 jit_solution(9890357236022438653)
XLA Ops:
  0.7 0.9 copy-done
  1.6 4.7 %collective-permute-start.2 = (bf16[32,1536]{1,0:T(8,128)(2,1)S(1)}, bf16[32,1536]{1,0:T(8,128)(2,1)S(1)}, u32[]{:S(2)}, u32[]{:S(2)}) collective-permute-start(bf16[32,1536]{1,0:T(8,128)(2,1)S(1)} %constant_dynamic-slice_fusion), channel_id=1, source_target_pairs={{0,96},{8,104},{16,112},{24,120},{32,128},{40,136},{48,144},{56,15... | collective-permute-start | bytes 294920 | tf_op jit(solution)/shard_map/ppermute | solution.py:341
  6.3 3.6 %collective-permute-start.1 = (bf16[32,1536]{1,0:T(8,128)(2,1)S(1)}, bf16[32,1536]{1,0:T(8,128)(2,1)S(1)}, u32[]{:S(2)}, u32[]{:S(2)}) collective-permute-start(bf16[32,1536]{1,0:T(8,128)(2,1)S(1)} %constant_dynamic-slice_fusion), channel_id=1, source_target_pairs={{0,64},{8,72},{16,80},{24,88},{32,96},{40,104},{48,112},{56,120},{... | collective-permute-start | bytes 294920 | tf_op jit(solution)/shard_map/ppermute | solution.py:341
  9.9 1.0 collective-permute-start
  10.9 2.2 collective-permute-start.6
  13.5 1.1 copy-done.4
  14.7 0.9 shard_map.85
  15.6 8.0 %all-to-all-start = ((bf16[32,32,384]{2,1,0:T(8,128)(2,1)}), bf16[32,32,384]{2,1,0:T(8,128)(2,1)S(1)}, u32[]{:S(2)}, u32[]{:S(2)}) async-start(bf16[32,32,384]{2,1,0:T(8,128)(2,1)} %shard_map.85), calls=%async_computation | async-start | bytes 1572864 | tf_op jit(solution)/shard_map/all_to_all | solution.py:367
  23.7 4.6 %collective-permute-start.4 = (bf16[32,1536]{1,0:T(8,128)(2,1)S(1)}, bf16[32,1536]{1,0:T(8,128)(2,1)S(1)}, u32[]{:S(2)}, u32[]{:S(2)}) collective-permute-start(bf16[32,1536]{1,0:T(8,128)(2,1)S(1)} %constant_dynamic-slice_fusion), channel_id=1, source_target_pairs={{0,160},{8,168},{16,176},{24,184},{32,192},{40,200},{48,208},{56,2... | collective-permute-start | bytes 294920 | tf_op jit(solution)/shard_map/ppermute | solution.py:341
  28.3 1.4 collective-permute-start.3
  29.8 1.5 collective-permute-start.7
  31.3 17.0 %collective-permute-done.4 = bf16[32,1536]{1,0:T(8,128)(2,1)S(1)} collective-permute-done((bf16[32,1536]{1,0:T(8,128)(2,1)S(1)}, bf16[32,1536]{1,0:T(8,128)(2,1)S(1)}, u32[]{:S(2)}, u32[]{:S(2)}) %collective-permute-start.4) | collective-permute-done | bytes 98336 | tf_op jit(solution)/shard_map/ppermute | solution.py:341
  49.0 1.5 collective-permute-start.8
  51.1 1.6 collective-permute-start.12
  53.2 4.6 %collective-permute-done.8.refs_3_ = bf16[4,32,1536]{2,1,0:T(8,128)(2,1)S(1)} collective-permute-done((bf16[4,32,1536]{2,1,0:T(8,128)(2,1)S(1)}, bf16[4,32,1536]{2,1,0:T(8,128)(2,1)S(1)}, u32[]{:S(2)}, u32[]{:S(2)}) %collective-permute-start.8) | collective-permute-done | bytes 393248 | tf_op jit(solution)/shard_map/ppermute | solution.py:346
  57.7 2.5 collective-permute-start.9
  60.2 2.3 collective-permute-done.10.refs_7_
  63.1 7.1 %collective-permute-done.12.refs_6_ = bf16[4,32,1536]{2,1,0:T(8,128)(2,1)S(1)} collective-permute-done((bf16[4,32,1536]{2,1,0:T(8,128)(2,1)S(1)}, bf16[4,32,1536]{2,1,0:T(8,128)(2,1)S(1)}, u32[]{:S(2)}, u32[]{:S(2)}) %collective-permute-start.12) | collective-permute-done | bytes 393248 | tf_op jit(solution)/shard_map/ppermute | solution.py:347
  71.7 2.8 %collective-permute-done.11.refs_5_ = bf16[4,32,1536]{2,1,0:T(8,128)(2,1)} collective-permute-done((bf16[4,32,1536]{2,1,0:T(8,128)(2,1)S(1)}, bf16[4,32,1536]{2,1,0:T(8,128)(2,1)}, u32[]{:S(2)}, u32[]{:S(2)}) %collective-permute-start.11) | collective-permute-done | bytes 393248 | tf_op jit(solution)/shard_map/ppermute | solution.py:349
  75.1 2.1 shard_map.86
  77.2 1.2 copy-done.3
  78.3 0.8 copy-done.5
  79.2 9.2 %shard_map.87 = (bf16[1024,1536]{1,0:T(8,128)(2,1)}, bf16[1024,1536]{1,0:T(8,128)(2,1)}, f32[1024,384]{1,0:T(8,128)}, f32[8,4,1024]{2,1,0:T(4,128)S(1)}) custom-call(s32[3]{0:T(128)S(1)} %pad_add_fusion.at_ref, bf16[4,32,1536]{2,1,0:T(8,128)(2,1)S(1)} %pad_maximum_fusion.refs_0_, bf16[4,32,1536]{2,1,0:T(8,128)(2,1)S(1)} %pad_maximum_fusion.1.refs_1_, ...), custom_call_target="tpu_custom_call" | custom-call | tf_op jit(solution)/shard_map/pallas_call | solution.py:118
  88.4 10.2 %all_to_all.20.x_ref = f32[8,4,1024]{2,1,0:T(4,128)S(1)} all-to-all(f32[8,4,1024]{2,1,0:T(4,128)S(1)} %get-tuple-element.23), channel_id=1, replica_groups=mesh['trainer'=32,'vocab'=8] {'vocab'}, dimensions={0} | all-to-all | bytes 262144 | tf_op jit(solution)/shard_map/all_to_all | solution.py:383
  98.6 0.9 shard_map.88
  99.5 12.4 %all-to-all-start.2 = ((f32[32,4,1024]{2,1,0:T(4,128)}), f32[32,4,1024]{2,1,0:T(4,128)S(1)}, u32[]{:S(2)}, u32[]{:S(2)}) async-start(f32[32,4,1024]{2,1,0:T(4,128)} %shard_map.88), calls=%async_computation.2 | async-start | bytes 1048576 | tf_op jit(solution)/shard_map/all_to_all | solution.py:384
  111.9 2.9 %dynamic-slice_bitcast_fusion = (bf16[4,384,384]{2,1,0:T(8,128)(2,1)}, bf16[4,384,384]{2,1,0:T(8,128)(2,1)S(1)}) fusion(bf16[4,2,384,384]{3,2,1,0:T(8,128)(2,1)} %bitcast.36, s32[]{:T(128)S(6)} %select_n.36, s32[]{:T(128)S(6)} %select_n.35), kind=kLoop, calls=%fused_computation.1 | loop fusion | bytes 4718600 | tf_op jit(solution)/shard_map/jit(dynamic_index_in_dim)/squeeze | solution.py:374
  114.9 13.7 %all-to-all-done.2.x_ref = f32[32,4,1024]{2,1,0:T(4,128)S(1)} async-done(((f32[32,4,1024]{2,1,0:T(4,128)}), f32[32,4,1024]{2,1,0:T(4,128)S(1)}, u32[]{:S(2)}, u32[]{:S(2)}) %all-to-all-start.2) | async-done | bytes 524320 | tf_op jit(solution)/shard_map/all_to_all | solution.py:384
  128.6 1.4 copy-done.2
  130.0 6.3 %shard_map.89 = (bf16[1024,384]{1,0:T(8,128)(2,1)S(1)}, bf16[1024,384]{1,0:T(8,128)(2,1)S(1)}, f32[1,1]{1,0:T(1,128)}) custom-call(f32[32,4,1024]{2,1,0:T(4,128)S(1)} %all-to-all-done.2.x_ref, f32[1024,384]{1,0:T(8,128)S(1)} %copy-done.2, bf16[1024,384]{1,0:T(8,128)(2,1)S(1)} %bitcast.31, f32[1,1024]{1,0:T(1,128)S(1)} %bitcast.33, ...), custom_call_target="tpu_custom_call" | custom-call | tf_op jit(solution)/shard_map/pallas_call | solution.py:215
  136.3 0.9 copy-done.7
  137.3 1.9 shard_map.91.w_ref
  139.2 1.4 copy-done.1
  140.6 1.0 copy-done.10
  141.6 4.9 %shard_map.92 = (f32[1024,384]{1,0:T(8,128)}, f32[512,384]{1,0:T(8,128)S(1)}, f32[512,384]{1,0:T(8,128)S(1)}, f32[512,384]{1,0:T(8,128)S(1)}, f32[512,384]{1,0:T...) custom-call(bf16[1024,384]{1,0:T(8,128)(2,1)S(1)} %get-tuple-element.25.high_ref.own_ref, ...), custom_call_target="tpu_custom_call" | custom-call | tf_op jit(solution)/shard_map/pallas_call | solution.py:268
  146.5 1.2 collective-permute-start.27
  147.6 0.9 collective-permute-start.23
  149.1 2.6 %collective-permute-start.25 = (f32[512,384]{1,0:T(8,128)S(1)}, f32[512,384]{1,0:T(8,128)S(1)}, u32[]{:S(2)}, u32[]{:S(2)}) collective-permute-start(f32[512,384]{1,0:T(8,128)S(1)} %get-tuple-element.30), channel_id=1, source_target_pairs={{0,6},{1,7},{2,0},{3,1},{4,2},{5,3},{6,4},{7,5},{8,14},{9,15},{10,... | collective-permute-start | bytes 2359304 | tf_op jit(solution)/shard_map/ppermute | solution.py:393
  151.7 15.1 %collective-permute-done.27 = f32[512,384]{1,0:T(8,128)S(1)} collective-permute-done((f32[512,384]{1,0:T(8,128)S(1)}, f32[512,384]{1,0:T(8,128)S(1)}, u32[]{:S(2)}, u32[]{:S(2)}) %collective-permute-start.27) | collective-permute-done | bytes 786464 | tf_op jit(solution)/shard_map/ppermute | solution.py:391
  166.9 2.5 collective-permute-start.28
  169.5 16.6 %collective-permute-done.26 = f32[512,384]{1,0:T(8,128)S(1)} collective-permute-done((f32[512,384]{1,0:T(8,128)S(1)}, f32[512,384]{1,0:T(8,128)S(1)}, u32[]{:S(2)}, u32[]{:S(2)}) %collective-permute-start.26) | collective-permute-done | bytes 786464 | tf_op jit(solution)/shard_map/ppermute | solution.py:392
  186.1 14.1 %collective-permute-done.28 = f32[512,384]{1,0:T(8,128)S(1)} collective-permute-done((f32[512,384]{1,0:T(8,128)S(1)}, f32[512,384]{1,0:T(8,128)S(1)}, u32[]{:S(2)}, u32[]{:S(2)}) %collective-permute-start.28) | collective-permute-done | bytes 786464 | tf_op jit(solution)/shard_map/ppermute | solution.py:395
  200.2 2.0 collective-permute-done.24
  202.3 1.3 maximum_add_fusion
  203.6 5.7 %all-to-all-start.3 = ((f32[32,32,384]{2,1,0:T(8,128)}), f32[32,32,384]{2,1,0:T(8,128)S(1)}, u32[]{:S(2)}, u32[]{:S(2)}) async-start(f32[32,32,384]{2,1,0:T(8,128)} %bitcast.37), calls=%async_computation.3 | async-start | bytes 3145728 | tf_op jit(solution)/shard_map/all_to_all | solution.py:398
  211.3 1.9 copy-done.6
  213.2 12.5 %shard_map.90 = f32[9216,128]{1,0:T(8,128)} custom-call(s32[1]{0:T(128)} %bitcast.c_ref, bf16[1024,1536]{1,0:T(8,128)(2,1)S(1)} %copy-done.6, bf16[1024,1536]{1,0:T(8,128)(2,1)} %get-tuple-element.22.other_ref, bf16[1024,384]{1,0:T(8,128)(2,1)S(1)} %get-tuple-element.25.high_ref.own_ref, bf16[1024,384]{1,0:T(8,128)(2,1)S(1)} %copy-done.8), custom_call_target="tpu_custom_call" | custom-call | flops 4831838208 | bytes 12582912 | tf_op jit(solution)/shard_map/pallas_call | solution.py:306
  225.7 22.6 %all-to-all-done.3 = f32[32,32,384]{2,1,0:T(8,128)S(1)} async-done(((f32[32,32,384]{2,1,0:T(8,128)}), f32[32,32,384]{2,1,0:T(8,128)S(1)}, u32[]{:S(2)}, u32[]{:S(2)}) %all-to-all-start.3) | async-done | bytes 1572896 | tf_op jit(solution)/shard_map/all_to_all | solution.py:398
  (70 shorter events, 7.3 us)
Async XLA Ops:
  0.6 0.9 copy-start
  1.6 22.1 %collective-permute-start.2 = (bf16[32,1536]{1,0:T(8,128)(2,1)S(1)}, bf16[32,1536]{1,0:T(8,128)(2,1)S(1)}, u32[]{:S(2)}, u32[]{:S(2)}) collective-permute-start(bf16[32,1536]{1,0:T(8,128)(2,1)S(1)} %constant_dynamic-slice_fusion), channel_id=1, source_target_pairs={{0,96},{8,104},{16,112},{24,120},{32,128},{40,136},{48,144},{56,15... | collective-permute-start | bytes 294920 | tf_op jit(solution)/shard_map/ppermute | solution.py:341
  6.3 22.0 %collective-permute-start.1 = (bf16[32,1536]{1,0:T(8,128)(2,1)S(1)}, bf16[32,1536]{1,0:T(8,128)(2,1)S(1)}, u32[]{:S(2)}, u32[]{:S(2)}) collective-permute-start(bf16[32,1536]{1,0:T(8,128)(2,1)S(1)} %constant_dynamic-slice_fusion), channel_id=1, source_target_pairs={{0,64},{8,72},{16,80},{24,88},{32,96},{40,104},{48,112},{56,120},{... | collective-permute-start | bytes 294920 | tf_op jit(solution)/shard_map/ppermute | solution.py:341
  9.9 19.9 %collective-permute-start = (bf16[32,1536]{1,0:T(8,128)(2,1)S(1)}, bf16[32,1536]{1,0:T(8,128)(2,1)S(1)}, u32[]{:S(2)}, u32[]{:S(2)}) collective-permute-start(bf16[32,1536]{1,0:T(8,128)(2,1)S(1)} %constant_dynamic-slice_fusion), channel_id=1, source_target_pairs={{0,32},{8,40},{16,48},{24,56},{32,64},{40,72},{48,80},{56,88},{64,... | collective-permute-start | bytes 294920 | tf_op jit(solution)/shard_map/ppermute | solution.py:341
  10.9 20.4 %collective-permute-start.6 = (bf16[32,1536]{1,0:T(8,128)(2,1)S(1)}, bf16[32,1536]{1,0:T(8,128)(2,1)S(1)}, u32[]{:S(2)}, u32[]{:S(2)}) collective-permute-start(bf16[32,1536]{1,0:T(8,128)(2,1)S(1)} %constant_dynamic-slice_fusion), channel_id=1, source_target_pairs={{0,224},{8,232},{16,240},{24,248},{32,0},{40,8},{48,16},{56,24},{6... | collective-permute-start | bytes 294920 | tf_op jit(solution)/shard_map/ppermute | solution.py:341
  13.1 18.2 %collective-permute-start.5 = (bf16[32,1536]{1,0:T(8,128)(2,1)S(1)}, bf16[32,1536]{1,0:T(8,128)(2,1)S(1)}, u32[]{:S(2)}, u32[]{:S(2)}) collective-permute-start(bf16[32,1536]{1,0:T(8,128)(2,1)S(1)} %constant_dynamic-slice_fusion), channel_id=1, source_target_pairs={{0,192},{8,200},{16,208},{24,216},{32,224},{40,232},{48,240},{56,2... | collective-permute-start | bytes 294920 | tf_op jit(solution)/shard_map/ppermute | solution.py:341
  13.5 1.1 copy-start.4
  15.6 54.6 %copy-start.13 = (s32[32]{0:T(128)S(1)}, s32[32]{0:T(128)}, u32[]{:S(2)}) copy-start(s32[32]{0:T(128)} %param.9) | copy-start | bytes 388
  15.6 59.4 %copy-start.11 = (s32[1024]{0:T(1024)S(1)}, s32[1024]{0:T(1024)}, u32[]{:S(2)}) copy-start(s32[1024]{0:T(1024)} %param.11) | copy-start | bytes 12292
  15.6 59.4 %copy-start.12 = (s32[1024]{0:T(1024)S(1)}, s32[1024]{0:T(1024)}, u32[]{:S(2)}) copy-start(s32[1024]{0:T(1024)} %param.10) | copy-start | bytes 12292
  15.6 59.5 %all-to-all-start = ((bf16[32,32,384]{2,1,0:T(8,128)(2,1)}), bf16[32,32,384]{2,1,0:T(8,128)(2,1)S(1)}, u32[]{:S(2)}, u32[]{:S(2)}) async-start(bf16[32,32,384]{2,1,0:T(8,128)(2,1)} %shard_map.85), calls=%async_computation | async-start | bytes 1572864 | tf_op jit(solution)/shard_map/all_to_all | solution.py:367
  23.7 24.6 %collective-permute-start.4 = (bf16[32,1536]{1,0:T(8,128)(2,1)S(1)}, bf16[32,1536]{1,0:T(8,128)(2,1)S(1)}, u32[]{:S(2)}, u32[]{:S(2)}) collective-permute-start(bf16[32,1536]{1,0:T(8,128)(2,1)S(1)} %constant_dynamic-slice_fusion), channel_id=1, source_target_pairs={{0,160},{8,168},{16,176},{24,184},{32,192},{40,200},{48,208},{56,2... | collective-permute-start | bytes 294920 | tf_op jit(solution)/shard_map/ppermute | solution.py:341
  28.3 20.7 %collective-permute-start.3 = (bf16[32,1536]{1,0:T(8,128)(2,1)S(1)}, bf16[32,1536]{1,0:T(8,128)(2,1)S(1)}, u32[]{:S(2)}, u32[]{:S(2)}) collective-permute-start(bf16[32,1536]{1,0:T(8,128)(2,1)S(1)} %constant_dynamic-slice_fusion), channel_id=1, source_target_pairs={{0,128},{8,136},{16,144},{24,152},{32,160},{40,168},{48,176},{56,1... | collective-permute-start | bytes 294920 | tf_op jit(solution)/shard_map/ppermute | solution.py:341
  29.8 22.9 %collective-permute-start.7 = (bf16[4,32,1536]{2,1,0:T(8,128)(2,1)S(1)}, bf16[4,32,1536]{2,1,0:T(8,128)(2,1)S(1)}, u32[]{:S(2)}, u32[]{:S(2)}) collective-permute-start(bf16[4,32,1536]{2,1,0:T(8,128)(2,1)S(1)} %pad_maximum_fusion.refs_0_), channel_id=1, source_target_pairs={{0,8},{8,16},{16,24},{24,0},{32,40},{40,48},{48,56},{56,32},{64,72... | collective-permute-start | bytes 1179656 | tf_op jit(solution)/shard_map/ppermute | solution.py:344
  49.0 8.8 %collective-permute-start.8 = (bf16[4,32,1536]{2,1,0:T(8,128)(2,1)S(1)}, bf16[4,32,1536]{2,1,0:T(8,128)(2,1)S(1)}, u32[]{:S(2)}, u32[]{:S(2)}) collective-permute-start(bf16[4,32,1536]{2,1,0:T(8,128)(2,1)S(1)} %pad_maximum_fusion.1.refs_1_), channel_id=1, source_target_pairs={{0,8},{8,16},{16,24},{24,0},{32,40},{40,48},{48,56},{56,32},{64,72... | collective-permute-start | bytes 1179656 | tf_op jit(solution)/shard_map/ppermute | solution.py:346
  50.5 12.1 %collective-permute-start.10 = (bf16[4,32,1536]{2,1,0:T(8,128)(2,1)S(1)}, bf16[4,32,1536]{2,1,0:T(8,128)(2,1)S(1)}, u32[]{:S(2)}, u32[]{:S(2)}) collective-permute-start(bf16[4,32,1536]{2,1,0:T(8,128)(2,1)S(1)} %pad_maximum_fusion.1.refs_1_), channel_id=1, source_target_pairs={{0,24},{8,0},{16,8},{24,16},{32,56},{40,32},{48,40},{56,48},{64,88... | collective-permute-start | bytes 1179656 | tf_op jit(solution)/shard_map/ppermute | solution.py:345
  51.1 19.1 %collective-permute-start.12 = (bf16[4,32,1536]{2,1,0:T(8,128)(2,1)S(1)}, bf16[4,32,1536]{2,1,0:T(8,128)(2,1)S(1)}, u32[]{:S(2)}, u32[]{:S(2)}) collective-permute-start(bf16[4,32,1536]{2,1,0:T(8,128)(2,1)S(1)} %pad_maximum_fusion.refs_0_), channel_id=1, source_target_pairs={{0,24},{8,0},{16,8},{24,16},{32,56},{40,32},{48,40},{56,48},{64,88... | collective-permute-start | bytes 1179656 | tf_op jit(solution)/shard_map/ppermute | solution.py:347
  52.7 17.8 %collective-permute-start.13 = (bf16[4,32,1536]{2,1,0:T(8,128)(2,1)S(1)}, bf16[4,32,1536]{2,1,0:T(8,128)(2,1)}, u32[]{:S(2)}, u32[]{:S(2)}) collective-permute-start(bf16[4,32,1536]{2,1,0:T(8,128)(2,1)S(1)} %pad_maximum_fusion.refs_0_), channel_id=1, source_target_pairs={{0,1},{1,0},{2,3},{3,2},{4,5},{5,4},{6,7},{7,6},{8,9},{9,8},{10,11... | collective-permute-start | bytes 1179656 | tf_op jit(solution)/shard_map/ppermute | solution.py:365
  52.7 18.5 %collective-permute-start.14 = (bf16[4,32,1536]{2,1,0:T(8,128)(2,1)S(1)}, bf16[4,32,1536]{2,1,0:T(8,128)(2,1)}, u32[]{:S(2)}, u32[]{:S(2)}) collective-permute-start(bf16[4,32,1536]{2,1,0:T(8,128)(2,1)S(1)} %pad_maximum_fusion.1.refs_1_), channel_id=1, source_target_pairs={{0,1},{1,0},{2,3},{3,2},{4,5},{5,4},{6,7},{7,6},{8,9},{9,8},{10,11... | collective-permute-start | bytes 1179656 | tf_op jit(solution)/shard_map/ppermute | solution.py:365
  57.7 13.5 %collective-permute-start.9 = (bf16[4,32,1536]{2,1,0:T(8,128)(2,1)S(1)}, bf16[4,32,1536]{2,1,0:T(8,128)(2,1)}, u32[]{:S(2)}, u32[]{:S(2)}) collective-permute-start(bf16[4,32,1536]{2,1,0:T(8,128)(2,1)S(1)} %collective-permute-done.7.refs_2_), channel_id=1, source_target_pairs={{0,8},{8,16},{16,24},{24,0},{32,40},{40,48},{48,56},{56,32},{64,72... | collective-permute-start | bytes 1179656 | tf_op jit(solution)/shard_map/ppermute | solution.py:348
  62.6 12.0 %collective-permute-start.11 = (bf16[4,32,1536]{2,1,0:T(8,128)(2,1)S(1)}, bf16[4,32,1536]{2,1,0:T(8,128)(2,1)}, u32[]{:S(2)}, u32[]{:S(2)}) collective-permute-start(bf16[4,32,1536]{2,1,0:T(8,128)(2,1)S(1)} %collective-permute-done.10.refs_7_), channel_id=1, source_target_pairs={{0,24},{8,0},{16,8},{24,16},{32,56},{40,32},{48,40},{56,48},{64,88... | collective-permute-start | bytes 1179656 | tf_op jit(solution)/shard_map/ppermute | solution.py:349
  70.2 4.3 %collective-permute-start.15 = (bf16[4,32,1536]{2,1,0:T(8,128)(2,1)S(1)}, bf16[4,32,1536]{2,1,0:T(8,128)(2,1)}, u32[]{:S(2)}, u32[]{:S(2)}) collective-permute-start(bf16[4,32,1536]{2,1,0:T(8,128)(2,1)S(1)} %collective-permute-done.7.refs_2_), channel_id=1, source_target_pairs={{0,1},{1,0},{2,3},{3,2},{4,5},{5,4},{6,7},{7,6},{8,9},{9,8},{10,11... | collective-permute-start | bytes 1179656 | tf_op jit(solution)/shard_map/ppermute | solution.py:365
  70.4 8.7 %collective-permute-start.20 = (bf16[4,32,1536]{2,1,0:T(8,128)(2,1)S(1)}, bf16[4,32,1536]{2,1,0:T(8,128)(2,1)}, u32[]{:S(2)}, u32[]{:S(2)}) collective-permute-start(bf16[4,32,1536]{2,1,0:T(8,128)(2,1)S(1)} %collective-permute-done.10.refs_7_), channel_id=1, source_target_pairs={{0,1},{1,0},{2,3},{3,2},{4,5},{5,4},{6,7},{7,6},{8,9},{9,8},{10,11... | collective-permute-start | bytes 1179656 | tf_op jit(solution)/shard_map/ppermute | solution.py:365
  71.2 8.0 %collective-permute-start.16 = (bf16[4,32,1536]{2,1,0:T(8,128)(2,1)S(1)}, bf16[4,32,1536]{2,1,0:T(8,128)(2,1)}, u32[]{:S(2)}, u32[]{:S(2)}) collective-permute-start(bf16[4,32,1536]{2,1,0:T(8,128)(2,1)S(1)} %collective-permute-done.8.refs_3_), channel_id=1, source_target_pairs={{0,1},{1,0},{2,3},{3,2},{4,5},{5,4},{6,7},{7,6},{8,9},{9,8},{10,11... | collective-permute-start | bytes 1179656 | tf_op jit(solution)/shard_map/ppermute | solution.py:365
  71.3 7.9 %collective-permute-start.19 = (bf16[4,32,1536]{2,1,0:T(8,128)(2,1)S(1)}, bf16[4,32,1536]{2,1,0:T(8,128)(2,1)}, u32[]{:S(2)}, u32[]{:S(2)}) collective-permute-start(bf16[4,32,1536]{2,1,0:T(8,128)(2,1)S(1)} %collective-permute-done.12.refs_6_), channel_id=1, source_target_pairs={{0,1},{1,0},{2,3},{3,2},{4,5},{5,4},{6,7},{7,6},{8,9},{9,8},{10,11... | collective-permute-start | bytes 1179656 | tf_op jit(solution)/shard_map/ppermute | solution.py:365
  74.5 4.6 %collective-permute-start.17 = (bf16[4,32,1536]{2,1,0:T(8,128)(2,1)}, bf16[4,32,1536]{2,1,0:T(8,128)(2,1)}, u32[]{:S(2)}, u32[]{:S(2)}) collective-permute-start(bf16[4,32,1536]{2,1,0:T(8,128)(2,1)} %collective-permute-done.9.refs_4_), channel_id=1, source_target_pairs={{0,1},{1,0},{2,3},{3,2},{4,5},{5,4},{6,7},{7,6},{8,9},{9,8},{10,11... | collective-permute-start | bytes 1179656 | tf_op jit(solution)/shard_map/ppermute | solution.py:365
  74.5 4.6 %collective-permute-start.18 = (bf16[4,32,1536]{2,1,0:T(8,128)(2,1)}, bf16[4,32,1536]{2,1,0:T(8,128)(2,1)}, u32[]{:S(2)}, u32[]{:S(2)}) collective-permute-start(bf16[4,32,1536]{2,1,0:T(8,128)(2,1)} %collective-permute-done.11.refs_5_), channel_id=1, source_target_pairs={{0,1},{1,0},{2,3},{3,2},{4,5},{5,4},{6,7},{7,6},{8,9},{9,8},{10,11... | collective-permute-start | bytes 1179656 | tf_op jit(solution)/shard_map/ppermute | solution.py:365
  77.2 1.2 copy-start.3
  78.3 0.8 copy-start.5
  99.5 29.0 %all-to-all-start.2 = ((f32[32,4,1024]{2,1,0:T(4,128)}), f32[32,4,1024]{2,1,0:T(4,128)S(1)}, u32[]{:S(2)}, u32[]{:S(2)}) async-start(f32[32,4,1024]{2,1,0:T(4,128)} %shard_map.88), calls=%async_computation.2 | async-start | bytes 1048576 | tf_op jit(solution)/shard_map/all_to_all | solution.py:384
  114.9 22.4 %collective-permute-start.22 = (bf16[4,384,384]{2,1,0:T(8,128)(2,1)}, bf16[4,384,384]{2,1,0:T(8,128)(2,1)}, u32[]{:S(2)}, u32[]{:S(2)}) collective-permute-start(bf16[4,384,384]{2,1,0:T(8,128)(2,1)} %get-tuple-element.40), channel_id=1, source_target_pairs={{0,1},{1,0},{2,3},{3,2},{4,5},{5,4},{6,7},{7,6},{8,9},{9,8},{10,11... | collective-permute-start | bytes 3538952 | tf_op jit(solution)/shard_map/ppermute | solution.py:375
  128.6 1.4 copy-start.2
  136.3 1.0 copy-start.7
  137.3 3.3 %collective-permute-start.21 = (bf16[1024,384]{1,0:T(8,128)(2,1)S(1)}, bf16[1024,384]{1,0:T(8,128)(2,1)S(1)}, u32[]{:S(2)}, u32[]{:S(2)}) collective-permute-start(bf16[1024,384]{1,0:T(8,128)(2,1)S(1)} %get-tuple-element.25.high_ref.own_ref), channel_id=1, source_target_pairs={{0,1},{1,0},{2,3},{3,2},{4,5},{5,4},{6,7},{7,6},{8,9},{9,8},{10,11... | collective-permute-start | bytes 2359304 | tf_op jit(solution)/shard_map/ppermute | solution.py:389
  139.2 1.4 copy-start.1
  140.6 1.0 copy-start.10
  146.5 20.3 %collective-permute-start.27 = (f32[512,384]{1,0:T(8,128)S(1)}, f32[512,384]{1,0:T(8,128)S(1)}, u32[]{:S(2)}, u32[]{:S(2)}) collective-permute-start(f32[512,384]{1,0:T(8,128)S(1)} %get-tuple-element.33), channel_id=1, source_target_pairs={{0,6},{1,7},{2,0},{3,1},{4,2},{5,3},{6,4},{7,5},{8,14},{9,15},{10,... | collective-permute-start | bytes 2359304 | tf_op jit(solution)/shard_map/ppermute | solution.py:391
  147.6 21.7 %collective-permute-start.23 = (f32[512,384]{1,0:T(8,128)S(1)}, f32[512,384]{1,0:T(8,128)S(1)}, u32[]{:S(2)}, u32[]{:S(2)}) collective-permute-start(f32[512,384]{1,0:T(8,128)S(1)} %get-tuple-element.29), channel_id=1, source_target_pairs={{0,2},{1,3},{2,4},{3,5},{4,6},{5,7},{6,0},{7,1},{8,10},{9,11},{10,... | collective-permute-start | bytes 2359304 | tf_op jit(solution)/shard_map/ppermute | solution.py:390
  148.5 37.6 %collective-permute-start.26 = (f32[512,384]{1,0:T(8,128)S(1)}, f32[512,384]{1,0:T(8,128)S(1)}, u32[]{:S(2)}, u32[]{:S(2)}) collective-permute-start(f32[512,384]{1,0:T(8,128)S(1)} %get-tuple-element.31), channel_id=1, source_target_pairs={{0,2},{1,3},{2,4},{3,5},{4,6},{5,7},{6,0},{7,1},{8,10},{9,11},{10,... | collective-permute-start | bytes 2359304 | tf_op jit(solution)/shard_map/ppermute | solution.py:392
  149.1 51.1 %collective-permute-start.25 = (f32[512,384]{1,0:T(8,128)S(1)}, f32[512,384]{1,0:T(8,128)S(1)}, u32[]{:S(2)}, u32[]{:S(2)}) collective-permute-start(f32[512,384]{1,0:T(8,128)S(1)} %get-tuple-element.30), channel_id=1, source_target_pairs={{0,6},{1,7},{2,0},{3,1},{4,2},{5,3},{6,4},{7,5},{8,14},{9,15},{10,... | collective-permute-start | bytes 2359304 | tf_op jit(solution)/shard_map/ppermute | solution.py:393
  166.9 33.2 %collective-permute-start.28 = (f32[512,384]{1,0:T(8,128)S(1)}, f32[512,384]{1,0:T(8,128)S(1)}, u32[]{:S(2)}, u32[]{:S(2)}) collective-permute-start(f32[512,384]{1,0:T(8,128)S(1)} %add.51), channel_id=1, source_target_pairs={{0,6},{1,7},{2,0},{3,1},{4,2},{5,3},{6,4},{7,5},{8,14},{9,15},{10,... | collective-permute-start | bytes 2359304 | tf_op jit(solution)/shard_map/ppermute | solution.py:395
  169.4 32.8 %collective-permute-start.24 = (f32[512,384]{1,0:T(8,128)S(1)}, f32[512,384]{1,0:T(8,128)S(1)}, u32[]{:S(2)}, u32[]{:S(2)}) collective-permute-start(f32[512,384]{1,0:T(8,128)S(1)} %add.49), channel_id=1, source_target_pairs={{0,2},{1,3},{2,4},{3,5},{4,6},{5,7},{6,0},{7,1},{8,10},{9,11},{10,... | collective-permute-start | bytes 2359304 | tf_op jit(solution)/shard_map/ppermute | solution.py:394
  200.2 2.1 copy-start.9
  203.6 7.7 %copy-start.8 = (bf16[1024,384]{1,0:T(8,128)(2,1)S(1)}, bf16[1024,384]{1,0:T(8,128)(2,1)}, u32[]{:S(2)}) copy-start(bf16[1024,384]{1,0:T(8,128)(2,1)} %copy-done.7) | copy-start | bytes 2359300
  203.6 44.6 %all-to-all-start.3 = ((f32[32,32,384]{2,1,0:T(8,128)}), f32[32,32,384]{2,1,0:T(8,128)S(1)}, u32[]{:S(2)}, u32[]{:S(2)}) async-start(f32[32,32,384]{2,1,0:T(8,128)} %bitcast.37), calls=%async_computation.3 | async-start | bytes 3145728 | tf_op jit(solution)/shard_map/all_to_all | solution.py:398
  211.3 1.9 copy-start.6

commit v3 on v2

--- a/solution.py
+++ b/solution.py
@@ -19,8 +19,7 @@
 BLOCK = 256
 BF16 = jnp.bfloat16
 F32 = jnp.float32
-VMEM_LIMIT = 48 * 1024 * 1024
-PARAMS = pltpu.CompilerParams(vmem_limit_bytes=VMEM_LIMIT)
+PARAMS = pltpu.CompilerParams(vmem_limit_bytes=24 * 1024 * 1024)
 VMEM = pl.BlockSpec(memory_space=pltpu.VMEM)
 SMEM = pl.BlockSpec(memory_space=pltpu.SMEM)
 
@@ -44,38 +43,6 @@
     )(x)
 
 
-def target_kernel(gid_ref, live_ref, p_ref, psum_ref, stat_ref):
-    base = pl.program_id(0) * BLOCK
-    rows = lax.broadcasted_iota(jnp.int32, (BLOCK, ROWS), 0) + base
-    hot = jnp.where(gid_ref[...] == rows, live_ref[...], 0.0).astype(BF16)
-    psum = dot(hot, p_ref[...])
-    psum_ref[...] = psum
-    lane = lax.broadcasted_iota(jnp.int32, (BLOCK, 128), 1)
-    mass = jnp.sum(psum, axis=1, keepdims=True)
-    stat_ref[...] = jnp.where(lane == 1, mass, 0.0)
-
-
-def target_sums(gid, live, probs):
-    return pl.pallas_call(
-        target_kernel,
-        grid=(ROWS // BLOCK,),
-        out_shape=(
-            jax.ShapeDtypeStruct((ROWS, LOCAL), F32),
-            jax.ShapeDtypeStruct((ROWS, 128), F32),
-        ),
-        in_specs=[
-            pl.BlockSpec((1, ROWS), lambda i: (0, 0)),
-            pl.BlockSpec((1, ROWS), lambda i: (0, 0)),
-            pl.BlockSpec((ROWS, LOCAL), lambda i: (0, 0)),
-        ],
-        out_specs=(
-            pl.BlockSpec((BLOCK, LOCAL), lambda i: (i, 0)),
-            pl.BlockSpec((BLOCK, 128), lambda i: (i, 0)),
-        ),
-        compiler_params=PARAMS,
-    )(gid, live, probs)
-
-
 Z = 8
 Y = 4
 PIECE = (Z // 2, SLOTS, HALF)
@@ -83,7 +50,7 @@
 
 def logit_kernel(at_ref, *refs):
     pieces, refs = refs[:16], refs[16:]
-    w_ref, psum_ref, stat_ref, own_ref, other_ref, logits_ref, o_ref = refs
+    w_ref, own_ref, other_ref, logits_ref, o_ref = refs
     c, y, z = at_ref[0], at_ref[1], at_ref[2]
     for side, tab_ref in enumerate((own_ref, other_ref)):
         for dy in range(Y):
@@ -105,15 +72,14 @@
         logits_ref[rows, :] = logits
         top = jnp.max(logits, axis=1, keepdims=True)
         lse = top + jnp.log(jnp.sum(jnp.exp(logits - top), axis=1, keepdims=True))
-        cross = jnp.sum(psum_ref[rows, :] * logits, axis=1, keepdims=True)
-        lane = lax.broadcasted_iota(jnp.int32, (block, 128), 1)
-        stat = jnp.where(lane == 0, lse, jnp.where(lane == 2, cross, stat_ref[rows, :]))
-        flat = stat.T[0:4]
-        for k in range(SHARDS):
-            o_ref[k, :, rows] = flat
-
-
-def logits_and_stats(at, pieces, weight, psum, stat):
+        flat = jnp.broadcast_to(lse, (block, 128)).T
+        for j in range(block // 128):
+            row = flat[0:1, j * 128 : (j + 1) * 128]
+            for k in range(SHARDS):
+                o_ref[k, pl.ds(i * (block // 128) + j, 1), :] = row
+
+
+def logits_and_stats(at, pieces, weight):
     table = jax.ShapeDtypeStruct((ROWS, HALF), BF16)
     return pl.pallas_call(
         logit_kernel,
@@ -121,33 +87,29 @@
             table,
             table,
             jax.ShapeDtypeStruct((ROWS, LOCAL), F32),
-            jax.ShapeDtypeStruct((SHARDS, 4, ROWS), F32),
-        ),
-        in_specs=[SMEM] + [VMEM] * 19,
+            jax.ShapeDtypeStruct((SHARDS, 8, 128), F32),
+        ),
+        in_specs=[SMEM] + [VMEM] * 17,
         out_specs=(VMEM,) * 4,
         compiler_params=PARAMS,
-    )(at, *pieces, weight, psum, stat)
+    )(at, *pieces, weight)
 
 
 def merge(x):
-    lse = x[:, 0, :]
-    top = jnp.max(lse, axis=0, keepdims=True)
-    lse = top + jnp.log(jnp.sum(jnp.exp(lse - top), axis=0, keepdims=True))
-    rest = jnp.sum(x[:, 1:3, :], axis=0)
-    return lse, rest[0:1], rest[1:2]
+    top = jnp.max(x, axis=0)
+    return top + jnp.log(jnp.sum(jnp.exp(x - top[None]), axis=0))
 
 
 def merge_kernel(x_ref, o_ref):
-    lse, mass, cross = merge(x_ref[...])
-    flat = jnp.concatenate([lse, mass, cross, jnp.zeros_like(lse)], axis=0)
+    lse = merge(x_ref[...])
     for k in range(TRAINERS):
-        o_ref[k] = flat
+        o_ref[k] = lse
 
 
 def merge_stats(x):
     return pl.pallas_call(
         merge_kernel,
-        out_shape=jax.ShapeDtypeStruct((TRAINERS, 4, ROWS), F32),
+        out_shape=jax.ShapeDtypeStruct((TRAINERS, 8, 128), F32),
         in_specs=[VMEM],
         out_specs=VMEM,
         compiler_params=PARAMS,
@@ -159,14 +121,14 @@
 
 
 def grad_kernel(
-    x_ref, logits_ref, p_ref, gid_ref, live_ref, high_ref, low_ref, loss_ref, parts_ref, g_ref
+    x_ref, logits_ref, p_ref, gid_ref, live_ref, high_ref, low_ref, loss_ref, parts_ref, gp_ref, lse_ref
 ):
-    lse, mass, cross = merge(x_ref[...])
-    loss_ref[0, 0] = jnp.sum(lse * mass - cross)
-    lse_col = column(lse)
+    lse = merge(x_ref[...])
+    for j in range(8):
+        lse_ref[pl.ds(j * 128, 128), :] = column(lse[j : j + 1])
     for j in range(LOCAL // 128):
         cols = pl.ds(j * 128, 128)
-        p = jnp.exp(logits_ref[:, cols] - lse_col)
+        p = jnp.exp(logits_ref[:, cols] - lse_ref[...])
         first = p.astype(BF16)
         p = p - first.astype(F32)
         second = p.astype(BF16)
@@ -180,7 +142,7 @@
     def _(i):
         rows = pl.ds(pl.multiple_of(i * BLOCK, BLOCK), BLOCK)
         gid = column(gid_ref[:, rows])
-        live = column(live_ref[:, rows])
+        factor = column(live_ref[:, rows]) * scale
         lane = lax.broadcasted_iota(jnp.int32, (BLOCK, 128), 1).astype(F32)
         hot = jnp.concatenate(
             [
@@ -191,24 +153,28 @@
         )
         sel = dot(hot, parts_ref[...])
         p = sel[:, 0:LOCAL] + sel[:, LOCAL : 2 * LOCAL] + sel[:, 2 * LOCAL :]
-        diff = p - p_ref[rows, :].astype(F32)
-        factor = live * scale
-        g = jnp.concatenate(
-            [factor * diff[:, j * 128 : (j + 1) * 128] for j in range(LOCAL // 128)],
-            axis=1,
-        )
-        g_ref[rows, :] = g.astype(BF16)
-
-    @pl.loop(0, ROWS // BLOCK)
-    def _(i):
+        targets = p_ref[rows, :]
+        diff = p - targets.astype(F32)
+        for j in range(LOCAL // 128):
+            cols = slice(j * 128, (j + 1) * 128)
+            gp_ref[rows, cols] = (factor * diff[:, cols]).astype(BF16)
+        gp_ref[rows, LOCAL:] = targets
+
+    def total(i, loss):
         rows = pl.ds(pl.multiple_of(i * BLOCK, BLOCK), BLOCK)
         row = lax.broadcasted_iota(jnp.int32, (BLOCK, ROWS), 0) + i * BLOCK
-        hot = jnp.where(gid_ref[...] == row.astype(F32), 1.0, 0.0).astype(BF16)
-        total = dot(hot, g_ref[...])
-        high = total.astype(BF16)
-        low = (total - high.astype(F32)).astype(BF16)
+        hot = jnp.where(gid_ref[...] == row.astype(F32), live_ref[...], 0.0).astype(BF16)
+        sums = dot(hot, gp_ref[...])
+        high = sums[:, 0:LOCAL].astype(BF16)
         high_ref[rows, :] = high
-        low_ref[rows, :] = low
+        low_ref[rows, :] = (sums[:, 0:LOCAL] - high.astype(F32)).astype(BF16)
+        for j in range(LOCAL // 128):
+            cols = pl.ds(j * 128, 128)
+            gap = lse_ref[rows, :] - logits_ref[rows, cols]
+            loss += jnp.sum(sums[:, LOCAL + j * 128 : LOCAL + (j + 1) * 128] * gap)
+        return loss
+
+    loss_ref[0, 0] = lax.fori_loop(0, ROWS // BLOCK, total, jnp.float32(0))
 
 
 def gradients(x, logits, probs, gid, live):
@@ -223,10 +189,60 @@
         out_specs=(VMEM, VMEM, SMEM),
         scratch_shapes=[
             pltpu.VMEM((ROWS, 3 * LOCAL), BF16),
-            pltpu.VMEM((ROWS, LOCAL), BF16),
+            pltpu.VMEM((ROWS, 2 * LOCAL), BF16),
+            pltpu.VMEM((ROWS, 128), F32),
         ],
         compiler_params=PARAMS,
     )(x, logits, probs, gid, live)
+
+
+TOP = 32700.0
+ROWS2 = ROWS // 2
+TAIL = 16
+I16 = jnp.int16
+
+
+def exponent(x):
+    return jnp.ceil(jnp.log(jnp.maximum(x, 1e-30) / TOP) * (256.0 / math.log(2.0)))
+
+
+def power(e):
+    return jnp.exp2(e * (1.0 / 256.0))
+
+
+def to16(x):
+    return x.astype(jnp.int32).astype(I16)
+
+
+def from16(x):
+    return x.astype(jnp.int32).astype(F32)
+
+
+def encode(val):
+    e = exponent(jnp.max(jnp.abs(val), axis=1, keepdims=True))
+    return to16(jnp.round(val * power(-e))), jnp.broadcast_to(e, (128, 128)).T[0:1]
+
+
+def write_message(out_ref, block_of):
+    tail = []
+    for j in range(ROWS2 // 128):
+        code, e = encode(block_of(j))
+        out_ref[pl.ds(j * 128, 128), :] = code
+        tail.append(e)
+    tail.append(jnp.zeros((TAIL - len(tail), 128), F32))
+    tail = jnp.concatenate(tail, axis=0)
+    tail = jnp.concatenate([tail] + [jnp.zeros_like(tail)] * (LOCAL // 128 - 1), axis=1)
+    out_ref[pl.ds(ROWS2, TAIL), :] = to16(tail)
+
+
+def read_message(ref, j):
+    tail = from16(ref[pl.ds(ROWS2, TAIL), 0:128])
+    scale = power(column(tail[j : j + 1]))
+    rows = pl.ds(j * 128, 128)
+    return [from16(ref[rows, k * 128 : (k + 1) * 128]) * scale for k in range(LOCAL // 128)]
+
+
+MESSAGE = jax.ShapeDtypeStruct((ROWS2 + TAIL, LOCAL), I16)
 
 
 def weight_kernel(x_ref, own_ref, other_ref, o_ref):
@@ -247,32 +263,127 @@
     )(x, own, other)
 
 
-ROWS2 = ROWS // 2
-
-
-def term_kernel(own_ref, other_ref, w_ref, c0, l1, h1, l2, h2, l3, h3, g_ref):
+def term_kernel(own_ref, other_ref, w_ref, c0, l1, h1, l2, h2, l3, h3, g_ref, val_ref):
     g_ref[:, 0:LOCAL] = own_ref[...]
     g_ref[:, LOCAL:] = other_ref[...]
-    outs = {1: (l1, h1), 2: (l2, h2), 3: (l3, h3)}
-
+    outs = {2: (l2, h2), 1: (l1, h1), 3: (l3, h3)}
     for i in range(2):
         rows = pl.ds(i * ROWS2, ROWS2)
-        val = dot(g_ref[rows, :], w_ref[...])
-        c0[rows, :] = val[:, 0:LOCAL]
-        for k in range(1, 4):
-            outs[k][i][...] = val[:, k * LOCAL : (k + 1) * LOCAL]
+        val_ref[...] = dot(g_ref[rows, :], w_ref[...])
+        c0[rows, :] = val_ref[:, 0:LOCAL]
+        for k in (1, 2, 3):
+            out, cols = outs[k][i], slice(k * LOCAL, (k + 1) * LOCAL)
+            if out.dtype == F32:
+                out[...] = val_ref[:, cols]
+            else:
+                write_message(out, lambda j: val_ref[pl.ds(j * 128, 128), cols])
 
 
 def terms(own, other, weights):
     part = jax.ShapeDtypeStruct((ROWS2, LOCAL), F32)
     return pl.pallas_call(
         term_kernel,
-        out_shape=(jax.ShapeDtypeStruct((ROWS, LOCAL), F32),) + (part,) * 6,
+        out_shape=(
+            jax.ShapeDtypeStruct((ROWS, LOCAL), F32),
+            part,
+            MESSAGE,
+            MESSAGE,
+            MESSAGE,
+            MESSAGE,
+            part,
+        ),
         in_specs=[VMEM] * 3,
         out_specs=(VMEM,) * 7,
-        scratch_shapes=[pltpu.VMEM((ROWS, 2 * LOCAL), BF16)],
+        scratch_shapes=[
+            pltpu.VMEM((ROWS, 2 * LOCAL), BF16),
+            pltpu.VMEM((ROWS2, 4 * LOCAL), F32),
+        ],
         compiler_params=PARAMS,
     )(own, other, weights)
+
+
+def relay_kernel(own_ref, got_ref, out_ref):
+    def block(j):
+        got = jnp.concatenate(read_message(got_ref, j), axis=1)
+        return own_ref[pl.ds(j * 128, 128), :] + got
+
+    write_message(out_ref, block)
+
+
+def relay(own, got):
+    return pl.pallas_call(
+        relay_kernel,
+        out_shape=MESSAGE,
+        in_specs=[VMEM] * 2,
+        out_specs=VMEM,
+        compiler_params=PARAMS,
+    )(own, got)
+
+
+PACKED = 3 * SLOTS + TAIL
+
+
+def pack_kernel(loss_ref, own_ref, low_r, low_l, high_r, high_l, o_ref):
+    loss = jnp.full((1, 128), loss_ref[0, 0], F32)
+    e = exponent(jnp.abs(loss))
+    whole = loss * power(-e)
+    first = jnp.round(whole)
+    rest = jnp.round((whole - first) * TOP)
+    lane = lax.broadcasted_iota(jnp.int32, (1, 128), 1)
+    loss = jnp.where(lane == 0, e, jnp.where(lane == 1, first, jnp.where(lane == 2, rest, 0.0)))
+    pad = jnp.zeros((TAIL - 2, 128), F32)
+    for i, (right, left) in enumerate(((low_r, low_l), (high_r, high_l))):
+        for j in range(ROWS2 // 128):
+            a, b = read_message(right, j), read_message(left, j)
+            val = jnp.concatenate([p + q for p, q in zip(a, b)], axis=1)
+            at = i * (ROWS2 // 128) + j
+            code, e = encode(own_ref[pl.ds(at * 128, 128), :] + val)
+            tail = to16(jnp.concatenate([e, loss, pad], axis=0))
+            for n in range(128 // SLOTS):
+                for k in range(3):
+                    o_ref[at * 4 + n, k * SLOTS : (k + 1) * SLOTS, :] = code[
+                        n * SLOTS : (n + 1) * SLOTS, k * 128 : (k + 1) * 128
+                    ]
+                o_ref[at * 4 + n, 3 * SLOTS :, :] = tail
+
+
+def pack(loss, own, low_r, low_l, high_r, high_l):
+    return pl.pallas_call(
+        pack_kernel,
+        out_shape=jax.ShapeDtypeStruct((TRAINERS, PACKED, 128), I16),
+        in_specs=[SMEM] + [VMEM] * 5,
+        out_specs=VMEM,
+        compiler_params=PARAMS,
+    )(loss, own, low_r, low_l, high_r, high_l)
+
+
+def finish_kernel(at_ref, x_ref, grad_ref, loss_ref, e_ref):
+    tail = from16(x_ref[:, 3 * SLOTS :, :])
+    e = tail[:, 0, :]
+    e_ref[...] = jnp.concatenate([e, jnp.zeros((128 - TRAINERS, 128), F32)], axis=0).T
+    scale = power(e_ref[pl.ds(pl.multiple_of(at_ref[0] * SLOTS, SLOTS), SLOTS), :])
+    total = [jnp.zeros((SLOTS, 128), F32)] * 3
+    for s in range(TRAINERS):
+        for k in range(3):
+            total[k] += from16(x_ref[s, k * SLOTS : (k + 1) * SLOTS, :]) * scale[:, s : s + 1]
+    for k in range(3):
+        grad_ref[:, k * 128 : (k + 1) * 128] = total[k]
+    loss = tail[:, 1, :]
+    loss_ref[0, 0] = jnp.sum((loss[:, 1:2] + loss[:, 2:3] * (1.0 / TOP)) * power(loss[:, 0:1]))
+
+
+def finish(at, x):
+    return pl.pallas_call(
+        finish_kernel,
+        out_shape=(
+            jax.ShapeDtypeStruct((SLOTS, LOCAL), F32),
+            jax.ShapeDtypeStruct((1, 1), F32),
+        ),
+        in_specs=[SMEM, VMEM],
+        out_specs=(VMEM, SMEM),
+        scratch_shapes=[pltpu.VMEM((128, 128), F32)],
+        compiler_params=PARAMS,
+    )(at, x)
 
 
 HEAD_BLOCK = 256
@@ -337,7 +448,7 @@
     return [(i, i // Y * Y + (i + k) % Y) for i in range(TRAINERS)]
 
 
-def gather_pieces(half):
+def gather_pieces(half, targets):
     near = [half] + [lax.ppermute(half, "trainer", along_z(k)) for k in range(1, Z)]
     low0 = jnp.stack(near[: Z // 2])
     high0 = jnp.stack(near[Z // 2 :])
@@ -345,9 +456,11 @@
     high3 = lax.ppermute(high0, "trainer", along_y(-1))
     high1 = lax.ppermute(high0, "trainer", along_y(1))
     low3 = lax.ppermute(low0, "trainer", along_y(-1))
+    targets, _ = lax.optimization_barrier((targets, high0))
+    probs = lax.all_to_all(targets, "trainer", split_axis=0, concat_axis=0, tiled=True)
     low2 = lax.ppermute(low1, "trainer", along_y(1))
     high2 = lax.ppermute(high3, "trainer", along_y(-1))
-    return low0, high0, low1, high1, low2, high2, low3, high3
+    return (low0, high0, low1, high1, low2, high2, low3, high3), probs.reshape(ROWS, LOCAL)
 
 
 def on_device(hidden_table, head_weight, targets, counts, dest, token):
@@ -361,13 +474,8 @@
     weight = head_weight[:, 0, :]
 
     half = lax.dynamic_slice(hidden_table, (0, c * HALF), (SLOTS, HALF))
-    pieces = gather_pieces(half)
+    pieces, probs = gather_pieces(half, split_targets(targets[:, 0, :]))
     pieces += tuple(lax.ppermute(p, "vocab", PAIR) for p in pieces)
-
-    moved = lax.all_to_all(
-        split_targets(targets[:, 0, :]), "trainer", split_axis=0, concat_axis=0, tiled=True
-    )
-    probs = moved.reshape(ROWS, LOCAL)
 
     blocks = weight.reshape(4, 2, LOCAL, LOCAL)
     w_own = lax.dynamic_index_in_dim(blocks, c, axis=1, keepdims=False)
@@ -377,28 +485,27 @@
     gid = dest * SLOTS + token
     index = jnp.arange(ROWS, dtype=jnp.int32)
     live = (index % SLOTS < jnp.repeat(counts, SLOTS)).astype(F32).reshape(1, ROWS)
-    psum, mass = target_sums(gid.reshape(1, ROWS), live, probs)
-
-    own, other, logits, stats = logits_and_stats(at, pieces, weight, psum, mass)
+
+    at, weights = lax.optimization_barrier((at, weights))
+    own, other, logits, stats = logits_and_stats(at, pieces, weight)
     stats = lax.all_to_all(stats, "vocab", split_axis=0, concat_axis=0, tiled=True)
     stats = lax.all_to_all(merge_stats(stats), "trainer", split_axis=0, concat_axis=0, tiled=True)
 
     high, low, loss = gradients(stats, logits, probs, gid.astype(F32).reshape(1, ROWS), live)
-    mean_loss = loss[0, 0] / jnp.sum(counts).astype(F32)
 
     t0, l1, h1, l2, h2, l3, h3 = terms(high, lax.ppermute(high, "vocab", PAIR), weights)
     low_r = lax.ppermute(l2, "vocab", RIGHT)
     high_l = lax.ppermute(h2, "vocab", LEFT)
     high_r = lax.ppermute(h1, "vocab", RIGHT)
     low_l = lax.ppermute(l3, "vocab", LEFT)
-    low_r = lax.ppermute(l1 + low_r, "vocab", RIGHT)
-    high_l = lax.ppermute(h3 + high_l, "vocab", LEFT)
+    low_r = lax.ppermute(relay(l1, low_r), "vocab", RIGHT)
+    high_l = lax.ppermute(relay(h3, high_l), "vocab", LEFT)
     head = head_gradient(c1, own, other, high, low)
-    total = t0 + jnp.concatenate([low_r + low_l, high_r + high_l], axis=0)
-    got = lax.all_to_all(
-        total.reshape(TRAINERS, SLOTS, LOCAL), "trainer", split_axis=0, concat_axis=0, tiled=True
-    )
-    table_grad = jnp.sum(got, axis=0)
+    loss = lax.psum(loss, "vocab")
+    packed = pack(loss, t0, low_r, low_l, high_r, high_l)
+    packed = lax.all_to_all(packed, "trainer", split_axis=0, concat_axis=0, tiled=True)
+    table_grad, loss = finish(lax.rem(trainer, 4).reshape(1).astype(jnp.int32), packed)
+    mean_loss = loss[0, 0] / jnp.sum(counts).astype(F32)
     return head.reshape(D, 1, LOCAL), table_grad, mean_loss
 
 

time: 251 us -> 223 us (0.89)
  waiting for transfers between devices: 118 us -> 75.8 us
  blocking collectives: 10.2 us -> 30.9 us
  starting transfers between devices: 62.4 us -> 49.2 us
  local copies, waits for them, and re-layouts: 13.7 us -> 25.6 us
  Pallas kernels: 38.8 us -> 36.2 us
    psum x0 -> x1, blocking collectives: none -> 21.3 us  [on_device(): loss = lax.psum(loss, 'vocab')]
    ppermute x1, waiting for transfers between devices: 16.6 us -> 0.01 us  [on_device(): high_r = lax.ppermute(h1, 'vocab', RIGHT)]
    ppermute x2, waiting for transfers between devices: 16 us -> 0.01 us  [the longest x1 0.01 us: on_device(): high_l = lax.ppermute(relay(h3, high_l), 'vocab', LEFT)]
    unnamed x28 -> x60, local copies, waits for them, and re-layouts: 10.6 us -> 22.6 us
    ppermute x7, waiting for transfers between devices: 17.6 us -> 9.96 us  [gather_pieces(): lax.ppermute(half, 'trainer', along_z(k))]
    ppermute x1, waiting for transfers between devices: 15.1 us -> 7.82 us  [on_device(): high_l = lax.ppermute(h2, 'vocab', LEFT)]
    all_to_all x2, waiting for transfers between devices: 22.6 us -> 29.8 us  [the longest x1 21.1 us: gather_pieces(): lax.all_to_all(targets, 'trainer', split_axis=0, concat_axis=0, tiled=True)]
    ppermute x1, waiting for transfers between devices: 7.07 us -> 0.01 us  [gather_pieces(): low3 = lax.ppermute(low0, 'trainer', along_y(-1))]
  transfers between devices with their start and end apart: 32 -> 32, of which waited for: 12 -> 14; matrix products, arithmetic and copies ran while one was open for 2% -> 2% of each run, Pallas kernels for 10% -> 6%
where the time goes in v3:
time: 223 us; the launch traced here: 222 us
  waiting for transfers between devices  75.8 us (34%)
  starting transfers between devices  49.2 us (22%)
  Pallas kernels  36.2 us (16%)
  blocking collectives  30.9 us (14%)
  local copies, waits for them, and re-layouts  25.6 us (11%)
  between operations  3.37 us (2%)
    unnamed x60, local copies, waits for them, and re-layouts  22.6 us
    psum x1, blocking collectives, on_device(): loss = lax.psum(loss, 'vocab')  21.3 us
    all_to_all x1, waiting for transfers between devices, gather_pieces(): lax.all_to_all(targets, 'trainer', split_axis=0, concat_axis=0, tiled=True)  21.1 us
    ppermute x7, starting transfers between devices, gather_pieces(): lax.ppermute(half, 'trainer', along_z(k))  15.6 us
    pallas_call x1, Pallas kernels, head_gradient(): pl.pallas_call(head_kernel, grid_spec=pltpu.PrefetchScalarGridSpec(num_sc...  10.5 us
    ppermute x7, waiting for transfers between devices, gather_pieces(): lax.ppermute(half, 'trainer', along_z(k))  9.96 us
    all_to_all x1, blocking collectives, on_device(): lax.all_to_all(stats, 'vocab', split_axis=0, concat_axis=0, tiled=True)  9.64 us
    all_to_all x1, waiting for transfers between devices, on_device(): lax.all_to_all(packed, 'trainer', split_axis=0, concat_axis=0, tiled=True)  8.68 us
  transfers between devices with their start and end apart: 32, of which 14 were waited for; matrix products, arithmetic and copies ran while one was open for 2% of the time, Pallas kernels for 6%

profile of v3, /device:TPU:8, one launch (start us, length us, event | category | flops | bytes accessed | tf_op | source)
XLA Modules:
  0.0 221.9 jit_solution(9919599680127807033)
XLA Ops:
  1.6 7.3 %collective-permute-start.4 = (bf16[32,1536]{1,0:T(8,128)(2,1)S(1)}, bf16[32,1536]{1,0:T(8,128)(2,1)S(1)}, u32[]{:S(2)}, u32[]{:S(2)}) collective-permute-start(bf16[32,1536]{1,0:T(8,128)(2,1)S(1)} %constant_dynamic-slice_fusion), channel_id=1, source_target_pairs={{0,128},{8,136},{16,144},{24,152},{32,160},{40,168},{48,176},{56,1... | collective-permute-start | bytes 294920 | tf_op jit(solution)/shard_map/ppermute | solution.py:452
  8.8 4.6 %collective-permute-start.6 = (bf16[32,1536]{1,0:T(8,128)(2,1)S(1)}, bf16[32,1536]{1,0:T(8,128)(2,1)S(1)}, u32[]{:S(2)}, u32[]{:S(2)}) collective-permute-start(bf16[32,1536]{1,0:T(8,128)(2,1)S(1)} %constant_dynamic-slice_fusion), channel_id=1, source_target_pairs={{0,192},{8,200},{16,208},{24,216},{32,224},{40,232},{48,240},{56,2... | collective-permute-start | bytes 294920 | tf_op jit(solution)/shard_map/ppermute | solution.py:452
  14.5 2.9 %dynamic-slice_bitcast_fusion = (bf16[4,384,384]{2,1,0:T(8,128)(2,1)S(1)}, bf16[4,384,384]{2,1,0:T(8,128)(2,1)}) fusion(bf16[4,2,384,384]{3,2,1,0:T(8,128)(2,1)} %bitcast.28, s32[]{:T(128)S(6)} %select_n.34, s32[]{:T(128)S(6)} %select_n.33), kind=kLoop, calls=%fused_computation | loop fusion | bytes 4718600 | tf_op jit(solution)/shard_map/jit(dynamic_index_in_dim)/squeeze | solution.py:482
  17.3 1.5 collective-permute-start.1
  18.8 1.6 collective-permute-done.5
  20.4 1.3 collective-permute-start.2
  21.7 3.1 %collective-permute-done.6 = bf16[32,1536]{1,0:T(8,128)(2,1)S(1)} collective-permute-done((bf16[32,1536]{1,0:T(8,128)(2,1)S(1)}, bf16[32,1536]{1,0:T(8,128)(2,1)S(1)}, u32[]{:S(2)}, u32[]{:S(2)}) %collective-permute-start.6) | collective-permute-done | bytes 98336 | tf_op jit(solution)/shard_map/ppermute | solution.py:452
  24.8 2.3 %collective-permute-done.7 = bf16[32,1536]{1,0:T(8,128)(2,1)S(1)} collective-permute-done((bf16[32,1536]{1,0:T(8,128)(2,1)S(1)}, bf16[32,1536]{1,0:T(8,128)(2,1)S(1)}, u32[]{:S(2)}, u32[]{:S(2)}) %collective-permute-start.7) | collective-permute-done | bytes 98336 | tf_op jit(solution)/shard_map/ppermute | solution.py:452
  27.8 2.9 %collective-permute-done.2 = bf16[32,1536]{1,0:T(8,128)(2,1)S(1)} collective-permute-done((bf16[32,1536]{1,0:T(8,128)(2,1)S(1)}, bf16[32,1536]{1,0:T(8,128)(2,1)S(1)}, u32[]{:S(2)}, u32[]{:S(2)}) %collective-permute-start.2) | collective-permute-done | bytes 98336 | tf_op jit(solution)/shard_map/ppermute | solution.py:452
  30.7 1.7 collective-permute-start.8
  32.4 1.3 collective-permute-start.9
  34.4 5.1 %collective-permute-done.11.refs_7_ = bf16[4,32,1536]{2,1,0:T(8,128)(2,1)} collective-permute-done((bf16[4,32,1536]{2,1,0:T(8,128)(2,1)S(1)}, bf16[4,32,1536]{2,1,0:T(8,128)(2,1)}, u32[]{:S(2)}, u32[]{:S(2)}) %collective-permute-start.11) | collective-permute-done | bytes 393248 | tf_op jit(solution)/shard_map/ppermute | solution.py:456
  39.5 3.5 %collective-permute-done.8.refs_2_ = bf16[4,32,1536]{2,1,0:T(8,128)(2,1)} collective-permute-done((bf16[4,32,1536]{2,1,0:T(8,128)(2,1)S(1)}, bf16[4,32,1536]{2,1,0:T(8,128)(2,1)}, u32[]{:S(2)}, u32[]{:S(2)}) %collective-permute-start.8) | collective-permute-done | bytes 393248 | tf_op jit(solution)/shard_map/ppermute | solution.py:455
  42.9 5.2 %collective-permute-done.9.refs_3_ = bf16[4,32,1536]{2,1,0:T(8,128)(2,1)S(1)} collective-permute-done((bf16[4,32,1536]{2,1,0:T(8,128)(2,1)S(1)}, bf16[4,32,1536]{2,1,0:T(8,128)(2,1)S(1)}, u32[]{:S(2)}, u32[]{:S(2)}) %collective-permute-start.9) | collective-permute-done | bytes 393248 | tf_op jit(solution)/shard_map/ppermute | solution.py:457
  48.2 1.9 collective-permute-start.12
  53.0 3.6 %collective-permute-done.12.refs_5_ = bf16[4,32,1536]{2,1,0:T(8,128)(2,1)} collective-permute-done((bf16[4,32,1536]{2,1,0:T(8,128)(2,1)}, bf16[4,32,1536]{2,1,0:T(8,128)(2,1)}, u32[]{:S(2)}, u32[]{:S(2)}) %collective-permute-start.12) | collective-permute-done | bytes 393248 | tf_op jit(solution)/shard_map/ppermute | solution.py:462
  56.6 1.7 collective-permute-done.10.refs_4_
  60.8 1.3 copy-done.2
  62.0 1.3 copy-done.9
  65.4 6.7 %shard_map.86 = (bf16[1024,1536]{1,0:T(8,128)(2,1)S(1)}, bf16[1024,1536]{1,0:T(8,128)(2,1)S(1)}, f32[1024,384]{1,0:T(8,128)S(1)}, f32[8,8,128]{2,1,0:T(8,128)S(1)}) custom-call(s32[3]{0:T(128)S(1)} %pad_add_fusion.at_ref, bf16[4,32,1536]{2,1,0:T(8,128)(2,1)S(1)} %pad_maximum_fusion.refs_0_, bf16[4,32,1536]{2,1,0:T(8,128)(2,1)S(1)} %pad_maximum_fusion.1.refs_1_, ...), custom_call_target="tpu_custom_call" | custom-call | tf_op jit(solution)/shard_map/pallas_call | solution.py:84
  72.1 1.2 copy-done.6
  73.2 1.7 copy-done.21
  74.9 1.6 copy-done.23
  76.5 9.6 %all_to_all.20.x_ref = f32[8,8,128]{2,1,0:T(8,128)S(1)} all-to-all(f32[8,8,128]{2,1,0:T(8,128)S(1)} %get-tuple-element.25), channel_id=1, replica_groups=mesh['trainer'=32,'vocab'=8] {'vocab'}, dimensions={0} | all-to-all | bytes 65536 | tf_op jit(solution)/shard_map/all_to_all | solution.py:491
  86.9 8.4 %all-to-all-start.1 = ((f32[32,8,128]{2,1,0:T(8,128)}), f32[32,8,128]{2,1,0:T(8,128)S(1)}, u32[]{:S(2)}, u32[]{:S(2)}) async-start(f32[32,8,128]{2,1,0:T(8,128)} %shard_map.87), calls=%async_computation.1 | async-start | bytes 262144 | tf_op jit(solution)/shard_map/all_to_all | solution.py:492
  95.2 1.1 copy-done.10
  97.3 6.8 %all-to-all-done.1.x_ref = f32[32,8,128]{2,1,0:T(8,128)S(1)} async-done(((f32[32,8,128]{2,1,0:T(8,128)}), f32[32,8,128]{2,1,0:T(8,128)S(1)}, u32[]{:S(2)}, u32[]{:S(2)}) %all-to-all-start.1) | async-done | bytes 131104 | tf_op jit(solution)/shard_map/all_to_all | solution.py:492
  104.1 5.4 %all-to-all-start.2 = ((bf16[32,32,384]{2,1,0:T(8,128)(2,1)}), bf16[32,32,384]{2,1,0:T(8,128)(2,1)S(1)}, u32[]{:S(2)}, u32[]{:S(2)}) async-start(bf16[32,32,384]{2,1,0:T(8,128)(2,1)} %copy-done.3), calls=%async_computation.2 | async-start | bytes 1572864 | tf_op jit(solution)/shard_map/all_to_all | solution.py:460
  109.7 21.1 %all-to-all-done.2 = bf16[32,32,384]{2,1,0:T(8,128)(2,1)S(1)} async-done(((bf16[32,32,384]{2,1,0:T(8,128)(2,1)}), bf16[32,32,384]{2,1,0:T(8,128)(2,1)S(1)}, u32[]{:S(2)}, u32[]{:S(2)}) %all-to-all-start.2) | async-done | bytes 786464 | tf_op jit(solution)/shard_map/all_to_all | solution.py:460
  130.9 1.4 copy-done.7
  132.3 7.7 %shard_map.89 = (bf16[1024,384]{1,0:T(8,128)(2,1)S(1)}, bf16[1024,384]{1,0:T(8,128)(2,1)S(1)}, f32[1,1]{1,0:T(1,128)}) custom-call(f32[32,8,128]{2,1,0:T(8,128)S(1)} %all-to-all-done.1.x_ref, f32[1024,384]{1,0:T(8,128)S(1)} %copy-done.7, bf16[1024,384]{1,0:T(8,128)(2,1)S(1)} %bitcast.30, f32[1,1024]{1,0:T(1,128)S(1)} %bitcast.32, ...), custom_call_target="tpu_custom_call" | custom-call | tf_op jit(solution)/shard_map/pallas_call | solution.py:181
  140.9 2.3 %collective-permute-done.22.other_ref = bf16[1024,384]{1,0:T(8,128)(2,1)S(1)} collective-permute-done((bf16[1024,384]{1,0:T(8,128)(2,1)S(1)}, bf16[1024,384]{1,0:T(8,128)(2,1)S(1)}, u32[]{:S(2)}, u32[]{:S(2)}) %collective-permute-start.22) | collective-permute-done | bytes 786464 | tf_op jit(solution)/shard_map/ppermute | solution.py:496
  143.2 3.4 %shard_map.91 = (f32[1024,384]{1,0:T(8,128)S(1)}, f32[512,384]{1,0:T(8,128)S(1)}, s16[528,384]{1,0:T(8,128)(2,1)}, s16[528,384]{1,0:T(8,128)(2,1)S(1)}, s16[528,...) custom-call(bf16[1024,384]{1,0:T(8,128)(2,1)S(1)} %get-tuple-element.28.high_ref.own_ref, ...), custom_call_target="tpu_custom_call" | custom-call | tf_op jit(solution)/shard_map/pallas_call | solution.py:284
  146.6 1.2 copy-done.4
  147.8 1.2 collective-permute-start.27
  149.8 2.4 %collective-permute-start.25 = (s16[528,384]{1,0:T(8,128)(2,1)}, s16[528,384]{1,0:T(8,128)(2,1)S(1)}, u32[]{:S(2)}, u32[]{:S(2)}) collective-permute-start(s16[528,384]{1,0:T(8,128)(2,1)} %get-tuple-element.35), channel_id=1, source_target_pairs={{0,6},{1,7},{2,0},{3,1},{4,2},{5,3},{6,4},{7,5},{8,14},{9,15},{10,... | collective-permute-start | bytes 1216520 | tf_op jit(solution)/shard_map/ppermute | solution.py:500
  152.2 7.8 %collective-permute-done.27.got_ref = s16[528,384]{1,0:T(8,128)(2,1)S(1)} collective-permute-done((s16[528,384]{1,0:T(8,128)(2,1)S(1)}, s16[528,384]{1,0:T(8,128)(2,1)S(1)}, u32[]{:S(2)}, u32[]{:S(2)}) %collective-permute-start.27) | collective-permute-done | bytes 405536 | tf_op jit(solution)/shard_map/ppermute | solution.py:498
  160.0 1.2 shard_map.93
  161.2 2.4 %collective-permute-start.28 = (s16[528,384]{1,0:T(8,128)(2,1)}, s16[528,384]{1,0:T(8,128)(2,1)S(1)}, u32[]{:S(2)}, u32[]{:S(2)}) collective-permute-start(s16[528,384]{1,0:T(8,128)(2,1)} %shard_map.93), channel_id=1, source_target_pairs={{0,6},{1,7},{2,0},{3,1},{4,2},{5,3},{6,4},{7,5},{8,14},{9,15},{10,... | collective-permute-start | bytes 1216520 | tf_op jit(solution)/shard_map/ppermute | solution.py:502
  163.5 1.2 shard_map.92
  164.8 21.3 %psum.7.loss_ref = f32[1,1]{1,0:T(1,128)} all-reduce(f32[1,1]{1,0:T(1,128)} %get-tuple-element.30), channel_id=1, replica_groups=mesh['trainer'=32,'vocab'=8] {'vocab'}, use_global_device_ids=true, to_apply=%region_0.1 | all-reduce | flops 1 | bytes 8 | tf_op jit(solution)/shard_map/psum | solution.py:504
  186.1 2.8 %shard_map.94 = s16[32,112,128]{2,1,0:T(8,128)(2,1)} custom-call(f32[1,1]{1,0:T(1,128)} %psum.7.loss_ref, f32[1024,384]{1,0:T(8,128)S(1)} %copy-done.5, s16[528,384]{1,0:T(8,128)(2,1)S(1)} %collective-permute-done.24.low_r, s16[528,384]{1,0:T(8,128)(2,1)S(1)} %collective-permute-done.25.low_l, s16[528,384]{1,0:T(8,128)(2,1)S(1)} %collective-permute-done.26.high_r, ...), custom_call_target="tpu_custom_call" | custom-call | tf_op jit(solution)/shard_map/pallas_call | solution.py:351
  188.9 5.7 %all-to-all-start.3 = ((s16[32,112,128]{2,1,0:T(8,128)(2,1)}), s16[32,112,128]{2,1,0:T(8,128)(2,1)S(1)}, u32[]{:S(2)}, u32[]{:S(2)}) async-start(s16[32,112,128]{2,1,0:T(8,128)(2,1)} %shard_map.94), calls=%async_computation.3 | async-start | bytes 1835008 | tf_op jit(solution)/shard_map/all_to_all | solution.py:506
  195.9 1.9 copy-done.22
  197.8 1.9 copy-done.24
  199.7 10.5 %shard_map.90 = f32[9216,128]{1,0:T(8,128)} custom-call(s32[1]{0:T(128)} %bitcast.c_ref, bf16[1024,1536]{1,0:T(8,128)(2,1)S(1)} %copy-done.22, bf16[1024,1536]{1,0:T(8,128)(2,1)S(1)} %copy-done.24, bf16[1024,384]{1,0:T(8,128)(2,1)S(1)} %copy-done.12, bf16[1024,384]{1,0:T(8,128)(2,1)S(1)} %copy-done.26), custom_call_target="tpu_custom_call" | custom-call | flops 4831838208 | bytes 12582912 | tf_op jit(solution)/shard_map/pallas_call | solution.py:417
  210.2 8.7 %all-to-all-done.3.x_ref = s16[32,112,128]{2,1,0:T(8,128)(2,1)S(1)} async-done(((s16[32,112,128]{2,1,0:T(8,128)(2,1)}), s16[32,112,128]{2,1,0:T(8,128)(2,1)S(1)}, u32[]{:S(2)}, u32[]{:S(2)}) %all-to-all-start.3) | async-done | bytes 917536 | tf_op jit(solution)/shard_map/all_to_all | solution.py:506
  218.9 1.2 shard_map.95
  (100 shorter events, 14.9 us)
Async XLA Ops:
  1.6 15.8 %collective-permute-start.4 = (bf16[32,1536]{1,0:T(8,128)(2,1)S(1)}, bf16[32,1536]{1,0:T(8,128)(2,1)S(1)}, u32[]{:S(2)}, u32[]{:S(2)}) collective-permute-start(bf16[32,1536]{1,0:T(8,128)(2,1)S(1)} %constant_dynamic-slice_fusion), channel_id=1, source_target_pairs={{0,128},{8,136},{16,144},{24,152},{32,160},{40,168},{48,176},{56,1... | collective-permute-start | bytes 294920 | tf_op jit(solution)/shard_map/ppermute | solution.py:452
  8.8 11.6 %collective-permute-start.5 = (bf16[32,1536]{1,0:T(8,128)(2,1)S(1)}, bf16[32,1536]{1,0:T(8,128)(2,1)S(1)}, u32[]{:S(2)}, u32[]{:S(2)}) collective-permute-start(bf16[32,1536]{1,0:T(8,128)(2,1)S(1)} %constant_dynamic-slice_fusion), channel_id=1, source_target_pairs={{0,160},{8,168},{16,176},{24,184},{32,192},{40,200},{48,208},{56,2... | collective-permute-start | bytes 294920 | tf_op jit(solution)/shard_map/ppermute | solution.py:452
  8.8 16.0 %collective-permute-start.6 = (bf16[32,1536]{1,0:T(8,128)(2,1)S(1)}, bf16[32,1536]{1,0:T(8,128)(2,1)S(1)}, u32[]{:S(2)}, u32[]{:S(2)}) collective-permute-start(bf16[32,1536]{1,0:T(8,128)(2,1)S(1)} %constant_dynamic-slice_fusion), channel_id=1, source_target_pairs={{0,192},{8,200},{16,208},{24,216},{32,224},{40,232},{48,240},{56,2... | collective-permute-start | bytes 294920 | tf_op jit(solution)/shard_map/ppermute | solution.py:452
  13.4 13.7 %collective-permute-start.7 = (bf16[32,1536]{1,0:T(8,128)(2,1)S(1)}, bf16[32,1536]{1,0:T(8,128)(2,1)S(1)}, u32[]{:S(2)}, u32[]{:S(2)}) collective-permute-start(bf16[32,1536]{1,0:T(8,128)(2,1)S(1)} %constant_dynamic-slice_fusion), channel_id=1, source_target_pairs={{0,224},{8,232},{16,240},{24,248},{32,0},{40,8},{48,16},{56,24},{6... | collective-permute-start | bytes 294920 | tf_op jit(solution)/shard_map/ppermute | solution.py:452
  14.5 13.3 %collective-permute-start.3 = (bf16[32,1536]{1,0:T(8,128)(2,1)S(1)}, bf16[32,1536]{1,0:T(8,128)(2,1)S(1)}, u32[]{:S(2)}, u32[]{:S(2)}) collective-permute-start(bf16[32,1536]{1,0:T(8,128)(2,1)S(1)} %constant_dynamic-slice_fusion), channel_id=1, source_target_pairs={{0,96},{8,104},{16,112},{24,120},{32,128},{40,136},{48,144},{56,15... | collective-permute-start | bytes 294920 | tf_op jit(solution)/shard_map/ppermute | solution.py:452
  17.3 10.4 %collective-permute-start.1 = (bf16[32,1536]{1,0:T(8,128)(2,1)S(1)}, bf16[32,1536]{1,0:T(8,128)(2,1)S(1)}, u32[]{:S(2)}, u32[]{:S(2)}) collective-permute-start(bf16[32,1536]{1,0:T(8,128)(2,1)S(1)} %constant_dynamic-slice_fusion), channel_id=1, source_target_pairs={{0,32},{8,40},{16,48},{24,56},{32,64},{40,72},{48,80},{56,88},{64,... | collective-permute-start | bytes 294920 | tf_op jit(solution)/shard_map/ppermute | solution.py:452
  20.4 10.2 %collective-permute-start.2 = (bf16[32,1536]{1,0:T(8,128)(2,1)S(1)}, bf16[32,1536]{1,0:T(8,128)(2,1)S(1)}, u32[]{:S(2)}, u32[]{:S(2)}) collective-permute-start(bf16[32,1536]{1,0:T(8,128)(2,1)S(1)} %constant_dynamic-slice_fusion), channel_id=1, source_target_pairs={{0,64},{8,72},{16,80},{24,88},{32,96},{40,104},{48,112},{56,120},{... | collective-permute-start | bytes 294920 | tf_op jit(solution)/shard_map/ppermute | solution.py:452
  24.8 34.8 %collective-permute-start = (bf16[4,384,384]{2,1,0:T(8,128)(2,1)S(1)}, bf16[4,384,384]{2,1,0:T(8,128)(2,1)S(1)}, u32[]{:S(2)}, u32[]{:S(2)}) collective-permute-start(bf16[4,384,384]{2,1,0:T(8,128)(2,1)S(1)} %get-tuple-element.44), channel_id=1, source_target_pairs={{0,1},{1,0},{2,3},{3,2},{4,5},{5,4},{6,7},{7,6},{8,9},{9,8},{10,11... | collective-permute-start | bytes 3538952 | tf_op jit(solution)/shard_map/ppermute | solution.py:483
  27.2 12.2 %collective-permute-start.11 = (bf16[4,32,1536]{2,1,0:T(8,128)(2,1)S(1)}, bf16[4,32,1536]{2,1,0:T(8,128)(2,1)}, u32[]{:S(2)}, u32[]{:S(2)}) collective-permute-start(bf16[4,32,1536]{2,1,0:T(8,128)(2,1)S(1)} %pad_maximum_fusion.1.refs_1_), channel_id=1, source_target_pairs={{0,24},{8,0},{16,8},{24,16},{32,56},{40,32},{48,40},{56,48},{64,88... | collective-permute-start | bytes 1179656 | tf_op jit(solution)/shard_map/ppermute | solution.py:456
  30.7 12.2 %collective-permute-start.8 = (bf16[4,32,1536]{2,1,0:T(8,128)(2,1)S(1)}, bf16[4,32,1536]{2,1,0:T(8,128)(2,1)}, u32[]{:S(2)}, u32[]{:S(2)}) collective-permute-start(bf16[4,32,1536]{2,1,0:T(8,128)(2,1)S(1)} %pad_maximum_fusion.refs_0_), channel_id=1, source_target_pairs={{0,8},{8,16},{16,24},{24,0},{32,40},{40,48},{48,56},{56,32},{64,72... | collective-permute-start | bytes 1179656 | tf_op jit(solution)/shard_map/ppermute | solution.py:455
  32.4 15.8 %collective-permute-start.9 = (bf16[4,32,1536]{2,1,0:T(8,128)(2,1)S(1)}, bf16[4,32,1536]{2,1,0:T(8,128)(2,1)S(1)}, u32[]{:S(2)}, u32[]{:S(2)}) collective-permute-start(bf16[4,32,1536]{2,1,0:T(8,128)(2,1)S(1)} %pad_maximum_fusion.1.refs_1_), channel_id=1, source_target_pairs={{0,8},{8,16},{16,24},{24,0},{32,40},{40,48},{48,56},{56,32},{64,72... | collective-permute-start | bytes 1179656 | tf_op jit(solution)/shard_map/ppermute | solution.py:457
  33.6 16.4 %collective-permute-start.13 = (bf16[4,32,1536]{2,1,0:T(8,128)(2,1)S(1)}, bf16[4,32,1536]{2,1,0:T(8,128)(2,1)}, u32[]{:S(2)}, u32[]{:S(2)}) collective-permute-start(bf16[4,32,1536]{2,1,0:T(8,128)(2,1)S(1)} %pad_maximum_fusion.refs_0_), channel_id=1, source_target_pairs={{0,24},{8,0},{16,8},{24,16},{32,56},{40,32},{48,40},{56,48},{64,88... | collective-permute-start | bytes 1179656 | tf_op jit(solution)/shard_map/ppermute | solution.py:458
  39.5 10.7 %collective-permute-start.15 = (bf16[4,32,1536]{2,1,0:T(8,128)(2,1)S(1)}, bf16[4,32,1536]{2,1,0:T(8,128)(2,1)S(1)}, u32[]{:S(2)}, u32[]{:S(2)}) collective-permute-start(bf16[4,32,1536]{2,1,0:T(8,128)(2,1)S(1)} %pad_maximum_fusion.1.refs_1_), channel_id=1, source_target_pairs={{0,1},{1,0},{2,3},{3,2},{4,5},{5,4},{6,7},{7,6},{8,9},{9,8},{10,11... | collective-permute-start | bytes 1179656 | tf_op jit(solution)/shard_map/ppermute | solution.py:478
  42.9 8.8 %collective-permute-start.14 = (bf16[4,32,1536]{2,1,0:T(8,128)(2,1)S(1)}, bf16[4,32,1536]{2,1,0:T(8,128)(2,1)S(1)}, u32[]{:S(2)}, u32[]{:S(2)}) collective-permute-start(bf16[4,32,1536]{2,1,0:T(8,128)(2,1)S(1)} %pad_maximum_fusion.refs_0_), channel_id=1, source_target_pairs={{0,1},{1,0},{2,3},{3,2},{4,5},{5,4},{6,7},{7,6},{8,9},{9,8},{10,11... | collective-permute-start | bytes 1179656 | tf_op jit(solution)/shard_map/ppermute | solution.py:478
  48.2 8.5 %collective-permute-start.12 = (bf16[4,32,1536]{2,1,0:T(8,128)(2,1)}, bf16[4,32,1536]{2,1,0:T(8,128)(2,1)}, u32[]{:S(2)}, u32[]{:S(2)}) collective-permute-start(bf16[4,32,1536]{2,1,0:T(8,128)(2,1)} %collective-permute-done.11.refs_7_), channel_id=1, source_target_pairs={{0,24},{8,0},{16,8},{24,16},{32,56},{40,32},{48,40},{56,48},{64,88... | collective-permute-start | bytes 1179656 | tf_op jit(solution)/shard_map/ppermute | solution.py:462
  50.0 8.3 %collective-permute-start.10 = (bf16[4,32,1536]{2,1,0:T(8,128)(2,1)}, bf16[4,32,1536]{2,1,0:T(8,128)(2,1)}, u32[]{:S(2)}, u32[]{:S(2)}) collective-permute-start(bf16[4,32,1536]{2,1,0:T(8,128)(2,1)} %collective-permute-done.8.refs_2_), channel_id=1, source_target_pairs={{0,8},{8,16},{16,24},{24,0},{32,40},{40,48},{48,56},{56,32},{64,72... | collective-permute-start | bytes 1179656 | tf_op jit(solution)/shard_map/ppermute | solution.py:461
  50.9 7.4 %collective-permute-start.17 = (bf16[4,32,1536]{2,1,0:T(8,128)(2,1)S(1)}, bf16[4,32,1536]{2,1,0:T(8,128)(2,1)S(1)}, u32[]{:S(2)}, u32[]{:S(2)}) collective-permute-start(bf16[4,32,1536]{2,1,0:T(8,128)(2,1)S(1)} %collective-permute-done.9.refs_3_), channel_id=1, source_target_pairs={{0,1},{1,0},{2,3},{3,2},{4,5},{5,4},{6,7},{7,6},{8,9},{9,8},{10,11... | collective-permute-start | bytes 1179656 | tf_op jit(solution)/shard_map/ppermute | solution.py:478
  52.5 11.5 %collective-permute-start.21 = (bf16[4,32,1536]{2,1,0:T(8,128)(2,1)}, bf16[4,32,1536]{2,1,0:T(8,128)(2,1)}, u32[]{:S(2)}, u32[]{:S(2)}) collective-permute-start(bf16[4,32,1536]{2,1,0:T(8,128)(2,1)} %collective-permute-done.11.refs_7_), channel_id=1, source_target_pairs={{0,1},{1,0},{2,3},{3,2},{4,5},{5,4},{6,7},{7,6},{8,9},{9,8},{10,11... | collective-permute-start | bytes 1179656 | tf_op jit(solution)/shard_map/ppermute | solution.py:478
  56.6 7.4 %collective-permute-start.16 = (bf16[4,32,1536]{2,1,0:T(8,128)(2,1)}, bf16[4,32,1536]{2,1,0:T(8,128)(2,1)}, u32[]{:S(2)}, u32[]{:S(2)}) collective-permute-start(bf16[4,32,1536]{2,1,0:T(8,128)(2,1)} %collective-permute-done.8.refs_2_), channel_id=1, source_target_pairs={{0,1},{1,0},{2,3},{3,2},{4,5},{5,4},{6,7},{7,6},{8,9},{9,8},{10,11... | collective-permute-start | bytes 1179656 | tf_op jit(solution)/shard_map/ppermute | solution.py:478
  58.3 5.7 %collective-permute-start.20 = (bf16[4,32,1536]{2,1,0:T(8,128)(2,1)}, bf16[4,32,1536]{2,1,0:T(8,128)(2,1)}, u32[]{:S(2)}, u32[]{:S(2)}) collective-permute-start(bf16[4,32,1536]{2,1,0:T(8,128)(2,1)} %collective-permute-done.13.refs_6_), channel_id=1, source_target_pairs={{0,1},{1,0},{2,3},{3,2},{4,5},{5,4},{6,7},{7,6},{8,9},{9,8},{10,11... | collective-permute-start | bytes 1179656 | tf_op jit(solution)/shard_map/ppermute | solution.py:478
  59.1 4.9 %collective-permute-start.19 = (bf16[4,32,1536]{2,1,0:T(8,128)(2,1)}, bf16[4,32,1536]{2,1,0:T(8,128)(2,1)}, u32[]{:S(2)}, u32[]{:S(2)}) collective-permute-start(bf16[4,32,1536]{2,1,0:T(8,128)(2,1)} %collective-permute-done.12.refs_5_), channel_id=1, source_target_pairs={{0,1},{1,0},{2,3},{3,2},{4,5},{5,4},{6,7},{7,6},{8,9},{9,8},{10,11... | collective-permute-start | bytes 1179656 | tf_op jit(solution)/shard_map/ppermute | solution.py:478
  60.7 3.4 %collective-permute-start.18 = (bf16[4,32,1536]{2,1,0:T(8,128)(2,1)}, bf16[4,32,1536]{2,1,0:T(8,128)(2,1)}, u32[]{:S(2)}, u32[]{:S(2)}) collective-permute-start(bf16[4,32,1536]{2,1,0:T(8,128)(2,1)} %collective-permute-done.10.refs_4_), channel_id=1, source_target_pairs={{0,1},{1,0},{2,3},{3,2},{4,5},{5,4},{6,7},{7,6},{8,9},{9,8},{10,11... | collective-permute-start | bytes 1179656 | tf_op jit(solution)/shard_map/ppermute | solution.py:478
  63.3 1.7 copy-start.1
  63.3 1.7 copy-start.14
  63.3 1.8 copy-start.16
  63.3 1.9 copy-start.18
  63.3 2.0 copy-start.20
  73.2 1.7 copy-start.21
  74.9 1.6 copy-start.23
  86.9 17.2 %all-to-all-start.1 = ((f32[32,8,128]{2,1,0:T(8,128)}), f32[32,8,128]{2,1,0:T(8,128)S(1)}, u32[]{:S(2)}, u32[]{:S(2)}) async-start(f32[32,8,128]{2,1,0:T(8,128)} %shard_map.87), calls=%async_computation.1 | async-start | bytes 262144 | tf_op jit(solution)/shard_map/all_to_all | solution.py:492
  96.4 13.2 %copy-start.29 = (s32[32]{0:T(128)S(1)}, s32[32]{0:T(128)}, u32[]{:S(2)}) copy-start(s32[32]{0:T(128)} %param.9) | copy-start | bytes 388
  96.4 13.3 %copy-start.27 = (s32[1024]{0:T(1024)S(1)}, s32[1024]{0:T(1024)}, u32[]{:S(2)}) copy-start(s32[1024]{0:T(1024)} %param.11) | copy-start | bytes 12292
  96.4 13.4 %copy-start.28 = (s32[1024]{0:T(1024)S(1)}, s32[1024]{0:T(1024)}, u32[]{:S(2)}) copy-start(s32[1024]{0:T(1024)} %param.10) | copy-start | bytes 12292
  104.1 26.8 %all-to-all-start.2 = ((bf16[32,32,384]{2,1,0:T(8,128)(2,1)}), bf16[32,32,384]{2,1,0:T(8,128)(2,1)S(1)}, u32[]{:S(2)}, u32[]{:S(2)}) async-start(bf16[32,32,384]{2,1,0:T(8,128)(2,1)} %copy-done.3), calls=%async_computation.2 | async-start | bytes 1572864 | tf_op jit(solution)/shard_map/all_to_all | solution.py:460
  140.9 5.7 %copy-start.11 = (bf16[1024,384]{1,0:T(8,128)(2,1)}, bf16[1024,384]{1,0:T(8,128)(2,1)S(1)}, u32[]{:S(2)}) copy-start(bf16[1024,384]{1,0:T(8,128)(2,1)S(1)} %get-tuple-element.28.high_ref.own_ref) | copy-start | bytes 2359300
  140.9 2.3 %collective-permute-start.22 = (bf16[1024,384]{1,0:T(8,128)(2,1)S(1)}, bf16[1024,384]{1,0:T(8,128)(2,1)S(1)}, u32[]{:S(2)}, u32[]{:S(2)}) collective-permute-start(bf16[1024,384]{1,0:T(8,128)(2,1)S(1)} %get-tuple-element.28.high_ref.own_ref), channel_id=1, source_target_pairs={{0,1},{1,0},{2,3},{3,2},{4,5},{5,4},{6,7},{7,6},{8,9},{9,8},{10,11... | collective-permute-start | bytes 2359304 | tf_op jit(solution)/shard_map/ppermute | solution.py:496
  147.8 12.2 %collective-permute-start.27 = (s16[528,384]{1,0:T(8,128)(2,1)S(1)}, s16[528,384]{1,0:T(8,128)(2,1)S(1)}, u32[]{:S(2)}, u32[]{:S(2)}) collective-permute-start(s16[528,384]{1,0:T(8,128)(2,1)S(1)} %get-tuple-element.38), channel_id=1, source_target_pairs={{0,6},{1,7},{2,0},{3,1},{4,2},{5,3},{6,4},{7,5},{8,14},{9,15},{10,... | collective-permute-start | bytes 1216520 | tf_op jit(solution)/shard_map/ppermute | solution.py:498
  148.9 14.6 %collective-permute-start.23 = (s16[528,384]{1,0:T(8,128)(2,1)S(1)}, s16[528,384]{1,0:T(8,128)(2,1)S(1)}, u32[]{:S(2)}, u32[]{:S(2)}) collective-permute-start(s16[528,384]{1,0:T(8,128)(2,1)S(1)} %get-tuple-element.34), channel_id=1, source_target_pairs={{0,2},{1,3},{2,4},{3,5},{4,6},{5,7},{6,0},{7,1},{8,10},{9,11},{10,... | collective-permute-start | bytes 1216520 | tf_op jit(solution)/shard_map/ppermute | solution.py:497
  149.8 36.2 %collective-permute-start.25 = (s16[528,384]{1,0:T(8,128)(2,1)}, s16[528,384]{1,0:T(8,128)(2,1)S(1)}, u32[]{:S(2)}, u32[]{:S(2)}) collective-permute-start(s16[528,384]{1,0:T(8,128)(2,1)} %get-tuple-element.35), channel_id=1, source_target_pairs={{0,6},{1,7},{2,0},{3,1},{4,2},{5,3},{6,4},{7,5},{8,14},{9,15},{10,... | collective-permute-start | bytes 1216520 | tf_op jit(solution)/shard_map/ppermute | solution.py:500
  152.2 33.9 %collective-permute-start.26 = (s16[528,384]{1,0:T(8,128)(2,1)}, s16[528,384]{1,0:T(8,128)(2,1)S(1)}, u32[]{:S(2)}, u32[]{:S(2)}) collective-permute-start(s16[528,384]{1,0:T(8,128)(2,1)} %get-tuple-element.36), channel_id=1, source_target_pairs={{0,2},{1,3},{2,4},{3,5},{4,6},{5,7},{6,0},{7,1},{8,10},{9,11},{10,... | collective-permute-start | bytes 1216520 | tf_op jit(solution)/shard_map/ppermute | solution.py:499
  160.0 26.1 %copy-start.5 = (f32[1024,384]{1,0:T(8,128)S(1)}, f32[1024,384]{1,0:T(8,128)}, u32[]{:S(2)}) copy-start(f32[1024,384]{1,0:T(8,128)} %copy-done.4) | copy-start | bytes 4718596
  161.2 24.9 %collective-permute-start.28 = (s16[528,384]{1,0:T(8,128)(2,1)}, s16[528,384]{1,0:T(8,128)(2,1)S(1)}, u32[]{:S(2)}, u32[]{:S(2)}) collective-permute-start(s16[528,384]{1,0:T(8,128)(2,1)} %shard_map.93), channel_id=1, source_target_pairs={{0,6},{1,7},{2,0},{3,1},{4,2},{5,3},{6,4},{7,5},{8,14},{9,15},{10,... | collective-permute-start | bytes 1216520 | tf_op jit(solution)/shard_map/ppermute | solution.py:502
  164.7 21.3 %collective-permute-start.24 = (s16[528,384]{1,0:T(8,128)(2,1)}, s16[528,384]{1,0:T(8,128)(2,1)S(1)}, u32[]{:S(2)}, u32[]{:S(2)}) collective-permute-start(s16[528,384]{1,0:T(8,128)(2,1)} %shard_map.92), channel_id=1, source_target_pairs={{0,2},{1,3},{2,4},{3,5},{4,6},{5,7},{6,0},{7,1},{8,10},{9,11},{10,... | collective-permute-start | bytes 1216520 | tf_op jit(solution)/shard_map/ppermute | solution.py:501
  188.9 7.0 %copy-start.12 = (bf16[1024,384]{1,0:T(8,128)(2,1)S(1)}, bf16[1024,384]{1,0:T(8,128)(2,1)}, u32[]{:S(2)}) copy-start(bf16[1024,384]{1,0:T(8,128)(2,1)} %copy-done.11) | copy-start | bytes 2359300
  188.9 7.0 %copy-start.26 = (bf16[1024,384]{1,0:T(8,128)(2,1)S(1)}, bf16[1024,384]{1,0:T(8,128)(2,1)}, u32[]{:S(2)}) copy-start(bf16[1024,384]{1,0:T(8,128)(2,1)} %copy-done.25) | copy-start | bytes 2359300
  188.9 30.0 %all-to-all-start.3 = ((s16[32,112,128]{2,1,0:T(8,128)(2,1)}), s16[32,112,128]{2,1,0:T(8,128)(2,1)S(1)}, u32[]{:S(2)}, u32[]{:S(2)}) async-start(s16[32,112,128]{2,1,0:T(8,128)(2,1)} %shard_map.94), calls=%async_computation.3 | async-start | bytes 1835008 | tf_op jit(solution)/shard_map/all_to_all | solution.py:506
  195.9 1.9 copy-start.22
  197.8 1.9 copy-start.24
  (14 other events, 14.2 us)

commit v4 on v3

v4 whole, which is shorter than its diff:
```python
import functools
import math

import jax
import jax.numpy as jnp
from jax import lax
from jax.experimental import pallas as pl
from jax.experimental.pallas import tpu as pltpu
from jax.sharding import PartitionSpec as P

D = 3072
VOCAB = 98304
ROWS = 1024
TRAINERS = 32
SLOTS = 32
SHARDS = 8
LOCAL = VOCAB // (TRAINERS * SHARDS)
HALF = D // 2
BLOCK = 256
BF16 = jnp.bfloat16
F32 = jnp.float32
PARAMS = pltpu.CompilerParams(vmem_limit_bytes=24 * 1024 * 1024)
FULL = pltpu.CompilerParams(vmem_limit_bytes=60 * 1024 * 1024)
VMEM = pl.BlockSpec(memory_space=pltpu.VMEM)
SMEM = pl.BlockSpec(memory_space=pltpu.SMEM)
ANY = pl.BlockSpec(memory_space=pl.ANY)


def dot(a, b, dims=((1,), (0,))):
    return lax.dot_general(a, b, (dims, ((), ())), preferred_element_type=F32)


def split_kernel(x_ref, o_ref):
    for j in range(TRAINERS):
        o_ref[j] = x_ref[:, j * LOCAL : (j + 1) * LOCAL]


def split_targets(x):
    return pl.pallas_call(
        split_kernel,
        out_shape=jax.ShapeDtypeStruct((TRAINERS, SLOTS, LOCAL), BF16),
        in_specs=[VMEM],
        out_specs=VMEM,
        compiler_params=FULL,
    )(x)


Z = 8
Y = 4


def order_kernel(z_ref, *refs):
    pieces, (low_ref, high_ref, sems) = refs[:Z], refs[Z:]
    for start in (True, False):
        for k, piece in enumerate(pieces):
            at = lax.rem(z_ref[0] + Z - k, Z)
            for side, out in enumerate((low_ref, high_ref)):

                @pl.when(at // (Z // 2) == side)
                def _():
                    copy = pltpu.make_async_copy(piece, out.at[lax.rem(at, Z // 2)], sems.at[k])
                    copy.start() if start else copy.wait()


def in_order(z, pieces):
    half = jax.ShapeDtypeStruct((Z // 2, SLOTS, HALF), BF16)
    return pl.pallas_call(
        order_kernel,
        out_shape=(half, half),
        in_specs=[SMEM] + [ANY] * Z,
        out_specs=(ANY, ANY),
        scratch_shapes=[pltpu.SemaphoreType.DMA((Z,))],
        compiler_params=FULL,
    )(z, *pieces)


def logit_kernel(at_ref, *refs):
    pieces, refs = refs[:16], refs[16:]
    far_ref, own_ref, other_ref, logits_ref, o_ref, tabs, w_ref, logit_buf, in_sems, out_sems = refs
    c, y = at_ref[0], at_ref[1]
    copies = [[], []]
    for side in range(2):
        rows = pl.ds(pl.multiple_of((c + side) % 2 * HALF, HALF), HALF)
        copies[side].append(
            pltpu.make_async_copy(far_ref.at[rows], w_ref.at[side], in_sems.at[16 + side])
        )
        for dy in range(Y):
            y_at = lax.rem(y + Y - dy, Y)
            for high in range(2):
                n = side * 8 + dy * 2 + high
                place = tabs.at[side, pl.ds(high * (Z // 2), Z // 2), y_at]
                copies[side].append(pltpu.make_async_copy(pieces[n], place, in_sems.at[n]))
        for copy in copies[side]:
            copy.start()
    block = 2 * BLOCK
    step = block // (Y * SLOTS)
    stores = []
    for side, out in enumerate((own_ref, other_ref)):
        for copy in copies[side]:
            copy.wait()
        stores.append(pltpu.make_async_copy(tabs.at[side], out, out_sems.at[side]))
        stores[-1].start()
        for i in range(ROWS // block):
            rows = pl.ds(i * block, block)
            part = dot(tabs[side, pl.ds(i * step, step)].reshape(block, HALF), w_ref[side])
            if side == 0:
                logit_buf[rows, :] = part
                continue
            logits = logit_buf[rows, :] + part
            logit_buf[rows, :] = logits
            stores.append(
                pltpu.make_async_copy(logit_buf.at[rows], logits_ref.at[rows], out_sems.at[2 + i])
            )
            stores[-1].start()
            top = jnp.max(logits, axis=1, keepdims=True)
            lse = top + jnp.log(jnp.sum(jnp.exp(logits - top), axis=1, keepdims=True))
            flat = jnp.broadcast_to(lse, (block, 128)).T
            for j in range(block // 128):
                row = flat[0:1, j * 128 : (j + 1) * 128]
                o_ref[pl.ds(i * (block // 128) + j, 1), :] = row
    for store in stores:
        store.wait()


def logits_and_stats(at, pieces, weight):
    table = jax.ShapeDtypeStruct((Z, Y, SLOTS, HALF), BF16)
    own, other, logits, stats = pl.pallas_call(
        logit_kernel,
        out_shape=(
            table,
            table,
            jax.ShapeDtypeStruct((ROWS, LOCAL), F32),
            jax.ShapeDtypeStruct((8, 128), F32),
        ),
        in_specs=[SMEM] + [ANY] * 17,
        out_specs=(ANY, ANY, ANY, VMEM),
        scratch_shapes=[
            pltpu.VMEM((2, Z, Y, SLOTS, HALF), BF16),
            pltpu.VMEM((2, HALF, LOCAL), BF16),
            pltpu.VMEM((ROWS, LOCAL), F32),
            pltpu.SemaphoreType.DMA((18,)),
            pltpu.SemaphoreType.DMA((4,)),
        ],
        compiler_params=FULL,
    )(at, *pieces, weight)
    return own.reshape(ROWS, HALF), other.reshape(ROWS, HALF), logits, stats


def merge(x):
    top = jnp.max(x, axis=0)
    return top + jnp.log(jnp.sum(jnp.exp(x - top[None]), axis=0))


def merge_kernel(copies, *refs):
    lse = merge(jnp.stack([ref[...] for ref in refs[:-1]]))
    if copies == 1:
        refs[-1][...] = lse
    for k in range(copies if copies > 1 else 0):
        refs[-1][k] = lse


def merge_stats(parts, copies=1):
    shape = (8, 128) if copies == 1 else (copies, 8, 128)
    return pl.pallas_call(
        functools.partial(merge_kernel, copies),
        out_shape=jax.ShapeDtypeStruct(shape, F32),
        in_specs=[VMEM] * len(parts),
        out_specs=VMEM,
        compiler_params=PARAMS if copies == 1 else FULL,
    )(*parts)


def column(row):
    return jnp.broadcast_to(row, (128, row.shape[1])).T


def grad_kernel(
    x_ref, far_ref, targets_ref, gid_ref, live_ref, high_ref, both_ref, loss_ref, *scratch
):
    parts_ref, gp_ref, lse_ref, logits_ref, p_ref, sums_ref, sems = scratch
    fetch = pltpu.make_async_copy(far_ref, logits_ref, sems.at[0])
    fetch.start()
    fetch_targets = pltpu.make_async_copy(targets_ref, p_ref, sems.at[1])
    fetch_targets.start()
    lse = merge(x_ref[...])
    for j in range(8):
        lse_ref[pl.ds(j * 128, 128), :] = column(lse[j : j + 1])
    fetch.wait()
    for j in range(LOCAL // 128):
        cols = pl.ds(j * 128, 128)
        p = jnp.exp(logits_ref[:, cols] - lse_ref[...])
        first = p.astype(BF16)
        p = p - first.astype(F32)
        second = p.astype(BF16)
        third = (p - second.astype(F32)).astype(BF16)
        parts_ref[:, pl.ds(j * 128, 128)] = first
        parts_ref[:, pl.ds(LOCAL + j * 128, 128)] = second
        parts_ref[:, pl.ds(2 * LOCAL + j * 128, 128)] = third
    scale = VOCAB / math.sqrt(ROWS)
    fetch_targets.wait()

    @pl.loop(0, ROWS // BLOCK)
    def _(i):
        rows = pl.ds(pl.multiple_of(i * BLOCK, BLOCK), BLOCK)
        gid = column(gid_ref[:, rows])
        factor = column(live_ref[:, rows]) * scale
        lane = lax.broadcasted_iota(jnp.int32, (BLOCK, 128), 1).astype(F32)
        hot = jnp.concatenate(
            [
                jnp.where(gid == lane + float(128 * k), 1.0, 0.0).astype(BF16)
                for k in range(ROWS // 128)
            ],
            axis=1,
        )
        sel = dot(hot, parts_ref[...])
        p = sel[:, 0:LOCAL] + sel[:, LOCAL : 2 * LOCAL] + sel[:, 2 * LOCAL :]
        targets = p_ref[rows, :]
        diff = p - targets.astype(F32)
        for j in range(LOCAL // 128):
            cols = slice(j * 128, (j + 1) * 128)
            gp_ref[rows, cols] = (factor * diff[:, cols]).astype(BF16)
        gp_ref[rows, LOCAL:] = targets

    def stores(rows, i):
        high = sums_ref.at[rows, pl.ds(0, LOCAL)]
        yield pltpu.make_async_copy(high, high_ref.at[rows], sems.at[2 + i])
        yield pltpu.make_async_copy(sums_ref.at[rows], both_ref.at[rows], sems.at[6 + i])

    def total(i, loss):
        rows = pl.ds(pl.multiple_of(i * BLOCK, BLOCK), BLOCK)
        row = lax.broadcasted_iota(jnp.int32, (BLOCK, ROWS), 0) + i * BLOCK
        hot = jnp.where(gid_ref[...] == row.astype(F32), live_ref[...], 0.0).astype(BF16)
        sums = dot(hot, gp_ref[...])
        high = sums[:, 0:LOCAL].astype(BF16)
        sums_ref[rows, 0:LOCAL] = high
        sums_ref[rows, LOCAL:] = (sums[:, 0:LOCAL] - high.astype(F32)).astype(BF16)
        for store in stores(rows, i):
            store.start()
        for j in range(LOCAL // 128):
            cols = pl.ds(j * 128, 128)
            gap = lse_ref[rows, :] - logits_ref[rows, cols]
            loss += jnp.sum(sums[:, LOCAL + j * 128 : LOCAL + (j + 1) * 128] * gap)
        return loss

    loss_ref[0, 0] = lax.fori_loop(0, ROWS // BLOCK, total, jnp.float32(0))
    for i in range(ROWS // BLOCK):
        for store in stores(pl.ds(i * BLOCK, BLOCK), i):
            store.wait()


def gradients(x, logits, probs, gid, live):
    return pl.pallas_call(
        grad_kernel,
        out_shape=(
            jax.ShapeDtypeStruct((ROWS, LOCAL), BF16),
            jax.ShapeDtypeStruct((ROWS, 2 * LOCAL), BF16),
            jax.ShapeDtypeStruct((1, 1), F32),
        ),
        in_specs=[VMEM, ANY, ANY, VMEM, VMEM],
        out_specs=(ANY, ANY, SMEM),
        scratch_shapes=[
            pltpu.VMEM((ROWS, 3 * LOCAL), BF16),
            pltpu.VMEM((ROWS, 2 * LOCAL), BF16),
            pltpu.VMEM((ROWS, 128), F32),
            pltpu.VMEM((ROWS, LOCAL), F32),
            pltpu.VMEM((ROWS, LOCAL), BF16),
            pltpu.VMEM((ROWS, 2 * LOCAL), BF16),
            pltpu.SemaphoreType.DMA((10,)),
        ],
        compiler_params=FULL,
    )(x, logits, probs, gid, live)


TOP = 32700.0
ROWS2 = ROWS // 2
TAIL = 16
I16 = jnp.int16


def exponent(x):
    return jnp.ceil(jnp.log(jnp.maximum(x, 1e-30) / TOP) * (256.0 / math.log(2.0)))


def power(e):
    return jnp.exp2(e * (1.0 / 256.0))


def to16(x):
    return x.astype(jnp.int32).astype(I16)


def from16(x):
    return x.astype(jnp.int32).astype(F32)


def encode(val):
    e = exponent(jnp.max(jnp.abs(val), axis=1, keepdims=True))
    return to16(jnp.round(val * power(-e))), jnp.broadcast_to(e, (128, 128)).T[0:1]


def wide(row):
    return jnp.concatenate([row] + [jnp.zeros_like(row)] * (LOCAL // 128 - 1), axis=1)


def write_message(out_ref, block_of, loss):
    tail = []
    for j in range(ROWS2 // 128):
        code, e = encode(block_of(j))
        out_ref[pl.ds(j * 128, 128), :] = code
        tail.append(e)
    tail += [loss, jnp.zeros((TAIL - len(tail) - 1, 128), F32)]
    out_ref[pl.ds(ROWS2, TAIL), :] = to16(wide(jnp.concatenate(tail, axis=0)))


def encode_loss(loss):
    e = exponent(jnp.abs(loss))
    whole = loss * power(-e)
    first = jnp.round(whole)
    rest = jnp.round((whole - first) * TOP)
    lane = lax.broadcasted_iota(jnp.int32, (1, 128), 1)
    return jnp.where(lane == 0, e, jnp.where(lane == 1, first, jnp.where(lane == 2, rest, 0.0)))


def decode_loss(code):
    return (code[:, 1:2] + code[:, 2:3] * (1.0 / TOP)) * power(code[:, 0:1])


def message_loss(ref):
    return from16(ref[pl.ds(ROWS2, TAIL), 0:128])[ROWS2 // 128 : ROWS2 // 128 + 1]


def read_message(ref, j):
    tail = from16(ref[pl.ds(ROWS2, TAIL), 0:128])
    scale = power(column(tail[j : j + 1]))
    rows = pl.ds(j * 128, 128)
    return [from16(ref[rows, k * 128 : (k + 1) * 128]) * scale for k in range(LOCAL // 128)]


MESSAGE = jax.ShapeDtypeStruct((ROWS2 + TAIL, LOCAL), I16)


def weight_kernel(at_ref, all_ref, other_ref, o_ref, own_ref, sems):
    c, x = at_ref[0], at_ref[1]
    fetches = [
        pltpu.make_async_copy(all_ref.at[lax.rem(x + k, 4), c], own_ref.at[k], sems.at[k])
        for k in range(4)
    ]
    for fetch in fetches:
        fetch.start()
    for k in range(4):
        o_ref[LOCAL : 2 * LOCAL, k * LOCAL : (k + 1) * LOCAL] = other_ref[lax.rem(x + k, 4)].T
    for k in range(4):
        fetches[k].wait()
        o_ref[0:LOCAL, k * LOCAL : (k + 1) * LOCAL] = own_ref[k].T


def pair_weights(at, blocks, other):
    return pl.pallas_call(
        weight_kernel,
        out_shape=jax.ShapeDtypeStruct((2 * LOCAL, 4 * LOCAL), BF16),
        in_specs=[SMEM, ANY, VMEM],
        out_specs=VMEM,
        scratch_shapes=[
            pltpu.VMEM((4, LOCAL, LOCAL), BF16),
            pltpu.SemaphoreType.DMA((4,)),
        ],
        compiler_params=FULL,
    )(at, blocks, other)


def term_kernel(
    loss_ref, more_ref, own_ref, other_ref, w_ref, c0, l1, h1, l2, h2, l3, h3, sum_ref, *scratch
):
    g_ref, val_ref, sems = scratch
    fetches = [
        pltpu.make_async_copy(ref, g_ref.at[:, pl.ds(k * LOCAL, LOCAL)], sems.at[k])
        for k, ref in enumerate((own_ref, other_ref))
    ]
    for fetch in fetches:
        fetch.start()
    loss = encode_loss(jnp.full((1, 128), loss_ref[0, 0] + more_ref[0, 0], F32))
    sum_ref[...] = loss
    for fetch in fetches:
        fetch.wait()
    outs = {2: (l2, h2), 1: (l1, h1), 3: (l3, h3)}
    for i in range(2):
        rows = pl.ds(i * ROWS2, ROWS2)
        val_ref[...] = dot(g_ref[rows, :], w_ref[...])
        c0[rows, :] = val_ref[:, 0:LOCAL]
        for k in (1, 2, 3):
            out, cols = outs[k][i], slice(k * LOCAL, (k + 1) * LOCAL)
            if out.dtype == F32:
                out[...] = val_ref[:, cols]
            else:
                write_message(out, lambda j: val_ref[pl.ds(j * 128, 128), cols], loss)


def terms(loss, more, own, other, weights):
    part = jax.ShapeDtypeStruct((ROWS2, LOCAL), F32)
    return pl.pallas_call(
        term_kernel,
        out_shape=(
            jax.ShapeDtypeStruct((ROWS, LOCAL), F32),
            part,
            MESSAGE,
            MESSAGE,
            MESSAGE,
            MESSAGE,
            part,
            jax.ShapeDtypeStruct((1, 128), F32),
        ),
        in_specs=[SMEM, SMEM, ANY, ANY, VMEM],
        out_specs=(VMEM,) * 8,
        scratch_shapes=[
            pltpu.VMEM((ROWS, 2 * LOCAL), BF16),
            pltpu.VMEM((ROWS2, 4 * LOCAL), F32),
            pltpu.SemaphoreType.DMA((2,)),
        ],
        compiler_params=PARAMS,
    )(loss, more, own, other, weights)


def relay_kernel(own_ref, got_ref, out_ref):
    def block(j):
        got = jnp.concatenate(read_message(got_ref, j), axis=1)
        return own_ref[pl.ds(j * 128, 128), :] + got

    write_message(out_ref, block, message_loss(got_ref))


def relay(own, got):
    return pl.pallas_call(
        relay_kernel,
        out_shape=MESSAGE,
        in_specs=[VMEM] * 2,
        out_specs=VMEM,
        compiler_params=PARAMS,
    )(own, got)


PACKED = 3 * SLOTS + TAIL


def pack_kernel(loss_ref, own_ref, low_r, low_l, high_r, high_l, o_ref):
    codes = [loss_ref[...]] + [message_loss(ref) for ref in (low_r, low_l, high_r)]
    loss = decode_loss(jnp.concatenate(codes, axis=0))
    loss = (loss[0:1] + loss[1:2]) + (loss[2:3] + loss[3:4])
    loss = encode_loss(jnp.broadcast_to(loss, (1, 128)))
    pad = jnp.zeros((TAIL - 2, 128), F32)
    for i, (right, left) in enumerate(((low_r, low_l), (high_r, high_l))):
        for j in range(ROWS2 // 128):
            a, b = read_message(right, j), read_message(left, j)
            val = jnp.concatenate([p + q for p, q in zip(a, b)], axis=1)
            at = i * (ROWS2 // 128) + j
            code, e = encode(own_ref[pl.ds(at * 128, 128), :] + val)
            tail = to16(jnp.concatenate([e, loss, pad], axis=0))
            for n in range(128 // SLOTS):
                for k in range(3):
                    o_ref[at * 4 + n, k * SLOTS : (k + 1) * SLOTS, :] = code[
                        n * SLOTS : (n + 1) * SLOTS, k * 128 : (k + 1) * 128
                    ]
                o_ref[at * 4 + n, 3 * SLOTS :, :] = tail


def pack(loss, own, low_r, low_l, high_r, high_l):
    return pl.pallas_call(
        pack_kernel,
        out_shape=jax.ShapeDtypeStruct((TRAINERS, PACKED, 128), I16),
        in_specs=[VMEM] * 6,
        out_specs=VMEM,
        compiler_params=PARAMS,
    )(loss, own, low_r, low_l, high_r, high_l)


def finish_kernel(at_ref, x_ref, grad_ref, loss_ref, e_ref):
    tail = from16(x_ref[:, 3 * SLOTS :, :])
    e = tail[:, 0, :]
    e_ref[...] = jnp.concatenate([e, jnp.zeros((128 - TRAINERS, 128), F32)], axis=0).T
    scale = power(e_ref[pl.ds(pl.multiple_of(at_ref[0] * SLOTS, SLOTS), SLOTS), :])
    total = [jnp.zeros((SLOTS, 128), F32)] * 3
    for s in range(TRAINERS):
        for k in range(3):
            total[k] += from16(x_ref[s, k * SLOTS : (k + 1) * SLOTS, :]) * scale[:, s : s + 1]
    for k in range(3):
        grad_ref[:, k * 128 : (k + 1) * 128] = total[k]
    loss_ref[0, 0] = jnp.sum(decode_loss(tail[:, 1, :]))


def finish(at, x):
    return pl.pallas_call(
        finish_kernel,
        out_shape=(
            jax.ShapeDtypeStruct((SLOTS, LOCAL), F32),
            jax.ShapeDtypeStruct((1, 1), F32),
        ),
        in_specs=[SMEM, VMEM],
        out_specs=(VMEM, SMEM),
        scratch_shapes=[pltpu.VMEM((128, 128), F32)],
        compiler_params=PARAMS,
    )(at, x)


HEAD_BLOCK = 256
HEAD_STEPS = HALF // HEAD_BLOCK


def head_kernel(c_ref, own_ref, other_ref, sums_ref, o_ref):
    i = pl.program_id(0)

    def work(t_ref):
        both = dot(t_ref[...], sums_ref[...], ((0,), (0,)))
        both = both[:, 0:LOCAL] + both[:, LOCAL:]
        for j in range(LOCAL // 128):
            o_ref[pl.ds(j, HEAD_BLOCK, stride=LOCAL // 128), :] = both[:, j * 128 : (j + 1) * 128]

    @pl.when(i < HEAD_STEPS)
    def _():
        work(own_ref)

    @pl.when(i >= HEAD_STEPS)
    def _():
        work(other_ref)


def head_gradient(c, own, other, sums):
    def place(i, c):
        mine = i < HEAD_STEPS
        side = jnp.where(mine, c[0], 1 - c[0])
        return (side * HEAD_STEPS + jnp.where(mine, i, i - HEAD_STEPS), 0)

    return pl.pallas_call(
        head_kernel,
        grid_spec=pltpu.PrefetchScalarGridSpec(
            num_scalar_prefetch=1,
            grid=(2 * HEAD_STEPS,),
            in_specs=[
                pl.BlockSpec((ROWS, HEAD_BLOCK), lambda i, c: (0, jnp.minimum(i, HEAD_STEPS - 1))),
                pl.BlockSpec((ROWS, HEAD_BLOCK), lambda i, c: (0, jnp.maximum(i - HEAD_STEPS, 0))),
                pl.BlockSpec((ROWS, 2 * LOCAL), lambda i, c: (0, 0)),
            ],
            out_specs=pl.BlockSpec((HEAD_BLOCK * LOCAL // 128, 128), place),
        ),
        out_shape=jax.ShapeDtypeStruct((D * LOCAL // 128, 128), F32),
        compiler_params=PARAMS,
        cost_estimate=pl.CostEstimate(
            flops=4 * ROWS * D * LOCAL, bytes_accessed=12 * 1024 * 1024, transcendentals=0
        ),
    )(c, own, other, sums)


PAIR = [(i, i ^ 1) for i in range(SHARDS)]


def along_x(k):
    return [(i, (i + 2 * k) % SHARDS) for i in range(SHARDS)]


RIGHT, LEFT = along_x(1), along_x(-1)


def along_z(k):
    return [(i, (i // Y + k) % Z * Y + i % Y) for i in range(TRAINERS)]


def along_y(k):
    return [(i, i // Y * Y + (i + k) % Y) for i in range(TRAINERS)]


def on_device(hidden_table, head_weight, targets, counts, dest, token):
    me = lax.axis_index("vocab")
    trainer = lax.axis_index("trainer")
    c = lax.rem(me, 2)
    x = me // 2
    y = lax.rem(trainer, Y)
    c1 = c.reshape(1).astype(jnp.int32)
    at_cx = jnp.stack([c, x]).astype(jnp.int32)
    at_cy = jnp.stack([c, y]).astype(jnp.int32)
    z1 = (trainer // Y).reshape(1).astype(jnp.int32)
    weight = head_weight[:, 0, :]

    half = lax.dynamic_slice(hidden_table, (0, c * HALF), (SLOTS, HALF))
    near = [half] + [lax.ppermute(half, "trainer", along_z(k)) for k in range(1, Z)]

    split = split_targets(targets[:, 0, :])

    gid = dest * SLOTS + token
    index = jnp.arange(ROWS, dtype=jnp.int32)
    live = (index % SLOTS < jnp.repeat(counts, SLOTS)).astype(F32).reshape(1, ROWS)
    gid = gid.astype(F32).reshape(1, ROWS)

    z1, split, gid, live = lax.optimization_barrier((z1, split, gid, live))
    low0, high0 = in_order(z1, near)
    low1 = lax.ppermute(low0, "trainer", along_y(1))
    high3 = lax.ppermute(high0, "trainer", along_y(-1))
    high1 = lax.ppermute(high0, "trainer", along_y(1))
    low3 = lax.ppermute(low0, "trainer", along_y(-1))
    low2 = lax.ppermute(low1, "trainer", along_y(1))
    high2 = lax.ppermute(high3, "trainer", along_y(-1))
    pieces = (low0, high0, low1, high1, low2, high2, low3, high3)
    pieces += tuple(lax.ppermute(p, "vocab", PAIR) for p in pieces)
    blocks = weight.reshape(4, 2, LOCAL, LOCAL)
    c, _ = lax.optimization_barrier((c, low1))
    give = lax.dynamic_index_in_dim(blocks, 1 - c, axis=1, keepdims=False)
    weights = pair_weights(at_cx, blocks, lax.ppermute(give, "vocab", PAIR))
    at_cy, weights = lax.optimization_barrier((at_cy, weights))
    split, _ = lax.optimization_barrier((split, (low1, high1, low3, high3)))
    probs = lax.all_to_all(split, "trainer", split_axis=0, concat_axis=0, tiled=True)

    own, other, logits, stats = logits_and_stats(at_cy, pieces, weight)
    stats = merge_stats([stats, lax.ppermute(stats, "vocab", PAIR)])
    stats = [stats] + [lax.ppermute(stats, "vocab", along_x(k)) for k in (1, 2, 3)]
    stats = merge_stats(stats, TRAINERS)
    stats, probs = lax.optimization_barrier((stats, probs.reshape(ROWS, LOCAL)))
    stats = lax.all_to_all(stats, "trainer", split_axis=0, concat_axis=0, tiled=True)

    high, sums, loss = gradients(stats, logits, probs, gid, live)

    more = lax.ppermute(loss, "vocab", PAIR)
    far = lax.ppermute(high, "vocab", PAIR)
    t0, l1, h1, l2, h2, l3, h3, loss = terms(loss, more, high, far, weights)
    low_r = lax.ppermute(l2, "vocab", RIGHT)
    high_l = lax.ppermute(h2, "vocab", LEFT)
    high_r = lax.ppermute(h1, "vocab", RIGHT)
    low_l = lax.ppermute(l3, "vocab", LEFT)
    low_r = lax.ppermute(relay(l1, low_r), "vocab", RIGHT)
    high_l = lax.ppermute(relay(h3, high_l), "vocab", LEFT)
    head = head_gradient(c1, own, other, sums)
    packed = pack(loss, t0, low_r, low_l, high_r, high_l)
    packed = lax.all_to_all(packed, "trainer", split_axis=0, concat_axis=0, tiled=True)
    table_grad, loss = finish(lax.rem(trainer, 4).reshape(1).astype(jnp.int32), packed)
    mean_loss = loss[0, 0] / jnp.sum(counts).astype(F32)
    return head.reshape(D, 1, LOCAL), table_grad, mean_loss


def solution(mesh):
    return jax.shard_map(
        on_device,
        mesh=mesh,
        in_specs=(
            P("trainer", None),
            P(None, "vocab", "trainer"),
            P("trainer", "vocab", None),
            P(),
            P(),
            P(),
        ),
        out_specs=(P(None, "vocab", "trainer"), P("trainer", "vocab"), P()),
        check_vma=False,
    )
```

time: 223 us -> 237 us (1.063)
  Pallas kernels: 36.2 us -> 70 us
  local copies, waits for them, and re-layouts: 25.6 us -> 10.5 us
  blocking collectives: 30.9 us -> 17 us
  starting transfers between devices: 49.2 us -> 56.4 us
  other arithmetic: 0.83 us -> 3.34 us
    all_to_all x2 -> x1, waiting for transfers between devices: 27.9 us -> 0.01 us  [on_device(): lax.all_to_all(split, 'trainer', split_axis=0, concat_axis=0, tiled=True)]
    pallas_call x1 -> x3, Pallas kernels: 0.69 us -> 26.4 us  [the longest x1 25 us: in_order(): pl.pallas_call(order_kernel, out_shape=(half, half), in_specs=[SMEM] + [A...]
    psum x1 -> x0, blocking collectives: 21.3 us -> none  [on_device(): loss = lax.psum(loss, 'vocab')]
    unnamed x60 -> x58, local copies, waits for them, and re-layouts: 22.6 us -> 8.52 us
    ppermute x15 -> x20, waiting for transfers between devices: 31.4 us -> 43.3 us  [the longest x1 15.4 us: on_device(): low2 = lax.ppermute(low1, 'trainer', along_y(1))]
    ppermute x15 -> x20, starting transfers between devices: 21.9 us -> 31.6 us  [the longest x7 18.5 us: on_device(): lax.ppermute(half, 'trainer', along_z(k))]
    all_to_all x1, blocking collectives: 9.64 us -> 17 us  [on_device(): lax.all_to_all(stats, 'trainer', split_axis=0, concat_axis=0, tiled=True)]
    all_to_all x2 -> x1, starting transfers between devices: 13.8 us -> 7.86 us  [on_device(): lax.all_to_all(split, 'trainer', split_axis=0, concat_axis=0, tiled=True)]
  transfers between devices with their start and end apart: 32 -> 36, of which waited for: 14 -> 20; matrix products, arithmetic and copies ran while one was open for 2% -> 2% of each run, Pallas kernels for 6% -> 11%
where the time goes in v4:
time: 237 us; the launch traced here: 236 us
  waiting for transfers between devices  75.7 us (32%)
  Pallas kernels  70 us (30%)
  starting transfers between devices  56.4 us (24%)
  blocking collectives  17 us (7%)
  local copies, waits for them, and re-layouts  10.5 us (4%)
  between operations  3.46 us (1%)
  other arithmetic  3.34 us (1%)
    pallas_call x1, Pallas kernels, in_order(): pl.pallas_call(order_kernel, out_shape=(half, half), in_specs=[SMEM] + [A...  25 us
    ppermute x7, starting transfers between devices, on_device(): lax.ppermute(half, 'trainer', along_z(k))  18.5 us
    all_to_all x1, blocking collectives, on_device(): lax.all_to_all(stats, 'trainer', split_axis=0, concat_axis=0, tiled=True)  17 us
    ppermute x1, waiting for transfers between devices, on_device(): low2 = lax.ppermute(low1, 'trainer', along_y(1))  15.4 us
    pallas_call x1, Pallas kernels, gradients(): pl.pallas_call(grad_kernel, out_shape=(jax.ShapeDtypeStruct((ROWS, LOCAL)...  10.7 us
    all_to_all x1, waiting for transfers between devices, on_device(): lax.all_to_all(packed, 'trainer', split_axis=0, concat_axis=0, tiled=True)  10.5 us
    pallas_call x1, Pallas kernels, head_gradient(): pl.pallas_call(head_kernel, grid_spec=pltpu.PrefetchScalarGridSpec(num_sc...  9.22 us
    unnamed x58, local copies, waits for them, and re-layouts  8.52 us
  transfers between devices with their start and end apart: 36, of which 20 were waited for; matrix products, arithmetic and copies ran while one was open for 2% of the time, Pallas kernels for 11%

profile of v4, /device:TPU:8, one launch (start us, length us, event | category | flops | bytes accessed | tf_op | source)
XLA Modules:
  0.0 236.3 jit_solution(16651294354411008393)
XLA Ops:
  1.6 2.0 collective-permute-start
  3.6 3.3 %collective-permute-start.1 = (bf16[32,1536]{1,0:T(8,128)(2,1)S(1)}, bf16[32,1536]{1,0:T(8,128)(2,1)S(1)}, u32[]{:S(2)}, u32[]{:S(2)}) collective-permute-start(bf16[32,1536]{1,0:T(8,128)(2,1)S(1)} %constant_dynamic-slice_fusion.refs_0_), channel_id=1, source_target_pairs={{0,64},{8,72},{16,80},{24,88},{32,96},{40,104},{48,112},{56,120},{... | collective-permute-start | bytes 294920 | tf_op jit(solution)/shard_map/ppermute | solution.py:582
  6.8 4.0 %collective-permute-start.2 = (bf16[32,1536]{1,0:T(8,128)(2,1)S(1)}, bf16[32,1536]{1,0:T(8,128)(2,1)S(1)}, u32[]{:S(2)}, u32[]{:S(2)}) collective-permute-start(bf16[32,1536]{1,0:T(8,128)(2,1)S(1)} %constant_dynamic-slice_fusion.refs_0_), channel_id=1, source_target_pairs={{0,96},{8,104},{16,112},{24,120},{32,128},{40,136},{48,144},{56,15... | collective-permute-start | bytes 294920 | tf_op jit(solution)/shard_map/ppermute | solution.py:582
  11.4 4.9 %collective-permute-start.4 = (bf16[32,1536]{1,0:T(8,128)(2,1)S(1)}, bf16[32,1536]{1,0:T(8,128)(2,1)S(1)}, u32[]{:S(2)}, u32[]{:S(2)}) collective-permute-start(bf16[32,1536]{1,0:T(8,128)(2,1)S(1)} %constant_dynamic-slice_fusion.refs_0_), channel_id=1, source_target_pairs={{0,160},{8,168},{16,176},{24,184},{32,192},{40,200},{48,208},{56,2... | collective-permute-start | bytes 294920 | tf_op jit(solution)/shard_map/ppermute | solution.py:582
  16.4 1.3 add_convert_fusion
  18.5 2.7 %collective-permute-start.5 = (bf16[32,1536]{1,0:T(8,128)(2,1)S(1)}, bf16[32,1536]{1,0:T(8,128)(2,1)S(1)}, u32[]{:S(2)}, u32[]{:S(2)}) collective-permute-start(bf16[32,1536]{1,0:T(8,128)(2,1)S(1)} %constant_dynamic-slice_fusion.refs_0_), channel_id=1, source_target_pairs={{0,192},{8,200},{16,208},{24,216},{32,224},{40,232},{48,240},{56,2... | collective-permute-start | bytes 294920 | tf_op jit(solution)/shard_map/ppermute | solution.py:582
  22.8 2.1 shard_map.85
  25.0 3.3 %collective-permute-done.4.refs_5_ = bf16[32,1536]{1,0:T(8,128)(2,1)S(1)} collective-permute-done((bf16[32,1536]{1,0:T(8,128)(2,1)S(1)}, bf16[32,1536]{1,0:T(8,128)(2,1)S(1)}, u32[]{:S(2)}, u32[]{:S(2)}) %collective-permute-start.4) | collective-permute-done | bytes 98336 | tf_op jit(solution)/shard_map/ppermute | solution.py:582
  28.3 1.7 collective-permute-done.5.refs_6_
  31.4 25.0 %shard_map.86 = (bf16[4,32,1536]{2,1,0:T(8,128)(2,1)}, bf16[4,32,1536]{2,1,0:T(8,128)(2,1)}) custom-call(s32[1]{0:T(128)} %bitcast.4.z_ref, bf16[32,1536]{1,0:T(8,128)(2,1)} %copy-done.17, bf16[32,1536]{1,0:T(8,128)(2,1)} %copy-done.18, bf16[32,1536]{1,0:T(8,128)(2,1)} %copy-done.19, bf16[32,1536]{1,0:T(8,128)(2,1)} %copy-done.20, ...), custom_call_target="tpu_custom_call" | custom-call | tf_op jit(solution)/shard_map/pallas_call | solution.py:67
  56.4 1.7 collective-permute-start.7
  58.5 1.6 collective-permute-start.9
  60.5 8.3 %collective-permute-done.7.refs_2_ = bf16[4,32,1536]{2,1,0:T(8,128)(2,1)} collective-permute-done((bf16[4,32,1536]{2,1,0:T(8,128)(2,1)}, bf16[4,32,1536]{2,1,0:T(8,128)(2,1)}, u32[]{:S(2)}, u32[]{:S(2)}) %collective-permute-start.7) | collective-permute-done | bytes 393248 | tf_op jit(solution)/shard_map/ppermute | solution.py:593
  68.8 1.1 dynamic-slice_bitcast_fusion
  70.4 5.6 %collective-permute-done.9.refs_3_ = bf16[4,32,1536]{2,1,0:T(8,128)(2,1)} collective-permute-done((bf16[4,32,1536]{2,1,0:T(8,128)(2,1)}, bf16[4,32,1536]{2,1,0:T(8,128)(2,1)}, u32[]{:S(2)}, u32[]{:S(2)}) %collective-permute-start.9) | collective-permute-done | bytes 393248 | tf_op jit(solution)/shard_map/ppermute | solution.py:595
  76.0 1.3 collective-permute-done.13.refs_6_
  77.3 7.9 %all-to-all-start = ((bf16[32,32,384]{2,1,0:T(8,128)(2,1)}), bf16[32,32,384]{2,1,0:T(8,128)(2,1)S(1)}, u32[]{:S(2)}, u32[]{:S(2)}) async-start(bf16[32,32,384]{2,1,0:T(8,128)(2,1)} %shard_map.85), calls=%async_computation | async-start | bytes 1572864 | tf_op jit(solution)/shard_map/all_to_all | solution.py:607
  85.8 1.5 collective-permute-start.10
  88.3 15.4 %collective-permute-done.10.refs_4_ = bf16[4,32,1536]{2,1,0:T(8,128)(2,1)} collective-permute-done((bf16[4,32,1536]{2,1,0:T(8,128)(2,1)}, bf16[4,32,1536]{2,1,0:T(8,128)(2,1)}, u32[]{:S(2)}, u32[]{:S(2)}) %collective-permute-start.10) | collective-permute-done | bytes 393248 | tf_op jit(solution)/shard_map/ppermute | solution.py:597
  103.8 1.3 collective-permute-done.12.refs_5_
  106.6 4.3 %shard_map.87.w_ref = bf16[768,1536]{1,0:T(8,128)(2,1)} custom-call(s32[2]{0:T(128)} %get-tuple-element.65.at_ref, bf16[4,2,384,384]{3,2,1,0:T(8,128)(2,1)} %bitcast.17, bf16[4,384,384]{2,1,0:T(8,128)(2,1)} %copy-done.10), custom_call_target="tpu_custom_call" | custom-call | tf_op jit(solution)/shard_map/pallas_call | solution.py:358
  111.7 8.4 %shard_map.88 = (bf16[8,4,32,1536]{3,2,1,0:T(8,128)(2,1)}, bf16[8,4,32,1536]{3,2,1,0:T(8,128)(2,1)}, f32[1024,384]{1,0:T(8,128)}, f32[8,128]{1,0:T(8,128)}) custom-call(s32[2]{0:T(128)} %get-tuple-element.35.at_ref, bf16[4,32,1536]{2,1,0:T(8,128)(2,1)} %get-tuple-element.33.refs_0_, bf16[4,32,1536]{2,1,0:T(8,128)(2,1)} %get-tuple-element.36.refs_1_, ...), custom_call_target="tpu_custom_call" | custom-call | tf_op jit(solution)/shard_map/pallas_call | solution.py:127
  120.4 1.1 collective-permute-done.22.refs_1_
  122.3 1.6 collective-permute-start.23
  123.8 2.7 %collective-permute-start.24 = (f32[8,128]{1,0:T(8,128)S(1)}, f32[8,128]{1,0:T(8,128)S(1)}, u32[]{:S(2)}, u32[]{:S(2)}) collective-permute-start(f32[8,128]{1,0:T(8,128)S(1)} %shard_map.89.refs_0_), channel_id=1, source_target_pairs={{0,4},{1,5},{2,6},{3,7},{4,0},{5,1},{6,2},{7,3},{8,12},{9,13},{10,... | collective-permute-start | bytes 12296 | tf_op jit(solution)/shard_map/ppermute | solution.py:611
  126.6 1.4 collective-permute-start.25
  129.0 1.2 collective-permute-done.25.refs_3_
  130.8 1.4 shard_map.90
  132.2 17.0 %all_to_all.15.x_ref = f32[32,8,128]{2,1,0:T(8,128)} all-to-all(f32[32,8,128]{2,1,0:T(8,128)} %shard_map.90), channel_id=1, replica_groups=mesh['trainer'=32,'vocab'=8] {'trainer'}, dimensions={0} | all-to-all | bytes 262144 | tf_op jit(solution)/shard_map/all_to_all | solution.py:614
  149.2 10.7 %shard_map.91 = (bf16[1024,384]{1,0:T(8,128)(2,1)}, bf16[1024,768]{1,0:T(8,128)(2,1)}, f32[1,1]{1,0:T(1,128)}) custom-call(f32[32,8,128]{2,1,0:T(8,128)} %all_to_all.15.x_ref, f32[1024,384]{1,0:T(8,128)} %get-tuple-element.43.far_ref, bf16[1024,384]{1,0:T(8,128)(2,1)} %bitcast.20, f32[1,1024]{1,0:T(1,128)} %bitcast.22, f32[1,1024]{1,0:T(1,128)} %compare_convert_fusion.live_ref), custom_call_target="tpu_custom_call" | custom-call | tf_op jit(solution)/shard_map/pallas_call | solution.py:252
  160.7 1.7 collective-permute-done.26.more_ref
  162.7 1.1 copy-done.2
  163.9 4.4 %shard_map.93 = (f32[1024,384]{1,0:T(8,128)S(1)}, f32[512,384]{1,0:T(8,128)S(1)}, s16[528,384]{1,0:T(8,128)(2,1)S(1)}, s16[528,384]{1,0:T(8,128)(2,1)S(1)}, s16[...) custom-call(f32[1,1]{1,0:T(1,128)} %get-tuple-element.48.loss_ref, ...), custom_call_target="tpu_custom_call" | custom-call | tf_op jit(solution)/shard_map/pallas_call | solution.py:400
  168.2 2.7 %collective-permute-start.32 = (s16[528,384]{1,0:T(8,128)(2,1)S(1)}, s16[528,384]{1,0:T(8,128)(2,1)S(1)}, u32[]{:S(2)}, u32[]{:S(2)}) collective-permute-start(s16[528,384]{1,0:T(8,128)(2,1)S(1)} %get-tuple-element.58), channel_id=1, source_target_pairs={{0,6},{1,7},{2,0},{3,1},{4,2},{5,3},{6,4},{7,5},{8,14},{9,15},{10,... | collective-permute-start | bytes 1216520 | tf_op jit(solution)/shard_map/ppermute | solution.py:622
  171.0 3.2 %collective-permute-start.30 = (s16[528,384]{1,0:T(8,128)(2,1)S(1)}, s16[528,384]{1,0:T(8,128)(2,1)S(1)}, u32[]{:S(2)}, u32[]{:S(2)}) collective-permute-start(s16[528,384]{1,0:T(8,128)(2,1)S(1)} %get-tuple-element.55), channel_id=1, source_target_pairs={{0,6},{1,7},{2,0},{3,1},{4,2},{5,3},{6,4},{7,5},{8,14},{9,15},{10,... | collective-permute-start | bytes 1216520 | tf_op jit(solution)/shard_map/ppermute | solution.py:624
  174.2 6.5 %collective-permute-done.32.got_ref = s16[528,384]{1,0:T(8,128)(2,1)S(1)} collective-permute-done((s16[528,384]{1,0:T(8,128)(2,1)S(1)}, s16[528,384]{1,0:T(8,128)(2,1)S(1)}, u32[]{:S(2)}, u32[]{:S(2)}) %collective-permute-start.32) | collective-permute-done | bytes 405536 | tf_op jit(solution)/shard_map/ppermute | solution.py:622
  181.1 3.7 %collective-permute-start.33 = (s16[528,384]{1,0:T(8,128)(2,1)S(1)}, s16[528,384]{1,0:T(8,128)(2,1)S(1)}, u32[]{:S(2)}, u32[]{:S(2)}) collective-permute-start(s16[528,384]{1,0:T(8,128)(2,1)S(1)} %shard_map.95), channel_id=1, source_target_pairs={{0,6},{1,7},{2,0},{3,1},{4,2},{5,3},{6,4},{7,5},{8,14},{9,15},{10,... | collective-permute-start | bytes 1216520 | tf_op jit(solution)/shard_map/ppermute | solution.py:626
  185.3 4.1 %collective-permute-done.30.low_l = s16[528,384]{1,0:T(8,128)(2,1)S(1)} collective-permute-done((s16[528,384]{1,0:T(8,128)(2,1)S(1)}, s16[528,384]{1,0:T(8,128)(2,1)S(1)}, u32[]{:S(2)}, u32[]{:S(2)}) %collective-permute-start.30) | collective-permute-done | bytes 405536 | tf_op jit(solution)/shard_map/ppermute | solution.py:624
  189.4 3.7 %collective-permute-done.31.high_r = s16[528,384]{1,0:T(8,128)(2,1)S(1)} collective-permute-done((s16[528,384]{1,0:T(8,128)(2,1)S(1)}, s16[528,384]{1,0:T(8,128)(2,1)S(1)}, u32[]{:S(2)}, u32[]{:S(2)}) %collective-permute-start.31) | collective-permute-done | bytes 405536 | tf_op jit(solution)/shard_map/ppermute | solution.py:623
  193.1 4.2 %collective-permute-done.33.high_l = s16[528,384]{1,0:T(8,128)(2,1)S(1)} collective-permute-done((s16[528,384]{1,0:T(8,128)(2,1)S(1)}, s16[528,384]{1,0:T(8,128)(2,1)S(1)}, u32[]{:S(2)}, u32[]{:S(2)}) %collective-permute-start.33) | collective-permute-done | bytes 405536 | tf_op jit(solution)/shard_map/ppermute | solution.py:626
  197.3 3.4 %collective-permute-done.29.low_r = s16[528,384]{1,0:T(8,128)(2,1)S(1)} collective-permute-done((s16[528,384]{1,0:T(8,128)(2,1)S(1)}, s16[528,384]{1,0:T(8,128)(2,1)S(1)}, u32[]{:S(2)}, u32[]{:S(2)}) %collective-permute-start.29) | collective-permute-done | bytes 405536 | tf_op jit(solution)/shard_map/ppermute | solution.py:625
  200.7 2.3 shard_map.96
  203.0 5.5 %all-to-all-start.2 = ((s16[32,112,128]{2,1,0:T(8,128)(2,1)}), s16[32,112,128]{2,1,0:T(8,128)(2,1)S(1)}, u32[]{:S(2)}, u32[]{:S(2)}) async-start(s16[32,112,128]{2,1,0:T(8,128)(2,1)} %shard_map.96), calls=%async_computation.2 | async-start | bytes 1835008 | tf_op jit(solution)/shard_map/all_to_all | solution.py:629
  209.8 1.9 copy-done.5
  211.7 1.9 copy-done.6
  213.6 9.2 %shard_map.92 = f32[9216,128]{1,0:T(8,128)} custom-call(s32[1]{0:T(128)} %bitcast.c_ref, bf16[1024,1536]{1,0:T(8,128)(2,1)S(1)} %bitcast.15, bf16[1024,1536]{1,0:T(8,128)(2,1)S(1)} %bitcast.16, bf16[1024,768]{1,0:T(8,128)(2,1)S(1)} %copy-done.7), custom_call_target="tpu_custom_call" | custom-call | flops 4831838208 | bytes 12582912 | tf_op jit(solution)/shard_map/pallas_call | solution.py:531
  222.8 10.5 %all-to-all-done.2.x_ref = s16[32,112,128]{2,1,0:T(8,128)(2,1)S(1)} async-done(((s16[32,112,128]{2,1,0:T(8,128)(2,1)}), s16[32,112,128]{2,1,0:T(8,128)(2,1)S(1)}, u32[]{:S(2)}, u32[]{:S(2)}) %all-to-all-start.2) | async-done | bytes 917536 | tf_op jit(solution)/shard_map/all_to_all | solution.py:629
  233.3 1.2 shard_map.97
  (104 shorter events, 15.7 us)
Async XLA Ops:
  0.6 68.2 %copy-start.8 = (bf16[3072,1,384]{2,0,1:T(8,128)(2,1)S(1)}, bf16[3072,1,384]{2,0,1:T(8,128)(2,1)}, u32[]{:S(2)}) copy-start(bf16[3072,1,384]{2,0,1:T(8,128)(2,1)} %param.7) | copy-start | bytes 7077892
  1.6 29.1 %copy-start.17 = (bf16[32,1536]{1,0:T(8,128)(2,1)}, bf16[32,1536]{1,0:T(8,128)(2,1)S(1)}, u32[]{:S(2)}) copy-start(bf16[32,1536]{1,0:T(8,128)(2,1)S(1)} %constant_dynamic-slice_fusion.refs_0_) | copy-start | bytes 294916
  1.6 16.9 %collective-permute-start = (bf16[32,1536]{1,0:T(8,128)(2,1)S(1)}, bf16[32,1536]{1,0:T(8,128)(2,1)S(1)}, u32[]{:S(2)}, u32[]{:S(2)}) collective-permute-start(bf16[32,1536]{1,0:T(8,128)(2,1)S(1)} %constant_dynamic-slice_fusion.refs_0_), channel_id=1, source_target_pairs={{0,32},{8,40},{16,48},{24,56},{32,64},{40,72},{48,80},{56,88},{64,... | collective-permute-start | bytes 294920 | tf_op jit(solution)/shard_map/ppermute | solution.py:582
  3.6 17.7 %collective-permute-start.1 = (bf16[32,1536]{1,0:T(8,128)(2,1)S(1)}, bf16[32,1536]{1,0:T(8,128)(2,1)S(1)}, u32[]{:S(2)}, u32[]{:S(2)}) collective-permute-start(bf16[32,1536]{1,0:T(8,128)(2,1)S(1)} %constant_dynamic-slice_fusion.refs_0_), channel_id=1, source_target_pairs={{0,64},{8,72},{16,80},{24,88},{32,96},{40,104},{48,112},{56,120},{... | collective-permute-start | bytes 294920 | tf_op jit(solution)/shard_map/ppermute | solution.py:582
  6.8 18.1 %collective-permute-start.2 = (bf16[32,1536]{1,0:T(8,128)(2,1)S(1)}, bf16[32,1536]{1,0:T(8,128)(2,1)S(1)}, u32[]{:S(2)}, u32[]{:S(2)}) collective-permute-start(bf16[32,1536]{1,0:T(8,128)(2,1)S(1)} %constant_dynamic-slice_fusion.refs_0_), channel_id=1, source_target_pairs={{0,96},{8,104},{16,112},{24,120},{32,128},{40,136},{48,144},{56,15... | collective-permute-start | bytes 294920 | tf_op jit(solution)/shard_map/ppermute | solution.py:582
  10.9 14.1 %collective-permute-start.3 = (bf16[32,1536]{1,0:T(8,128)(2,1)S(1)}, bf16[32,1536]{1,0:T(8,128)(2,1)S(1)}, u32[]{:S(2)}, u32[]{:S(2)}) collective-permute-start(bf16[32,1536]{1,0:T(8,128)(2,1)S(1)} %constant_dynamic-slice_fusion.refs_0_), channel_id=1, source_target_pairs={{0,128},{8,136},{16,144},{24,152},{32,160},{40,168},{48,176},{56,1... | collective-permute-start | bytes 294920 | tf_op jit(solution)/shard_map/ppermute | solution.py:582
  11.4 16.9 %collective-permute-start.4 = (bf16[32,1536]{1,0:T(8,128)(2,1)S(1)}, bf16[32,1536]{1,0:T(8,128)(2,1)S(1)}, u32[]{:S(2)}, u32[]{:S(2)}) collective-permute-start(bf16[32,1536]{1,0:T(8,128)(2,1)S(1)} %constant_dynamic-slice_fusion.refs_0_), channel_id=1, source_target_pairs={{0,160},{8,168},{16,176},{24,184},{32,192},{40,200},{48,208},{56,2... | collective-permute-start | bytes 294920 | tf_op jit(solution)/shard_map/ppermute | solution.py:582
  18.5 12.2 %copy-start.18 = (bf16[32,1536]{1,0:T(8,128)(2,1)}, bf16[32,1536]{1,0:T(8,128)(2,1)S(1)}, u32[]{:S(2)}) copy-start(bf16[32,1536]{1,0:T(8,128)(2,1)S(1)} %collective-permute-done.refs_1_) | copy-start | bytes 294916
  18.5 11.5 %collective-permute-start.5 = (bf16[32,1536]{1,0:T(8,128)(2,1)S(1)}, bf16[32,1536]{1,0:T(8,128)(2,1)S(1)}, u32[]{:S(2)}, u32[]{:S(2)}) collective-permute-start(bf16[32,1536]{1,0:T(8,128)(2,1)S(1)} %constant_dynamic-slice_fusion.refs_0_), channel_id=1, source_target_pairs={{0,192},{8,200},{16,208},{24,216},{32,224},{40,232},{48,240},{56,2... | collective-permute-start | bytes 294920 | tf_op jit(solution)/shard_map/ppermute | solution.py:582
  21.2 9.5 %copy-start.19 = (bf16[32,1536]{1,0:T(8,128)(2,1)}, bf16[32,1536]{1,0:T(8,128)(2,1)S(1)}, u32[]{:S(2)}) copy-start(bf16[32,1536]{1,0:T(8,128)(2,1)S(1)} %collective-permute-done.1.refs_2_) | copy-start | bytes 294916
  21.2 9.4 %collective-permute-start.6 = (bf16[32,1536]{1,0:T(8,128)(2,1)S(1)}, bf16[32,1536]{1,0:T(8,128)(2,1)S(1)}, u32[]{:S(2)}, u32[]{:S(2)}) collective-permute-start(bf16[32,1536]{1,0:T(8,128)(2,1)S(1)} %constant_dynamic-slice_fusion.refs_0_), channel_id=1, source_target_pairs={{0,224},{8,232},{16,240},{24,248},{32,0},{40,8},{48,16},{56,24},{6... | collective-permute-start | bytes 294920 | tf_op jit(solution)/shard_map/ppermute | solution.py:582
  56.4 28.8 %copy-start.11 = (bf16[4,32,1536]{2,1,0:T(8,128)(2,1)S(1)}, bf16[4,32,1536]{2,1,0:T(8,128)(2,1)}, u32[]{:S(2)}) copy-start(bf16[4,32,1536]{2,1,0:T(8,128)(2,1)} %get-tuple-element.33.refs_0_) | copy-start | bytes 1179652
  56.4 28.9 %copy-start.12 = (bf16[4,32,1536]{2,1,0:T(8,128)(2,1)S(1)}, bf16[4,32,1536]{2,1,0:T(8,128)(2,1)}, u32[]{:S(2)}) copy-start(bf16[4,32,1536]{2,1,0:T(8,128)(2,1)} %get-tuple-element.36.refs_1_) | copy-start | bytes 1179652
  56.4 12.4 %collective-permute-start.7 = (bf16[4,32,1536]{2,1,0:T(8,128)(2,1)}, bf16[4,32,1536]{2,1,0:T(8,128)(2,1)}, u32[]{:S(2)}, u32[]{:S(2)}) collective-permute-start(bf16[4,32,1536]{2,1,0:T(8,128)(2,1)} %get-tuple-element.33.refs_0_), channel_id=1, source_target_pairs={{0,8},{8,16},{16,24},{24,0},{32,40},{40,48},{48,56},{56,32},{64,72... | collective-permute-start | bytes 1179656 | tf_op jit(solution)/shard_map/ppermute | solution.py:593
  58.1 12.4 %collective-permute-start.11 = (bf16[4,32,1536]{2,1,0:T(8,128)(2,1)}, bf16[4,32,1536]{2,1,0:T(8,128)(2,1)}, u32[]{:S(2)}, u32[]{:S(2)}) collective-permute-start(bf16[4,32,1536]{2,1,0:T(8,128)(2,1)} %get-tuple-element.36.refs_1_), channel_id=1, source_target_pairs={{0,24},{8,0},{16,8},{24,16},{32,56},{40,32},{48,40},{56,48},{64,88... | collective-permute-start | bytes 1179656 | tf_op jit(solution)/shard_map/ppermute | solution.py:594
  58.5 17.5 %collective-permute-start.9 = (bf16[4,32,1536]{2,1,0:T(8,128)(2,1)}, bf16[4,32,1536]{2,1,0:T(8,128)(2,1)}, u32[]{:S(2)}, u32[]{:S(2)}) collective-permute-start(bf16[4,32,1536]{2,1,0:T(8,128)(2,1)} %get-tuple-element.36.refs_1_), channel_id=1, source_target_pairs={{0,8},{8,16},{16,24},{24,0},{32,40},{40,48},{48,56},{56,32},{64,72... | collective-permute-start | bytes 1179656 | tf_op jit(solution)/shard_map/ppermute | solution.py:595
  60.1 17.2 %collective-permute-start.13 = (bf16[4,32,1536]{2,1,0:T(8,128)(2,1)}, bf16[4,32,1536]{2,1,0:T(8,128)(2,1)}, u32[]{:S(2)}, u32[]{:S(2)}) collective-permute-start(bf16[4,32,1536]{2,1,0:T(8,128)(2,1)} %get-tuple-element.33.refs_0_), channel_id=1, source_target_pairs={{0,24},{8,0},{16,8},{24,16},{32,56},{40,32},{48,40},{56,48},{64,88... | collective-permute-start | bytes 1179656 | tf_op jit(solution)/shard_map/ppermute | solution.py:596
  69.9 35.6 %collective-permute-start.8 = (bf16[4,384,384]{2,1,0:T(8,128)(2,1)}, bf16[4,384,384]{2,1,0:T(8,128)(2,1)S(1)}, u32[]{:S(2)}, u32[]{:S(2)}) collective-permute-start(bf16[4,384,384]{2,1,0:T(8,128)(2,1)} %dynamic-slice_bitcast_fusion), channel_id=1, source_target_pairs={{0,1},{1,0},{2,3},{3,2},{4,5},{5,4},{6,7},{7,6},{8,9},{9,8},{10,11... | collective-permute-start | bytes 3538952 | tf_op jit(solution)/shard_map/ppermute | solution.py:604
  77.3 54.9 %all-to-all-start = ((bf16[32,32,384]{2,1,0:T(8,128)(2,1)}), bf16[32,32,384]{2,1,0:T(8,128)(2,1)S(1)}, u32[]{:S(2)}, u32[]{:S(2)}) async-start(bf16[32,32,384]{2,1,0:T(8,128)(2,1)} %shard_map.85), calls=%async_computation | async-start | bytes 1572864 | tf_op jit(solution)/shard_map/all_to_all | solution.py:607
  85.2 2.6 %collective-permute-start.14 = (bf16[4,32,1536]{2,1,0:T(8,128)(2,1)S(1)}, bf16[4,32,1536]{2,1,0:T(8,128)(2,1)S(1)}, u32[]{:S(2)}, u32[]{:S(2)}) collective-permute-start(bf16[4,32,1536]{2,1,0:T(8,128)(2,1)S(1)} %copy-done.11), channel_id=1, source_target_pairs={{0,1},{1,0},{2,3},{3,2},{4,5},{5,4},{6,7},{7,6},{8,9},{9,8},{10,11... | collective-permute-start | bytes 1179656 | tf_op jit(solution)/shard_map/ppermute | solution.py:600
  85.3 2.5 %collective-permute-start.15 = (bf16[4,32,1536]{2,1,0:T(8,128)(2,1)S(1)}, bf16[4,32,1536]{2,1,0:T(8,128)(2,1)S(1)}, u32[]{:S(2)}, u32[]{:S(2)}) collective-permute-start(bf16[4,32,1536]{2,1,0:T(8,128)(2,1)S(1)} %copy-done.12), channel_id=1, source_target_pairs={{0,1},{1,0},{2,3},{3,2},{4,5},{5,4},{6,7},{7,6},{8,9},{9,8},{10,11... | collective-permute-start | bytes 1179656 | tf_op jit(solution)/shard_map/ppermute | solution.py:600
  85.8 18.0 %collective-permute-start.10 = (bf16[4,32,1536]{2,1,0:T(8,128)(2,1)}, bf16[4,32,1536]{2,1,0:T(8,128)(2,1)}, u32[]{:S(2)}, u32[]{:S(2)}) collective-permute-start(bf16[4,32,1536]{2,1,0:T(8,128)(2,1)} %collective-permute-done.7.refs_2_), channel_id=1, source_target_pairs={{0,8},{8,16},{16,24},{24,0},{32,40},{40,48},{48,56},{56,32},{64,72... | collective-permute-start | bytes 1179656 | tf_op jit(solution)/shard_map/ppermute | solution.py:597
  87.3 17.8 %collective-permute-start.12 = (bf16[4,32,1536]{2,1,0:T(8,128)(2,1)}, bf16[4,32,1536]{2,1,0:T(8,128)(2,1)}, u32[]{:S(2)}, u32[]{:S(2)}) collective-permute-start(bf16[4,32,1536]{2,1,0:T(8,128)(2,1)} %collective-permute-done.11.refs_7_), channel_id=1, source_target_pairs={{0,24},{8,0},{16,8},{24,16},{32,56},{40,32},{48,40},{56,48},{64,88... | collective-permute-start | bytes 1179656 | tf_op jit(solution)/shard_map/ppermute | solution.py:598
  87.8 23.2 %copy-start.13 = (bf16[4,32,1536]{2,1,0:T(8,128)(2,1)}, bf16[4,32,1536]{2,1,0:T(8,128)(2,1)S(1)}, u32[]{:S(2)}) copy-start(bf16[4,32,1536]{2,1,0:T(8,128)(2,1)S(1)} %collective-permute-done.14.refs_8_) | copy-start | bytes 1179652
  87.8 17.2 %collective-permute-start.16 = (bf16[4,32,1536]{2,1,0:T(8,128)(2,1)}, bf16[4,32,1536]{2,1,0:T(8,128)(2,1)S(1)}, u32[]{:S(2)}, u32[]{:S(2)}) collective-permute-start(bf16[4,32,1536]{2,1,0:T(8,128)(2,1)} %collective-permute-done.7.refs_2_), channel_id=1, source_target_pairs={{0,1},{1,0},{2,3},{3,2},{4,5},{5,4},{6,7},{7,6},{8,9},{9,8},{10,11... | collective-permute-start | bytes 1179656 | tf_op jit(solution)/shard_map/ppermute | solution.py:600
  87.8 17.7 %copy-start.14 = (bf16[4,32,1536]{2,1,0:T(8,128)(2,1)}, bf16[4,32,1536]{2,1,0:T(8,128)(2,1)S(1)}, u32[]{:S(2)}) copy-start(bf16[4,32,1536]{2,1,0:T(8,128)(2,1)S(1)} %collective-permute-done.15.refs_9_) | copy-start | bytes 1179652
  87.9 23.1 %collective-permute-start.17 = (bf16[4,32,1536]{2,1,0:T(8,128)(2,1)}, bf16[4,32,1536]{2,1,0:T(8,128)(2,1)S(1)}, u32[]{:S(2)}, u32[]{:S(2)}) collective-permute-start(bf16[4,32,1536]{2,1,0:T(8,128)(2,1)} %collective-permute-done.9.refs_3_), channel_id=1, source_target_pairs={{0,1},{1,0},{2,3},{3,2},{4,5},{5,4},{6,7},{7,6},{8,9},{9,8},{10,11... | collective-permute-start | bytes 1179656 | tf_op jit(solution)/shard_map/ppermute | solution.py:600
  103.8 7.2 %collective-permute-start.20 = (bf16[4,32,1536]{2,1,0:T(8,128)(2,1)}, bf16[4,32,1536]{2,1,0:T(8,128)(2,1)}, u32[]{:S(2)}, u32[]{:S(2)}) collective-permute-start(bf16[4,32,1536]{2,1,0:T(8,128)(2,1)} %collective-permute-done.13.refs_6_), channel_id=1, source_target_pairs={{0,1},{1,0},{2,3},{3,2},{4,5},{5,4},{6,7},{7,6},{8,9},{9,8},{10,11... | collective-permute-start | bytes 1179656 | tf_op jit(solution)/shard_map/ppermute | solution.py:600
  105.1 5.9 %collective-permute-start.21 = (bf16[4,32,1536]{2,1,0:T(8,128)(2,1)}, bf16[4,32,1536]{2,1,0:T(8,128)(2,1)}, u32[]{:S(2)}, u32[]{:S(2)}) collective-permute-start(bf16[4,32,1536]{2,1,0:T(8,128)(2,1)} %collective-permute-done.11.refs_7_), channel_id=1, source_target_pairs={{0,1},{1,0},{2,3},{3,2},{4,5},{5,4},{6,7},{7,6},{8,9},{9,8},{10,11... | collective-permute-start | bytes 1179656 | tf_op jit(solution)/shard_map/ppermute | solution.py:600
  105.1 5.9 %collective-permute-start.18 = (bf16[4,32,1536]{2,1,0:T(8,128)(2,1)}, bf16[4,32,1536]{2,1,0:T(8,128)(2,1)}, u32[]{:S(2)}, u32[]{:S(2)}) collective-permute-start(bf16[4,32,1536]{2,1,0:T(8,128)(2,1)} %collective-permute-done.10.refs_4_), channel_id=1, source_target_pairs={{0,1},{1,0},{2,3},{3,2},{4,5},{5,4},{6,7},{7,6},{8,9},{9,8},{10,11... | collective-permute-start | bytes 1179656 | tf_op jit(solution)/shard_map/ppermute | solution.py:600
  105.6 5.4 %collective-permute-start.19 = (bf16[4,32,1536]{2,1,0:T(8,128)(2,1)}, bf16[4,32,1536]{2,1,0:T(8,128)(2,1)}, u32[]{:S(2)}, u32[]{:S(2)}) collective-permute-start(bf16[4,32,1536]{2,1,0:T(8,128)(2,1)} %collective-permute-done.12.refs_5_), channel_id=1, source_target_pairs={{0,1},{1,0},{2,3},{3,2},{4,5},{5,4},{6,7},{7,6},{8,9},{9,8},{10,11... | collective-permute-start | bytes 1179656 | tf_op jit(solution)/shard_map/ppermute | solution.py:600
  120.1 42.6 %copy-start.1 = (bf16[768,1536]{1,0:T(8,128)(2,1)S(1)}, bf16[768,1536]{1,0:T(8,128)(2,1)}, u32[]{:S(2)}) copy-start(bf16[768,1536]{1,0:T(8,128)(2,1)} %shard_map.87.w_ref) | copy-start | bytes 7077892
  120.1 1.5 collective-permute-start.22
  122.3 7.9 %copy-start.3 = (f32[8,128]{1,0:T(8,128)}, f32[8,128]{1,0:T(8,128)S(1)}, u32[]{:S(2)}) copy-start(f32[8,128]{1,0:T(8,128)S(1)} %shard_map.89.refs_0_) | copy-start | bytes 12292
  122.3 5.7 %collective-permute-start.23 = (f32[8,128]{1,0:T(8,128)S(1)}, f32[8,128]{1,0:T(8,128)S(1)}, u32[]{:S(2)}, u32[]{:S(2)}) collective-permute-start(f32[8,128]{1,0:T(8,128)S(1)} %shard_map.89.refs_0_), channel_id=1, source_target_pairs={{0,2},{1,3},{2,4},{3,5},{4,6},{5,7},{6,0},{7,1},{8,10},{9,11},{10,... | collective-permute-start | bytes 12296 | tf_op jit(solution)/shard_map/ppermute | solution.py:611
  123.8 5.1 %collective-permute-start.24 = (f32[8,128]{1,0:T(8,128)S(1)}, f32[8,128]{1,0:T(8,128)S(1)}, u32[]{:S(2)}, u32[]{:S(2)}) collective-permute-start(f32[8,128]{1,0:T(8,128)S(1)} %shard_map.89.refs_0_), channel_id=1, source_target_pairs={{0,4},{1,5},{2,6},{3,7},{4,0},{5,1},{6,2},{7,3},{8,12},{9,13},{10,... | collective-permute-start | bytes 12296 | tf_op jit(solution)/shard_map/ppermute | solution.py:611
  126.6 3.6 %collective-permute-start.25 = (f32[8,128]{1,0:T(8,128)S(1)}, f32[8,128]{1,0:T(8,128)S(1)}, u32[]{:S(2)}, u32[]{:S(2)}) collective-permute-start(f32[8,128]{1,0:T(8,128)S(1)} %shard_map.89.refs_0_), channel_id=1, source_target_pairs={{0,6},{1,7},{2,0},{3,1},{4,2},{5,3},{6,4},{7,5},{8,14},{9,15},{10,... | collective-permute-start | bytes 12296 | tf_op jit(solution)/shard_map/ppermute | solution.py:611
  132.2 17.0 %copy-start.9 = (bf16[32,32,384]{2,1,0:T(8,128)(2,1)}, bf16[32,32,384]{2,1,0:T(8,128)(2,1)S(1)}, u32[]{:S(2)}) copy-start(bf16[32,32,384]{2,1,0:T(8,128)(2,1)S(1)} %all-to-all-done) | copy-start | bytes 2359300
  159.9 2.8 %collective-permute-start.27 = (bf16[1024,384]{1,0:T(8,128)(2,1)}, bf16[1024,384]{1,0:T(8,128)(2,1)S(1)}, u32[]{:S(2)}, u32[]{:S(2)}) collective-permute-start(bf16[1024,384]{1,0:T(8,128)(2,1)} %get-tuple-element.49.own_ref), channel_id=1, source_target_pairs={{0,1},{1,0},{2,3},{3,2},{4,5},{5,4},{6,7},{7,6},{8,9},{9,8},{10,11... | collective-permute-start | bytes 2359304 | tf_op jit(solution)/shard_map/ppermute | solution.py:619
  160.2 2.2 collective-permute-start.26
  168.2 12.4 %collective-permute-start.32 = (s16[528,384]{1,0:T(8,128)(2,1)S(1)}, s16[528,384]{1,0:T(8,128)(2,1)S(1)}, u32[]{:S(2)}, u32[]{:S(2)}) collective-permute-start(s16[528,384]{1,0:T(8,128)(2,1)S(1)} %get-tuple-element.58), channel_id=1, source_target_pairs={{0,6},{1,7},{2,0},{3,1},{4,2},{5,3},{6,4},{7,5},{8,14},{9,15},{10,... | collective-permute-start | bytes 1216520 | tf_op jit(solution)/shard_map/ppermute | solution.py:622
  170.9 13.9 %collective-permute-start.28 = (s16[528,384]{1,0:T(8,128)(2,1)S(1)}, s16[528,384]{1,0:T(8,128)(2,1)S(1)}, u32[]{:S(2)}, u32[]{:S(2)}) collective-permute-start(s16[528,384]{1,0:T(8,128)(2,1)S(1)} %get-tuple-element.54), channel_id=1, source_target_pairs={{0,2},{1,3},{2,4},{3,5},{4,6},{5,7},{6,0},{7,1},{8,10},{9,11},{10,... | collective-permute-start | bytes 1216520 | tf_op jit(solution)/shard_map/ppermute | solution.py:621
  171.0 18.4 %collective-permute-start.30 = (s16[528,384]{1,0:T(8,128)(2,1)S(1)}, s16[528,384]{1,0:T(8,128)(2,1)S(1)}, u32[]{:S(2)}, u32[]{:S(2)}) collective-permute-start(s16[528,384]{1,0:T(8,128)(2,1)S(1)} %get-tuple-element.55), channel_id=1, source_target_pairs={{0,6},{1,7},{2,0},{3,1},{4,2},{5,3},{6,4},{7,5},{8,14},{9,15},{10,... | collective-permute-start | bytes 1216520 | tf_op jit(solution)/shard_map/ppermute | solution.py:624
  174.2 18.9 %collective-permute-start.31 = (s16[528,384]{1,0:T(8,128)(2,1)S(1)}, s16[528,384]{1,0:T(8,128)(2,1)S(1)}, u32[]{:S(2)}, u32[]{:S(2)}) collective-permute-start(s16[528,384]{1,0:T(8,128)(2,1)S(1)} %get-tuple-element.56), channel_id=1, source_target_pairs={{0,2},{1,3},{2,4},{3,5},{4,6},{5,7},{6,0},{7,1},{8,10},{9,11},{10,... | collective-permute-start | bytes 1216520 | tf_op jit(solution)/shard_map/ppermute | solution.py:623
  181.1 16.2 %collective-permute-start.33 = (s16[528,384]{1,0:T(8,128)(2,1)S(1)}, s16[528,384]{1,0:T(8,128)(2,1)S(1)}, u32[]{:S(2)}, u32[]{:S(2)}) collective-permute-start(s16[528,384]{1,0:T(8,128)(2,1)S(1)} %shard_map.95), channel_id=1, source_target_pairs={{0,6},{1,7},{2,0},{3,1},{4,2},{5,3},{6,4},{7,5},{8,14},{9,15},{10,... | collective-permute-start | bytes 1216520 | tf_op jit(solution)/shard_map/ppermute | solution.py:626
  185.2 15.4 %collective-permute-start.29 = (s16[528,384]{1,0:T(8,128)(2,1)S(1)}, s16[528,384]{1,0:T(8,128)(2,1)S(1)}, u32[]{:S(2)}, u32[]{:S(2)}) collective-permute-start(s16[528,384]{1,0:T(8,128)(2,1)S(1)} %shard_map.94), channel_id=1, source_target_pairs={{0,2},{1,3},{2,4},{3,5},{4,6},{5,7},{6,0},{7,1},{8,10},{9,11},{10,... | collective-permute-start | bytes 1216520 | tf_op jit(solution)/shard_map/ppermute | solution.py:625
  200.7 9.1 %copy-start.7 = (bf16[1024,768]{1,0:T(8,128)(2,1)S(1)}, bf16[1024,768]{1,0:T(8,128)(2,1)}, u32[]{:S(2)}) copy-start(bf16[1024,768]{1,0:T(8,128)(2,1)} %get-tuple-element.47.sums_ref) | copy-start | bytes 4718596
  203.0 30.3 %all-to-all-start.2 = ((s16[32,112,128]{2,1,0:T(8,128)(2,1)}), s16[32,112,128]{2,1,0:T(8,128)(2,1)S(1)}, u32[]{:S(2)}, u32[]{:S(2)}) async-start(s16[32,112,128]{2,1,0:T(8,128)(2,1)} %shard_map.96), calls=%async_computation.2 | async-start | bytes 1835008 | tf_op jit(solution)/shard_map/all_to_all | solution.py:629
  (17 other events, 41.3 us)
